TPU v7x, 512 devices: a whole 4x4x16 slice. The times are simulated.
512 devices in a mesh: replica: 64 (over x, z), tensor: 8 (over y, core).
Axes of the slice: x: 4, y: 4, z: 16, core: 2. Of those that a mesh axis runs over, the one named last changes fastest.
Arguments:
- hidden: bfloat16 [4096, 8192], P('replica', 'tensor'), may hold values from -6 to 6
- base_query: bfloat16 [4096, 8192], P('replica', 'tensor'), may hold values from -6 to 6
- key_value_cache: bfloat16 [16384, 16, 2048], P('replica', None, 'tensor'), may hold values from -6 to 6
- adapter_down_weight: bfloat16 [1024, 16, 8192], P('replica', None, 'tensor'), may hold values from -0.0625 to 0.0625
- adapter_up_weight: bfloat16 [1024, 16, 8192], P('replica', None, 'tensor'), may hold values from -1.5 to 1.5
- adapter_holder: int32 [4096, 1], P('replica'), may hold values from 0 to 63; in each aligned block of 64 rows (0 to 63, 64 to 127, ...) at most 2 rows name the same one
- adapter_position: int32 [4096], P('replica'), may hold values from 0 to 15
- request_page_table: int32 [4096, 4], P('replica'), may hold values from 0 to 383, as said below
- lengths: int32 [4096], P('replica'), may hold values from 1 to 64, as said below
- migration_page_lists: int32 [64, 64, 2], P('replica'), may hold values from 0 to 255, as said below
Outputs:
- attended: bfloat16 [4096, 8192], P('replica', 'tensor')
Inputs may be any that keep to these rules, and one draw needn't show every extreme that they name: `adapter_holder`: among the 64 requests of one device at most 2 name the same owner. Entries below 256 are distinct pages of the owner's own pool. A request with request_page_table[r, 0] of 256 or more has moved: all its entries are 256 + s * 2 + min(j, 1) for entry j, with one source s other than the owner; no two moved requests of one owner share a source. `lengths`: A moved request has at most 32 tokens. `migration_page_lists`: every entry of row s is a page of source s's pool; the pages that a moved request reads stand at entries 0 and 1 of the list of its source and owner.
All inputs are finite; a program needn't handle non-finite values.
Results may differ from a plain program's by a relative error of at most 0.011.
Values may be sent and summed in bfloat16 or wider, within the bound.
No kernel may reach another device: no remote copies, remote signals or barrier semaphores. Data moves between devices by JAX's collectives and lax.ppermute only.
A program may use at most 64 MiB of HBM per device.

v0:
```python
import jax
import jax.numpy as jnp
from jax import lax
from jax.sharding import PartitionSpec as P

HEAD_SIZE = 128
ADAPTER_RANK = 16
PAGE_TOKENS = 16


adapter_scale = 2.0


def attend(query_rows, page_rows, valid_len):
    row_count = query_rows.shape[0]
    key_count = page_rows.shape[1]
    kv_heads = page_rows.shape[2] // (2 * HEAD_SIZE)
    grouped = query_rows.reshape(row_count, kv_heads, -1, HEAD_SIZE)
    stacked = page_rows.reshape(row_count, key_count, kv_heads, 2, HEAD_SIZE)
    scores = jnp.einsum(
        "rhge,rlhe->rhgl", grouped, stacked[:, :, :, 0], preferred_element_type=jnp.float32
    ) * HEAD_SIZE ** (-0.5)
    live_mask = (jnp.arange(key_count, dtype=jnp.int32)[None, :] < valid_len[:, None])[
        :, None, None, :
    ]
    scores = jnp.where(live_mask, scores, -jnp.inf)
    row_max = jnp.max(scores, axis=-1, keepdims=True)
    weights = jnp.exp(scores - row_max)
    row_total = jnp.sum(weights, axis=-1, keepdims=True)
    weights_bf = (weights / row_total).astype(jnp.bfloat16)
    mixed = jnp.einsum(
        "rhgl,rlhe->rhge", weights_bf, stacked[:, :, :, 1], preferred_element_type=jnp.float32
    )
    return mixed.reshape(row_count, -1).astype(jnp.bfloat16)


def body(
    hidden,
    base_query,
    key_value_cache,
    adapter_down_weight,
    adapter_up_weight,
    adapter_holder,
    adapter_position,
    request_page_table,
    lengths,
    migration_page_lists,
):
    row_count = hidden.shape[0]
    partner_count = lax.axis_size("replica")
    position_count = max(2, (2 * row_count + partner_count - 1) // partner_count)
    row_ids = jnp.arange(row_count, dtype=jnp.int32)
    owners = adapter_holder[:, 0]
    same_owner = owners[:, None] == owners[None, :]
    earlier_rank = jnp.sum(same_owner & (row_ids[None, :] < row_ids[:, None]), axis=1)
    send_map = (
        owners[None, None, :] == jnp.arange(partner_count, dtype=jnp.int32)[:, None, None]
    ) & (earlier_rank[None, None, :] == jnp.arange(position_count, dtype=jnp.int32)[None, :, None])
    send_rows = jnp.einsum(
        "ncr,rd->ncd", send_map.astype(jnp.bfloat16), hidden, preferred_element_type=jnp.float32
    ).astype(jnp.bfloat16)
    send_slot = jnp.sum(send_map.astype(jnp.int32) * adapter_position[None, None, :], axis=2)
    got_rows, got_slot = (
        lax.all_to_all(send_rows, "replica", split_axis=0, concat_axis=0, tiled=True),
        lax.all_to_all(send_slot, "replica", split_axis=0, concat_axis=0, tiled=True),
    )
    flat_rows = got_rows.reshape(partner_count * position_count, -1)
    local_adapters = adapter_down_weight.shape[0]
    projected = jnp.einsum(
        "md,kd->mk",
        flat_rows,
        adapter_down_weight.reshape(local_adapters * ADAPTER_RANK, -1),
        preferred_element_type=jnp.float32,
    )
    adapter_pick = (
        got_slot.reshape(-1)[:, None] == jnp.arange(local_adapters, dtype=jnp.int32)[None, :]
    )
    partial_rank = jnp.sum(
        projected.reshape(-1, local_adapters, ADAPTER_RANK) * adapter_pick[:, :, None], axis=1
    )
    reduced_rank_state = lax.psum(partial_rank, "tensor").astype(jnp.bfloat16)
    spread_rank = (
        reduced_rank_state[:, None, :] * adapter_pick[:, :, None].astype(jnp.bfloat16)
    ).reshape(-1, local_adapters * ADAPTER_RANK)
    adapter_delta = (
        jnp.dot(
            spread_rank,
            adapter_up_weight.reshape(local_adapters * ADAPTER_RANK, -1),
            preferred_element_type=jnp.float32,
        )
        * adapter_scale
    ).astype(jnp.bfloat16)
    returned = lax.all_to_all(
        adapter_delta.reshape(partner_count, position_count, -1),
        "replica",
        split_axis=0,
        concat_axis=0,
        tiled=True,
    )
    own_delta = jnp.einsum(
        "ncr,ncd->rd", send_map.astype(jnp.bfloat16), returned, preferred_element_type=jnp.float32
    )
    query_matrix = (base_query.astype(jnp.float32) + own_delta).astype(jnp.bfloat16)
    columns = key_value_cache.shape[2]
    own_lists = migration_page_lists[0]
    outbox = key_value_cache[own_lists]
    received = lax.all_to_all(outbox, "replica", split_axis=0, concat_axis=0, tiled=True)
    extended = jnp.concatenate(
        [key_value_cache, received.reshape(-1, PAGE_TOKENS, columns)], axis=0
    )
    gathered = extended[request_page_table].reshape(row_count, -1, columns)
    attended = attend(query_matrix, gathered, lengths)
    return attended


def solution(mesh):
    in_specs = (
        P("replica", "tensor"),
        P("replica", "tensor"),
        P("replica", None, "tensor"),
        P("replica", None, "tensor"),
        P("replica", None, "tensor"),
        P("replica", None),
        P("replica"),
        P("replica", None),
        P("replica"),
        P("replica", None, None),
    )
    out_specs = P("replica", "tensor")
    return jax.shard_map(body, mesh=mesh, in_specs=in_specs, out_specs=out_specs, check_vma=False)
```

profile of v0, /device:TPU:6, one launch (start us, length us, event | category | flops | bytes accessed | tf_op | source)
XLA Modules:
  0.0 180.6 jit_solution(8827577131546570607)
XLA Ops:
  0.0 0.9 convert_reduce_fusion
  0.9 0.7 iota_compare_fusion.1
  1.6 0.8 fusion.15
  2.4 0.7 copy.27
  3.1 18.8 %all-to-all-start.1 = ((s32[64,1,2]{2,1,0:T(1,128)}), s32[64,1,2]{2,1,0:T(1,128)S(1)}, u32[]{:S(2)}, u32[]{:S(2)}) async-start(s32[64,1,2]{2,1,0:T(1,128)} %copy.27), calls=%async_computation.1 | async-start | bytes 65536 | tf_op jit(solution)/shard_map/all_to_all | solution.py:65
  21.9 1.2 convolution_convert_fusion
  23.1 1.0 copy.26
  24.1 10.3 %all-to-all-done.1 = s32[64,1,2]{2,1,0:T(1,128)S(1)} async-done(((s32[64,1,2]{2,1,0:T(1,128)}), s32[64,1,2]{2,1,0:T(1,128)S(1)}, u32[]{:S(2)}, u32[]{:S(2)}) %all-to-all-start.1) | async-done | bytes 544 | tf_op jit(solution)/shard_map/all_to_all | solution.py:65
  34.4 7.3 %all-to-all-start = ((bf16[64,2,1024]{2,1,0:T(2,128)(2,1)}), bf16[64,2,1024]{2,1,0:T(2,128)(2,1)}, u32[]{:S(2)}, u32[]{:S(2)}) async-start(bf16[64,2,1024]{2,1,0:T(2,128)(2,1)} %copy.26), calls=%async_computation | async-start | bytes 524288 | tf_op jit(solution)/shard_map/all_to_all | solution.py:64
  41.6 0.5 broadcast.106
  42.1 0.7 reduce.7
  43.0 18.3 %all-to-all-done = bf16[64,2,1024]{2,1,0:T(2,128)(2,1)} async-done(((bf16[64,2,1024]{2,1,0:T(2,128)(2,1)}), bf16[64,2,1024]{2,1,0:T(2,128)(2,1)}, u32[]{:S(2)}, u32[]{:S(2)}) %all-to-all-start) | async-done | bytes 262176 | tf_op jit(solution)/shard_map/all_to_all | solution.py:64
  61.3 1.0 reshape.229
  62.4 0.3 fusion.9
  62.7 12.7 %psum.7 = bf16[128,16]{0,1:T(8,128)(2,1)S(1)} all-reduce(f32[128,16]{0,1:T(8,128)S(1)} %fusion.9), channel_id=1, replica_groups=mesh['replica'=64,'tensor'=8] {'tensor'}, use_global_device_ids=true, to_apply=%region_3.0 | all-reduce | flops 2048 | bytes 12288 | tf_op jit(solution)/shard_map/psum | solution.py:81
  75.4 0.3 fusion.3
  75.6 0.8 reshape.203
  76.4 7.4 %all-to-all-start.2 = ((bf16[64,2,1024]{2,1,0:T(2,128)(2,1)}), bf16[64,2,1024]{2,1,0:T(2,128)(2,1)S(1)}, u32[]{:S(2)}, u32[]{:S(2)}) async-start(bf16[64,2,1024]{2,1,0:T(2,128)(2,1)} %reshape.203), calls=%async_computation.2 | async-start | bytes 524288 | tf_op jit(solution)/shard_map/all_to_all | solution.py:93
  83.9 0.1 reshape.210
  84.1 1.6 gather_fusion
  85.8 18.3 %all-to-all-done.2 = bf16[64,2,1024]{2,1,0:T(2,128)(2,1)S(1)} async-done(((bf16[64,2,1024]{2,1,0:T(2,128)(2,1)}), bf16[64,2,1024]{2,1,0:T(2,128)(2,1)S(1)}, u32[]{:S(2)}, u32[]{:S(2)}) %all-to-all-start.2) | async-done | bytes 262176 | tf_op jit(solution)/shard_map/all_to_all | solution.py:93
  104.1 6.7 %all-to-all-start.3 = ((bf16[64,2,16,256]{3,2,1,0:T(8,128)(2,1)}), bf16[64,2,16,256]{3,2,1,0:T(8,128)(2,1)}, u32[]{:S(2)}, u32[]{:S(2)}) async-start(bf16[64,2,16,256]{3,2,1,0:T(8,128)(2,1)} %bitcast.44), calls=%async_computation.3 | async-start | bytes 2097152 | tf_op jit(solution)/shard_map/all_to_all | solution.py:107
  111.1 0.3 fusion.8
  111.5 51.4 %all-to-all-done.3 = bf16[64,2,16,256]{3,2,1,0:T(8,128)(2,1)} async-done(((bf16[64,2,16,256]{3,2,1,0:T(8,128)(2,1)}), bf16[64,2,16,256]{3,2,1,0:T(8,128)(2,1)}, u32[]{:S(2)}, u32[]{:S(2)}) %all-to-all-start.3) | async-done | bytes 1048608 | tf_op jit(solution)/shard_map/all_to_all | solution.py:107
  162.9 3.2 %pad_maximum_fusion = bf16[384,16,256]{2,1,0:T(8,128)(2,1)} fusion(bf16[128,16,256]{2,1,0:T(8,128)(2,1)} %bitcast.7, bf16[256,16,256]{2,1,0:T(8,128)(2,1)S(1)} %copy-done.1), kind=kLoop, calls=%fused_computation.3 | loop fusion | flops 1572864 | bytes 6291456 | tf_op jit(solution)/shard_map/concatenate | solution.py:108
  166.0 4.0 %gather_fusion.1 = bf16[256,16,256]{2,1,0:T(8,128)(2,1)} fusion(bf16[384,16,256]{2,1,0:T(8,128)(2,1)} %pad_maximum_fusion, s32[1024]{0:T(1024)S(1)} %pad_clamp_fusion), kind=kCustom, calls=%fused_computation.1 | custom fusion | bytes 4195328 | tf_op jit(solution)/shard_map/gather | solution.py:111
  170.0 2.5 %reshape_reshape.3 = bf16[64,64,1,2,128]{4,3,1,0,2:T(2,128)(2,1)S(1)} reshape(bf16[256,16,256]{2,1,0:T(8,128)(2,1)} %gather_fusion.1) | data formatting | bytes 4194304 | tf_op jit(solution)/shard_map/reshape;reshape | solution.py:19
  172.6 3.8 %fusion.26 = (bf16[64,64,1,1,128]{4,3,1,0,2:T(2,128)(2,1)S(1)}, bf16[64,64,1,1,128]{4,3,1,0,2:T(2,128)(2,1)}) fusion(bf16[64,64,1,2,128]{4,3,1,0,2:T(2,128)(2,1)S(1)} %reshape_reshape.3), kind=kLoop, calls=%fused_computation.50 | loop fusion | bytes 4194304 | tf_op jit(solution)/shard_map/slice | solution.py:21
  176.4 0.7 fusion.5
  177.1 0.2 fusion.27
  177.3 2.6 %convolution_convert_fusion.1 = bf16[64,8,128]{2,1,0:T(8,128)(2,1)S(1)} fusion(bf16[64,64,1,1,128]{4,3,1,0,2:T(2,128)(2,1)} %get-tuple-element.6, f32[64,8]{1,0:T(8,128)S(1)} %fusion.27, f32[64,8,64]{2,1,0:T(8,128)S(1)} %fusion.5), kind=kOutput, calls=%fused_computation.15 | convolution fusion | flops 8553023 | bytes 1312768 | tf_op jit(solution)/shard_map/rhgl,rlhe->rhge/dot_general | solution.py:31
  179.9 0.7 copy.45
  (26 shorter events, 0.6 us)
Async XLA Ops:
  0.0 75.4 %copy-start = (bf16[16,16,1024]{2,1,0:T(8,128)(2,1)S(1)}, bf16[16,16,1024]{2,1,0:T(8,128)(2,1)}, u32[]{:S(2)}) copy-start(bf16[16,16,1024]{2,1,0:T(8,128)(2,1)} %param.14) | copy-start | bytes 1572868
  0.0 62.4 %copy-start.2 = (bf16[16,16,1024]{2,1,0:T(8,128)(2,1)S(1)}, bf16[16,16,1024]{2,1,0:T(8,128)(2,1)}, u32[]{:S(2)}) copy-start(bf16[16,16,1024]{2,1,0:T(8,128)(2,1)} %param.13) | copy-start | bytes 1572868
  3.1 31.3 %all-to-all-start.1 = ((s32[64,1,2]{2,1,0:T(1,128)}), s32[64,1,2]{2,1,0:T(1,128)S(1)}, u32[]{:S(2)}, u32[]{:S(2)}) async-start(s32[64,1,2]{2,1,0:T(1,128)} %copy.27), calls=%async_computation.1 | async-start | bytes 65536 | tf_op jit(solution)/shard_map/all_to_all | solution.py:65
  24.1 59.7 %copy-start.5 = (s32[1,64,2]{1,2,0:T(2,128)S(1)}, s32[1,64,2]{1,2,0:T(2,128)}, u32[]{:S(2)}) copy-start(s32[1,64,2]{1,2,0:T(2,128)} %param.19) | copy-start | bytes 1540
  24.1 60.0 %copy-start.1 = (bf16[256,16,256]{2,1,0:T(8,128)(2,1)S(1)}, bf16[256,16,256]{2,1,0:T(8,128)(2,1)}, u32[]{:S(2)}) copy-start(bf16[256,16,256]{2,1,0:T(8,128)(2,1)} %param.12) | copy-start | bytes 6291460
  34.4 26.9 %all-to-all-start = ((bf16[64,2,1024]{2,1,0:T(2,128)(2,1)}), bf16[64,2,1024]{2,1,0:T(2,128)(2,1)}, u32[]{:S(2)}, u32[]{:S(2)}) async-start(bf16[64,2,1024]{2,1,0:T(2,128)(2,1)} %copy.26), calls=%async_computation | async-start | bytes 524288 | tf_op jit(solution)/shard_map/all_to_all | solution.py:64
  76.4 27.6 %all-to-all-start.2 = ((bf16[64,2,1024]{2,1,0:T(2,128)(2,1)}), bf16[64,2,1024]{2,1,0:T(2,128)(2,1)S(1)}, u32[]{:S(2)}, u32[]{:S(2)}) async-start(bf16[64,2,1024]{2,1,0:T(2,128)(2,1)} %reshape.203), calls=%async_computation.2 | async-start | bytes 524288 | tf_op jit(solution)/shard_map/all_to_all | solution.py:93
  84.1 26.7 %copy-start.4 = (s32[64,4]{0,1:T(4,128)S(1)}, s32[64,4]{0,1:T(4,128)}, u32[]{:S(2)}) copy-start(s32[64,4]{0,1:T(4,128)} %param.17) | copy-start | bytes 3076
  84.1 26.9 %copy-start.6 = (s32[64]{0:T(128)S(1)}, s32[64]{0:T(128)}, u32[]{:S(2)}) copy-start(s32[64]{0:T(128)} %param.18) | copy-start | bytes 772
  84.1 27.0 %copy-start.3 = (bf16[64,1024]{1,0:T(8,128)(2,1)S(1)}, bf16[64,1024]{1,0:T(8,128)(2,1)}, u32[]{:S(2)}) copy-start(bf16[64,1024]{1,0:T(8,128)(2,1)} %param.11) | copy-start | bytes 393220
  104.1 58.8 %all-to-all-start.3 = ((bf16[64,2,16,256]{3,2,1,0:T(8,128)(2,1)}), bf16[64,2,16,256]{3,2,1,0:T(8,128)(2,1)}, u32[]{:S(2)}, u32[]{:S(2)}) async-start(bf16[64,2,16,256]{3,2,1,0:T(8,128)(2,1)} %bitcast.44), calls=%async_computation.3 | async-start | bytes 2097152 | tf_op jit(solution)/shard_map/all_to_all | solution.py:107
where the time goes:
time: 181 us
  waiting for transfers between devices  98.2 us (54%)
  starting transfers between devices  40.2 us (22%)
  local copies, waits for them, and re-layouts  17.4 us (10%)
  blocking collectives  12.7 us (7%)
  other arithmetic  6.57 us (4%)
  matrix products  5.3 us (3%)
    all_to_all x1, waiting for transfers between devices, body(): lax.all_to_all(outbox, 'replica', split_axis=0, concat_axis=0, tiled=True)  51.4 us
    all_to_all x1, starting transfers between devices, body(): lax.all_to_all(send_slot, 'replica', split_axis=0, concat_axis=0, tiled=T...  18.8 us
    all_to_all x1, waiting for transfers between devices, body(): lax.all_to_all(adapter_delta.reshape(partner_count, position_count, -1),...  18.3 us
    all_to_all x1, waiting for transfers between devices, body(): lax.all_to_all(send_rows, 'replica', split_axis=0, concat_axis=0, tiled=T...  18.3 us
    psum x1, blocking collectives, body(): reduced_rank_state = lax.psum(partial_rank, 'tensor').astype(jnp.bfloat16)  12.7 us
    all_to_all x1, waiting for transfers between devices, body(): lax.all_to_all(send_slot, 'replica', split_axis=0, concat_axis=0, tiled=T...  10.3 us
    all_to_all x1, starting transfers between devices, body(): lax.all_to_all(adapter_delta.reshape(partner_count, position_count, -1),...  7.36 us
    all_to_all x1, starting transfers between devices, body(): lax.all_to_all(send_rows, 'replica', split_axis=0, concat_axis=0, tiled=T...  7.27 us
  transfers between devices with their start and end apart: 4, of which 4 were waited for; matrix products, arithmetic and copies ran while one was open for 3% of the time, Pallas kernels for 0%

commit v1 on v0

v1 whole, which is shorter than its diff:
```python
import jax
import jax.numpy as jnp
from jax import lax
from jax.experimental import pallas as pl
from jax.experimental.pallas import tpu as pltpu
from jax.sharding import PartitionSpec as P

HEAD = 128
RANK = 16
PAGE = 16
POOL = 256
SCALE = 2.0
F32 = jnp.float32
BF16 = jnp.bfloat16
NEG = -1e30


def dot(a, b, dims):
    return lax.dot_general(a, b, (dims, ((), ())), preferred_element_type=F32)


def nn(a, b):
    return dot(a, b, ((1,), (0,)))


def nt(a, b):
    return dot(a, b, ((1,), (1,)))


def tn(a, b):
    return dot(a, b, ((0,), (0,)))


def iota(shape, dim):
    return lax.broadcasted_iota(jnp.int32, shape, dim)


def slot_maps(holder_row, peers):
    rows = holder_row.shape[1]
    named = iota((peers, rows), 0) == holder_row
    before = (iota((rows, rows), 0) < iota((rows, rows), 1)).astype(BF16)
    rank = nn(named.astype(BF16), before)
    return [(named & (rank == c)).astype(BF16) for c in range(2)]


def moved_map(table, peers):
    entry = table[0:1, :]
    source = lax.shift_right_arithmetic(entry - POOL, 1)
    return (iota((peers, entry.shape[1]), 0) == source) & (entry >= POOL)


def send_kernel(hidden_ref, holder_ref, position_ref, table_ref, lengths_ref, out_ref):
    peers, _, width = out_ref.shape
    features = width - HEAD
    maps = slot_maps(holder_ref[...], peers)
    hidden = hidden_ref[...]
    rows = hidden.shape[0]
    place = (iota((HEAD, rows), 0) == position_ref[...]).astype(BF16)
    moved = moved_map(table_ref[...], peers)
    length = jnp.sum(jnp.where(moved, lengths_ref[...], 0).astype(F32), axis=1, keepdims=True)
    lane = iota((peers, HEAD), 1)
    for c in range(2):
        out_ref[:, c, :features] = nn(maps[c], hidden).astype(BF16)
        out_ref[:, c, features:] = jnp.where(lane < RANK, nt(maps[c], place), length).astype(BF16)


def down_kernel(got_ref, down_ref, partial_ref, pick_ref, limit_ref):
    peers, _, width = got_ref.shape
    features = width - HEAD
    down = down_ref[...]
    many = down.shape[0]
    first, second = got_ref[:, 0, :], got_ref[:, 1, :]
    got = jnp.concatenate([first[:, :features], second[:, :features]], axis=0)
    place = jnp.concatenate([first[:, features:], second[:, features:]], axis=0)
    spread = (lax.shift_right_arithmetic(iota((many, HEAD), 0), 4) == iota((many, HEAD), 1)).astype(BF16)
    pick = nt(spread, place)
    projected = nt(down, got) * pick
    partial = jnp.sum(projected.reshape(many // RANK, RANK, 2 * peers), axis=0)
    for t in range(partial_ref.shape[0]):
        partial_ref[t] = partial
    pick_ref[...] = pick.astype(BF16)
    tail = first[:, features:].astype(F32)
    limit_ref[...] = jnp.broadcast_to(tail[:, None, :], limit_ref.shape)


def up_kernel(got_ref, pick_ref, up_ref, out_ref):
    peers = out_ref.shape[0]
    low = jnp.sum(got_ref[...], axis=0).astype(BF16)
    many = up_ref.shape[0]
    spread = jnp.concatenate([low] * (many // RANK), axis=0) * pick_ref[...]
    delta = (tn(spread, up_ref[...]) * SCALE).astype(BF16)
    for c in range(2):
        out_ref[:, c, :] = delta[c * peers:(c + 1) * peers, :]


def query_kernel(got_ref, base_ref, holder_ref, table_ref, query_ref, out_ref, wide_ref):
    peers = got_ref.shape[0]
    maps = slot_maps(holder_ref[...], peers)
    delta = tn(maps[0], got_ref[:, 0, :]) + tn(maps[1], got_ref[:, 1, :])
    query = (base_ref[...].astype(F32) + delta).astype(BF16)
    query_ref[...] = query
    moved = moved_map(table_ref[...], peers).astype(BF16)
    chosen = nn(moved, query)
    heads = wide_ref.shape[1]
    for h in range(heads):
        wide_ref[:, h, :] = chosen[:, h * HEAD:(h + 1) * HEAD]
    out_ref[...] = wide_ref[...].astype(BF16)


def weighted(scores, live, values):
    scores = jnp.where(live, scores * (HEAD ** -0.5), NEG)
    top = jnp.max(scores, axis=1, keepdims=True)
    weights = jnp.exp(scores - top)
    total = jnp.sum(weights, axis=1, keepdims=True)
    return nn((weights / total).astype(BF16), values)


def local_kernel(table_ref, lengths_ref, query_ref, cache_ref, row_ref, out_ref, wide_ref, mixed_ref):
    rows, heads, _ = wide_ref.shape
    pages = table_ref.shape[0]
    span = pages * PAGE
    query = query_ref[...]
    for h in range(heads):
        wide_ref[:, h, :] = query[:, h * HEAD:(h + 1) * HEAD].astype(F32)
    batch = 4
    shape = (batch * heads, batch * span)
    row_of = lax.div(iota(shape, 0), heads)
    column_of = lax.div(iota(shape, 1), span)
    place = lax.rem(iota(shape, 1), span)
    own = row_of == column_of

    def step(b, carry):
        first = b * batch
        found = []
        limit = jnp.zeros(shape, jnp.int32)
        for i in range(batch):
            limit = jnp.where(row_of == i, lengths_ref[0, first + i], limit)
            for j in range(pages):
                found.append(cache_ref[jnp.minimum(table_ref[j, first + i], POOL - 1)])
        both = jnp.concatenate(found, axis=0)
        q = wide_ref[pl.ds(first, batch)].reshape(batch * heads, HEAD).astype(BF16)
        scores = nt(q, both[:, :HEAD])
        mixed = weighted(scores, own & (place < limit), both[:, HEAD:])
        mixed_ref[pl.ds(first, batch)] = mixed.reshape(batch, heads, HEAD)
        return carry

    lax.fori_loop(0, rows // batch, step, 0, unroll=4)
    stays = jnp.where(row_ref[0:1, :] < POOL, 1.0, 0.0)
    eye = iota((rows, rows), 0) == iota((rows, rows), 1)
    keep = jnp.sum(jnp.where(eye, stays, 0.0), axis=1, keepdims=True)
    for h in range(heads):
        out_ref[:, h * HEAD:(h + 1) * HEAD] = (mixed_ref[:, h, :] * keep).astype(BF16)


def listed_kernel(list_ref, cache_ref, key_ref, value_ref):
    count, owners = list_ref.shape

    def step(o, carry):
        for k in range(count):
            page = cache_ref[list_ref[k, o]]
            at = pl.ds(pl.multiple_of((o * count + k) * PAGE, PAGE), PAGE)
            key_ref[at, :] = page[:, :HEAD]
            value_ref[at, :] = page[:, HEAD:]
        return carry

    lax.fori_loop(0, owners, step, 0, unroll=8)


def moved_kernel(query_ref, key_ref, value_ref, limit_ref, out_ref):
    owners, heads, _ = query_ref.shape
    span = key_ref.shape[0] // owners
    batch = 8
    shape = (batch * heads, batch * span)
    own = lax.div(iota(shape, 0), heads) == lax.div(iota(shape, 1), span)
    place = lax.rem(iota(shape, 1), span)
    for b in range(owners // batch):
        at = slice(b * batch, (b + 1) * batch)
        keys = slice(b * batch * span, (b + 1) * batch * span)
        q = query_ref[at].astype(F32).reshape(batch * heads, HEAD).astype(BF16)
        limit = limit_ref[at].reshape(batch * heads, HEAD)[:, HEAD - 1:HEAD]
        live = own & (place.astype(F32) < limit)
        mixed = weighted(nt(q, key_ref[keys, :]), live, value_ref[keys, :])
        out_ref[at] = mixed.reshape(batch, heads, HEAD).astype(BF16)


def final_kernel(got_ref, local_ref, table_ref, out_ref, wide_ref):
    peers, heads, _ = got_ref.shape
    wide_ref[...] = got_ref[...].astype(F32)
    moved = moved_map(table_ref[...], peers).astype(BF16)
    for h in range(heads):
        part = tn(moved, wide_ref[:, h, :].astype(BF16))
        at = slice(h * HEAD, (h + 1) * HEAD)
        out_ref[:, at] = (part + local_ref[:, at].astype(F32)).astype(BF16)


def call(kernel, out_shape, cost, scratch=(), scalars=0, inputs=0):
    smem = pl.BlockSpec(memory_space=pltpu.SMEM)
    vmem = pl.BlockSpec(memory_space=pltpu.VMEM)
    return pl.pallas_call(
        kernel,
        out_shape=out_shape,
        in_specs=[smem] * scalars + [vmem] * inputs,
        out_specs=jax.tree.map(lambda _: vmem, out_shape),
        scratch_shapes=list(scratch),
        cost_estimate=pl.CostEstimate(flops=cost, bytes_accessed=cost // 100, transcendentals=0),
        compiler_params=pltpu.CompilerParams(vmem_limit_bytes=24 * 1024 * 1024),
    )


def exchange(x, axis="replica"):
    return lax.all_to_all(x, axis, split_axis=0, concat_axis=0, tiled=True)


def body(
    hidden,
    base_query,
    key_value_cache,
    adapter_down_weight,
    adapter_up_weight,
    adapter_holder,
    adapter_position,
    request_page_table,
    lengths,
    migration_page_lists,
):
    rows, features = hidden.shape
    peers = lax.axis_size("replica")
    shards = lax.axis_size("tensor")
    heads = features // HEAD
    S = jax.ShapeDtypeStruct
    holder = adapter_holder.reshape(1, rows)
    position = adapter_position.reshape(1, rows)
    table = request_page_table.T
    length = lengths.reshape(1, rows)
    lists = migration_page_lists[0].T
    down = adapter_down_weight.reshape(-1, features)
    up = adapter_up_weight.reshape(-1, features)
    many = down.shape[0]

    sent = call(send_kernel, S((peers, 2, features + HEAD), BF16), 10**8, inputs=5)(
        hidden, holder, position, table, length
    )
    got = exchange(sent)
    span = lists.shape[0] * PAGE
    keys, values = call(
        listed_kernel, (S((peers * span, HEAD), BF16),) * 2, 10**9, scalars=1, inputs=1
    )(lists, key_value_cache)

    partial, pick, limit = call(
        down_kernel,
        (S((shards, RANK, 2 * peers), F32), S((many, 2 * peers), BF16), S((peers, heads, HEAD), F32)),
        10**8,
        inputs=2,
    )(got, down)
    partials = exchange(partial, "tensor")
    delta = call(up_kernel, S((peers, 2, features), BF16), 10**8, inputs=3)(partials, pick, up)
    returned = exchange(delta)
    wide = pltpu.VMEM((rows, heads, HEAD), F32)
    query, moved_query = call(
        query_kernel, (S((rows, features), BF16), S((peers, heads, HEAD), BF16)), 10**8, (wide,), inputs=4
    )(returned, base_query, holder, table)
    asked = exchange(moved_query)
    local = call(local_kernel, S((rows, features), BF16), 10**9, (wide, wide), scalars=2, inputs=3)(
        table, length, query, key_value_cache, table
    )
    answer = call(moved_kernel, S((peers, heads, HEAD), BF16), 10**8, inputs=4)(asked, keys, values, limit)
    answered = exchange(answer)
    return call(final_kernel, S((rows, features), BF16), 10**8, (wide,), inputs=3)(answered, local, table)


def solution(mesh):
    in_specs = (
        P("replica", "tensor"),
        P("replica", "tensor"),
        P("replica", None, "tensor"),
        P("replica", None, "tensor"),
        P("replica", None, "tensor"),
        P("replica", None),
        P("replica"),
        P("replica", None),
        P("replica"),
        P("replica", None, None),
    )
    return jax.shard_map(body, mesh=mesh, in_specs=in_specs, out_specs=P("replica", "tensor"), check_vma=False)
```

time: 181 us -> 134 us (0.74)
  waiting for transfers between devices: 98.2 us -> 20.5 us
  blocking collectives: 12.7 us -> 77.9 us
  starting transfers between devices: 40.2 us -> 13.1 us
  Pallas kernels: 0 us -> 15.3 us
  local copies, waits for them, and re-layouts: 17.4 us -> 6.22 us
  other arithmetic: 6.57 us -> 0 us
  matrix products: 5.3 us -> 0 us
    all_to_all x0 -> x3, blocking collectives: none -> 77.9 us  [exchange(): return lax.all_to_all(x, axis, split_axis=0, concat_axis=0, tiled=True)]
    all_to_all x4 -> x2, waiting for transfers between devices: 98.2 us -> 20.5 us  [exchange(): return lax.all_to_all(x, axis, split_axis=0, concat_axis=0, tiled=True)]
    all_to_all x4 -> x2, starting transfers between devices: 40.2 us -> 13.1 us  [exchange(): return lax.all_to_all(x, axis, split_axis=0, concat_axis=0, tiled=True)]
    pallas_call x0 -> x8, Pallas kernels: none -> 15.3 us  [the longest x1 6.46 us: body(): call(local_kernel, S((rows, features), BF16), 10 ** 9, (wide, wide), scal...]
    psum x1 -> x0, blocking collectives: 12.7 us -> none  [body(): reduced_rank_state = lax.psum(partial_rank, 'tensor').astype(jnp.bfloat16)]
    gather x2 -> x0, local copies, waits for them, and re-layouts: 5.65 us -> none  [the longest x1 4.01 us: body(): gathered = extended[request_page_table].reshape(row_count, -1, columns)]
    unnamed x16 -> x30, local copies, waits for them, and re-layouts: 0.74 us -> 6.22 us
    dot_general x6 -> x0, matrix products: 5.3 us -> none  [the longest x1 2.55 us: attend(): jnp.einsum('rhgl,rlhe->rhge', weights_bf, stacked[:, :, :, 1], preferred_...]
  transfers between devices with their start and end apart: 4 -> 2, of which waited for: 4 -> 2; matrix products, arithmetic and copies ran while one was open for 3% -> 0% of each run, Pallas kernels for 0% -> 6%
where the time goes in v1:
time: 134 us; the launch traced here: 133 us
  blocking collectives  77.9 us (58%)
  waiting for transfers between devices  20.5 us (15%)
  Pallas kernels  15.3 us (11%)
  starting transfers between devices  13.1 us (10%)
  local copies, waits for them, and re-layouts  6.22 us (5%)
    all_to_all x3, blocking collectives, exchange(): return lax.all_to_all(x, axis, split_axis=0, concat_axis=0, tiled=True)  77.9 us
    all_to_all x2, waiting for transfers between devices, exchange(): return lax.all_to_all(x, axis, split_axis=0, concat_axis=0, tiled=True)  20.5 us
    all_to_all x2, starting transfers between devices, exchange(): return lax.all_to_all(x, axis, split_axis=0, concat_axis=0, tiled=True)  13.1 us
    pallas_call x1, Pallas kernels, body(): call(local_kernel, S((rows, features), BF16), 10 ** 9, (wide, wide), scal...  6.46 us
    unnamed x30, local copies, waits for them, and re-layouts  6.22 us
    pallas_call x1, Pallas kernels, body(): call(moved_kernel, S((peers, heads, HEAD), BF16), 10 ** 8, inputs=4)  3.34 us
  transfers between devices with their start and end apart: 2, of which 2 were waited for; matrix products, arithmetic and copies ran while one was open for 0% of the time, Pallas kernels for 6%

profile of v1, /device:TPU:6, one launch (start us, length us, event | category | flops | bytes accessed | tf_op | source)
XLA Modules:
  0.0 133.1 jit_solution(3274386552019916133)
XLA Ops:
  0.0 1.0 copy-done.3
  1.0 0.7 copy-done.4
  1.7 0.7 copy-done.6
  2.3 0.7 copy-done.8
  3.0 0.7 copy-done.9
  3.6 0.4 shard_map.100
  4.1 40.8 %all_to_all.25.got_ref = bf16[64,2,1152]{2,1,0:T(2,128)(2,1)S(1)} all-to-all(bf16[64,2,1152]{2,1,0:T(2,128)(2,1)S(1)} %shard_map.100), channel_id=1, replica_groups=mesh['replica'=64,'tensor'=8] {'replica'}, dimensions={0} | all-to-all | bytes 589824 | tf_op jit(solution)/shard_map/all_to_all | solution.py:211
  44.9 1.0 copy-done.1
  46.0 0.9 shard_map.101
  46.9 9.9 %all_to_all.26.got_ref = f32[8,16,128]{2,1,0:T(8,128)S(1)} all-to-all(f32[8,16,128]{2,1,0:T(8,128)S(1)} %get-tuple-element.12), channel_id=1, replica_groups=mesh['replica'=64,'tensor'=8] {'tensor'}, dimensions={0} | all-to-all | bytes 131072 | tf_op jit(solution)/shard_map/all_to_all | solution.py:211
  56.8 0.0 copy-done
  56.8 0.3 shard_map.102
  57.1 27.1 %all_to_all.27.got_ref = bf16[64,2,1024]{2,1,0:T(2,128)(2,1)S(1)} all-to-all(bf16[64,2,1024]{2,1,0:T(2,128)(2,1)S(1)} %shard_map.102), channel_id=1, replica_groups=mesh['replica'=64,'tensor'=8] {'replica'}, dimensions={0} | all-to-all | bytes 524288 | tf_op jit(solution)/shard_map/all_to_all | solution.py:211
  84.3 0.0 copy-done.2
  84.3 0.0 copy-done.5
  84.3 0.0 copy-done.7
  84.3 1.7 %shard_map.103 = (bf16[64,1024]{1,0:T(8,128)(2,1)S(1)}, bf16[64,8,128]{2,1,0:T(8,128)(2,1)}) custom-call(bf16[64,2,1024]{2,1,0:T(2,128)(2,1)S(1)} %all_to_all.27.got_ref, bf16[64,1024]{1,0:T(8,128)(2,1)S(1)} %copy-done.2, s32[1,64]{1,0:T(1,128)S(1)} %bitcast.17, s32[4,64]{1,0:T(4,128)S(1)} %bitcast.12), custom_call_target="tpu_custom_call" | custom-call | flops 100000000 | bytes 1000000 | tf_op jit(solution)/shard_map/pallas_call | solution.py:259
  85.9 0.6 copy-done.12
  86.6 6.6 %all-to-all-start.3 = ((bf16[64,8,128]{2,1,0:T(8,128)(2,1)}), bf16[64,8,128]{2,1,0:T(8,128)(2,1)S(1)}, u32[]{:S(2)}, u32[]{:S(2)}) async-start(bf16[64,8,128]{2,1,0:T(8,128)(2,1)} %get-tuple-element.14), calls=%async_computation.3 | async-start | bytes 262144 | tf_op jit(solution)/shard_map/all_to_all | solution.py:211
  93.2 0.0 copy-done.14
  93.2 0.0 copy-done.11
  93.2 0.0 copy-start.10
  93.2 1.0 shard_map.104
  94.2 13.6 %all-to-all-done.3.query_ref = bf16[64,8,128]{2,1,0:T(8,128)(2,1)S(1)} async-done(((bf16[64,8,128]{2,1,0:T(8,128)(2,1)}), bf16[64,8,128]{2,1,0:T(8,128)(2,1)S(1)}, u32[]{:S(2)}, u32[]{:S(2)}) %all-to-all-start.3) | async-done | bytes 131104 | tf_op jit(solution)/shard_map/all_to_all | solution.py:211
  107.9 3.3 %shard_map.105 = bf16[64,8,128]{2,1,0:T(8,128)(2,1)} custom-call(bf16[64,8,128]{2,1,0:T(8,128)(2,1)S(1)} %all-to-all-done.3.query_ref, bf16[2048,128]{1,0:T(8,128)(2,1)S(1)} %get-tuple-element.15.key_ref, bf16[2048,128]{1,0:T(8,128)(2,1)S(1)} %get-tuple-element.16.value_ref, f32[64,8,128]{2,1,0:T(8,128)S(1)} %get-tuple-element.17.limit_ref), custom_call_target="tpu_custom_call" | custom-call | flops 100000000 | bytes 1000000 | tf_op jit(solution)/shard_map/pallas_call | solution.py:266
  111.2 6.6 %all-to-all-start.4 = ((bf16[64,8,128]{2,1,0:T(8,128)(2,1)}), bf16[64,8,128]{2,1,0:T(8,128)(2,1)S(1)}, u32[]{:S(2)}, u32[]{:S(2)}) async-start(bf16[64,8,128]{2,1,0:T(8,128)(2,1)} %shard_map.105), calls=%async_computation.4 | async-start | bytes 262144 | tf_op jit(solution)/shard_map/all_to_all | solution.py:211
  117.8 0.0 copy-done.10
  117.8 0.0 copy-start.13
  117.8 0.9 copy-done.13
  118.7 6.5 %shard_map.106.local_ref = bf16[64,1024]{1,0:T(8,128)(2,1)S(1)} custom-call(s32[4,64]{1,0:T(4,128)S(1)} %bitcast.13, s32[1,64]{1,0:T(1,128)S(1)} %bitcast.20, bf16[64,1024]{1,0:T(8,128)(2,1)S(1)} %copy-done.13, bf16[256,16,256]{2,1,0:T(8,128)(2,1)S(1)} %copy-done.11, s32[4,64]{1,0:T(4,128)S(1)} %bitcast.14), custom_call_target="tpu_custom_call" | custom-call | flops 1000000000 | bytes 10000000 | tf_op jit(solution)/shard_map/pallas_call | solution.py:263
  125.2 6.9 %all-to-all-done.4.got_ref = bf16[64,8,128]{2,1,0:T(8,128)(2,1)S(1)} async-done(((bf16[64,8,128]{2,1,0:T(8,128)(2,1)}), bf16[64,8,128]{2,1,0:T(8,128)(2,1)S(1)}, u32[]{:S(2)}, u32[]{:S(2)}) %all-to-all-start.4) | async-done | bytes 131104 | tf_op jit(solution)/shard_map/all_to_all | solution.py:211
  132.1 1.1 shard_map.107
  (13 shorter events, 0.0 us)
Async XLA Ops:
  0.0 56.8 %copy-start = (bf16[16,16,1024]{2,1,0:T(8,128)(2,1)S(1)}, bf16[16,16,1024]{2,1,0:T(8,128)(2,1)}, u32[]{:S(2)}) copy-start(bf16[16,16,1024]{2,1,0:T(8,128)(2,1)} %param.14) | copy-start | bytes 1572868
  0.0 84.3 %copy-start.2 = (bf16[64,1024]{1,0:T(8,128)(2,1)S(1)}, bf16[64,1024]{1,0:T(8,128)(2,1)}, u32[]{:S(2)}) copy-start(bf16[64,1024]{1,0:T(8,128)(2,1)} %base_ref.1) | copy-start | bytes 393220
  0.0 1.0 copy-start.3
  1.0 0.7 copy-start.4
  1.7 0.7 copy-start.6
  2.3 0.7 copy-start.8
  3.0 0.7 copy-start.9
  3.6 80.6 %copy-start.5 = (s32[64,4]{0,1:T(4,128)S(1)}, s32[64,4]{0,1:T(4,128)}, u32[]{:S(2)}) copy-start(s32[64,4]{0,1:T(4,128)} %param.17) | copy-start | bytes 3076
  3.6 80.6 %copy-start.7 = (s32[64,1]{0,1:T(1,128)S(1)}, s32[64,1]{0,1:T(1,128)}, u32[]{:S(2)}) copy-start(s32[64,1]{0,1:T(1,128)} %param.15) | copy-start | bytes 772
  3.6 89.5 %copy-start.14 = (s32[1,64,2]{1,2,0:T(2,128)S(1)}, s32[1,64,2]{1,2,0:T(2,128)}, u32[]{:S(2)}) copy-start(s32[1,64,2]{1,2,0:T(2,128)} %param.19) | copy-start | bytes 1540
  44.9 1.0 copy-start.1
  45.9 47.2 %copy-start.11 = (bf16[256,16,256]{2,1,0:T(8,128)(2,1)S(1)}, bf16[256,16,256]{2,1,0:T(8,128)(2,1)}, u32[]{:S(2)}) copy-start(bf16[256,16,256]{2,1,0:T(8,128)(2,1)} %cache_ref.3) | copy-start | bytes 6291460
  85.9 0.6 copy-start.12
  86.6 21.3 %all-to-all-start.3 = ((bf16[64,8,128]{2,1,0:T(8,128)(2,1)}), bf16[64,8,128]{2,1,0:T(8,128)(2,1)S(1)}, u32[]{:S(2)}, u32[]{:S(2)}) async-start(bf16[64,8,128]{2,1,0:T(8,128)(2,1)} %get-tuple-element.14), calls=%async_computation.3 | async-start | bytes 262144 | tf_op jit(solution)/shard_map/all_to_all | solution.py:211
  93.2 24.6 %copy-start.10 = (s32[64]{0:T(128)S(1)}, s32[64]{0:T(128)}, u32[]{:S(2)}) copy-start(s32[64]{0:T(128)} %param.18) | copy-start | bytes 772
  111.2 20.9 %all-to-all-start.4 = ((bf16[64,8,128]{2,1,0:T(8,128)(2,1)}), bf16[64,8,128]{2,1,0:T(8,128)(2,1)S(1)}, u32[]{:S(2)}, u32[]{:S(2)}) async-start(bf16[64,8,128]{2,1,0:T(8,128)(2,1)} %shard_map.105), calls=%async_computation.4 | async-start | bytes 262144 | tf_op jit(solution)/shard_map/all_to_all | solution.py:211
  117.8 0.9 copy-start.13

commit v2 on v1

v2 whole, which is shorter than its diff:
```python
import jax
import jax.numpy as jnp
from jax import lax
from jax.experimental import pallas as pl
from jax.experimental.pallas import tpu as pltpu
from jax.sharding import PartitionSpec as P

HEAD = 128
RANK = 16
PAGE = 16
POOL = 256
SCALE = 2.0
F32 = jnp.float32
BF16 = jnp.bfloat16
NEG = -1e30


def dot(a, b, dims):
    return lax.dot_general(a, b, (dims, ((), ())), preferred_element_type=F32)


def nn(a, b):
    return dot(a, b, ((1,), (0,)))


def nt(a, b):
    return dot(a, b, ((1,), (1,)))


def tn(a, b):
    return dot(a, b, ((0,), (0,)))


def iota(shape, dim):
    return lax.broadcasted_iota(jnp.int32, shape, dim)


def slot_maps(holder_row, peers):
    rows = holder_row.shape[1]
    named = iota((peers, rows), 0) == holder_row
    before = (iota((rows, rows), 0) < iota((rows, rows), 1)).astype(BF16)
    rank = nn(named.astype(BF16), before)
    return [(named & (rank == c)).astype(BF16) for c in range(2)]


def moved_map(table, peers):
    entry = table[0:1, :]
    source = lax.shift_right_arithmetic(entry - POOL, 1)
    return (iota((peers, entry.shape[1]), 0) == source) & (entry >= POOL)


def fetch(pairs, sems):
    copies = [pltpu.make_async_copy(src, dst, sems.at[i]) for i, (src, dst) in enumerate(pairs)]
    for copy in copies:
        copy.start()
    return copies


def send_kernel(
    hidden_hbm, holder_hbm, position_hbm, table_hbm, lengths_hbm, out_ref,
    hidden_ref, holder_ref, position_ref, table_ref, lengths_ref, sems,
):
    peers, _, width = out_ref.shape
    features = width - HEAD
    copies = fetch(
        [
            (holder_hbm, holder_ref),
            (position_hbm, position_ref),
            (table_hbm, table_ref),
            (lengths_hbm, lengths_ref),
            (hidden_hbm, hidden_ref),
        ],
        sems,
    )
    for copy in copies[:4]:
        copy.wait()
    maps = slot_maps(holder_ref[...], peers)
    rows = hidden_ref.shape[0]
    place = (iota((HEAD, rows), 0) == position_ref[...]).astype(BF16)
    moved = moved_map(table_ref[...], peers)
    length = jnp.sum(jnp.where(moved, lengths_ref[...], 0).astype(F32), axis=1, keepdims=True)
    lane = iota((peers, HEAD), 1)
    for c in range(2):
        out_ref[:, c, features:] = jnp.where(lane < RANK, nt(maps[c], place), length).astype(BF16)
    copies[4].wait()
    hidden = hidden_ref[...]
    for c in range(2):
        out_ref[:, c, :features] = nn(maps[c], hidden).astype(BF16)


def down_kernel(got_ref, down_ref, partial_ref, pick_ref, limit_ref):
    peers, _, width = got_ref.shape
    features = width - HEAD
    many = down_ref.shape[0]
    first, second = got_ref[:, 0, :], got_ref[:, 1, :]
    got = jnp.concatenate([first[:, :features], second[:, :features]], axis=0)
    place = jnp.concatenate([first[:, features:], second[:, features:]], axis=0)
    spread = (lax.shift_right_arithmetic(iota((many, HEAD), 0), 4) == iota((many, HEAD), 1)).astype(BF16)
    pick = nt(spread, place)
    pick_ref[...] = pick.astype(BF16)
    tail = first[:, width - 1:].astype(F32)
    limit_ref[...] = jnp.broadcast_to(tail[:, None, :], limit_ref.shape)
    projected = nt(down_ref[...], got) * pick
    partial = jnp.sum(projected.reshape(many // RANK, RANK, 2 * peers), axis=0)
    for t in range(partial_ref.shape[0]):
        partial_ref[t] = partial


def up_kernel(got_ref, pick_ref, up_ref, out_ref):
    peers = out_ref.shape[0]
    low = jnp.sum(got_ref[...], axis=0).astype(BF16)
    many = up_ref.shape[0]
    spread = jnp.concatenate([low] * (many // RANK), axis=0) * pick_ref[...]
    delta = (tn(spread, up_ref[...]) * SCALE).astype(BF16)
    for c in range(2):
        out_ref[:, c, :] = delta[c * peers:(c + 1) * peers, :]


def prepare_kernel(
    list_ref, cache_ref, holder_ref, table_ref, base_ref, weight_ref, page_ref, route_ref, start_ref, down_ref
):
    down_ref[...] = weight_ref[...]
    count, owners = list_ref.shape

    def step(o, carry):
        for k in range(count):
            at = pl.ds(pl.multiple_of((o * count + k) * PAGE, PAGE), PAGE)
            page_ref[at, :] = cache_ref[list_ref[k, o]]
        return carry

    lax.fori_loop(0, owners, step, 0, unroll=8)
    maps = slot_maps(holder_ref[...], owners)
    moved = moved_map(table_ref[...], owners).astype(BF16)
    route_ref[...] = nt(jnp.concatenate(maps, axis=0), moved).astype(BF16)
    start = nn(moved, base_ref[...])
    for h in range(start_ref.shape[1]):
        start_ref[:, h, :] = start[:, h * HEAD:(h + 1) * HEAD]


def query_kernel(got_ref, route_ref, start_ref, out_ref, wide_ref):
    got = jnp.concatenate([got_ref[:, 0, :], got_ref[:, 1, :]], axis=0)
    chosen = tn(route_ref[...], got)
    for h in range(wide_ref.shape[1]):
        wide_ref[:, h, :] = chosen[:, h * HEAD:(h + 1) * HEAD]
    out_ref[...] = (start_ref[...] + wide_ref[...]).astype(BF16)


def weighted(scores, live, values):
    scores = jnp.where(live, scores * (HEAD ** -0.5), NEG)
    top = jnp.max(scores, axis=1, keepdims=True)
    weights = jnp.exp(scores - top)
    total = jnp.sum(weights, axis=1, keepdims=True)
    return nn((weights / total).astype(BF16), values)


def local_kernel(
    table_ref, lengths_ref, got_ref, base_ref, holder_ref, row_ref, cache_ref, out_ref, wide_ref, mixed_ref
):
    rows, heads, _ = wide_ref.shape
    pages = table_ref.shape[0]
    span = pages * PAGE
    maps = jnp.concatenate(slot_maps(holder_ref[...], got_ref.shape[0]), axis=0)
    delta = tn(maps, jnp.concatenate([got_ref[:, 0, :], got_ref[:, 1, :]], axis=0))
    query = (base_ref[...].astype(F32) + delta).astype(BF16).astype(F32)
    for h in range(heads):
        wide_ref[:, h, :] = query[:, h * HEAD:(h + 1) * HEAD]
    batch = 4
    shape = (batch * heads, batch * span)
    row_of = lax.div(iota(shape, 0), heads)
    column_of = lax.div(iota(shape, 1), span)
    place = lax.rem(iota(shape, 1), span)
    own = row_of == column_of

    def step(b, carry):
        first = b * batch
        found = []
        limit = jnp.zeros(shape, jnp.int32)
        for i in range(batch):
            limit = jnp.where(row_of == i, lengths_ref[0, first + i], limit)
            for j in range(pages):
                found.append(cache_ref[jnp.minimum(table_ref[j, first + i], POOL - 1)])
        both = jnp.concatenate(found, axis=0)
        q = wide_ref[pl.ds(first, batch)].reshape(batch * heads, HEAD).astype(BF16)
        scores = nt(q, both[:, :HEAD])
        mixed = weighted(scores, own & (place < limit), both[:, HEAD:])
        mixed_ref[pl.ds(first, batch)] = mixed.reshape(batch, heads, HEAD)
        return carry

    lax.fori_loop(0, rows // batch, step, 0, unroll=4)
    stays = jnp.where(row_ref[0:1, :] < POOL, 1.0, 0.0)
    eye = iota((rows, rows), 0) == iota((rows, rows), 1)
    keep = jnp.sum(jnp.where(eye, stays, 0.0), axis=1, keepdims=True)
    for h in range(heads):
        out_ref[:, h * HEAD:(h + 1) * HEAD] = (mixed_ref[:, h, :] * keep).astype(BF16)


def moved_kernel(query_ref, page_ref, limit_ref, out_ref):
    owners, heads, _ = query_ref.shape
    span = page_ref.shape[0] // owners
    batch = HEAD // span
    groups = owners // batch
    wide = batch * heads
    shape = (wide, batch * span)
    own = lax.div(iota(shape, 0), heads) == lax.div(iota(shape, 1), span)
    place = jnp.where(own, lax.rem(iota(shape, 1), span), span).astype(F32)
    query = query_ref[...].astype(F32).reshape(owners * heads, HEAD).astype(BF16)
    pages = [page_ref[g * HEAD:(g + 1) * HEAD, :] for g in range(groups)]
    scores = [nt(query[g * wide:(g + 1) * wide], pages[g][:, :HEAD]) for g in range(groups)]
    live = [
        place < limit_ref[g * batch:(g + 1) * batch].reshape(wide, HEAD) for g in range(groups)
    ]
    scores = [jnp.where(m, x * (HEAD ** -0.5), NEG) for m, x in zip(live, scores)]
    tops = [jnp.max(x, axis=1, keepdims=True) for x in scores]
    weights = [jnp.exp(x - top) for x, top in zip(scores, tops)]
    totals = [jnp.sum(x, axis=1, keepdims=True) for x in weights]
    weights = [(x / total).astype(BF16) for x, total in zip(weights, totals)]
    mixed = [nn(x, page[:, HEAD:]) for x, page in zip(weights, pages)]
    for g in range(groups):
        out_ref[g * batch:(g + 1) * batch] = mixed[g].reshape(batch, heads, HEAD).astype(BF16)


def final_kernel(got_ref, local_ref, table_ref, out_ref, wide_ref):
    peers, heads, _ = got_ref.shape
    wide_ref[...] = got_ref[...].astype(F32)
    moved = moved_map(table_ref[...], peers).astype(BF16)
    for h in range(heads):
        part = tn(moved, wide_ref[:, h, :].astype(BF16))
        at = slice(h * HEAD, (h + 1) * HEAD)
        out_ref[:, at] = (part + local_ref[:, at].astype(F32)).astype(BF16)


def call(kernel, out_shape, cost, spaces, scratch=(), limit=24):
    kinds = {"s": pltpu.SMEM, "v": pltpu.VMEM, "h": pltpu.HBM}
    return pl.pallas_call(
        kernel,
        out_shape=out_shape,
        in_specs=[pl.BlockSpec(memory_space=kinds[x]) for x in spaces],
        out_specs=jax.tree.map(lambda _: pl.BlockSpec(memory_space=pltpu.VMEM), out_shape),
        scratch_shapes=list(scratch),
        cost_estimate=pl.CostEstimate(flops=cost, bytes_accessed=cost // 100, transcendentals=0),
        compiler_params=pltpu.CompilerParams(vmem_limit_bytes=limit * 1024 * 1024),
    )


def exchange(x, axis="replica"):
    return lax.all_to_all(x, axis, split_axis=0, concat_axis=0, tiled=True)


def body(
    hidden,
    base_query,
    key_value_cache,
    adapter_down_weight,
    adapter_up_weight,
    adapter_holder,
    adapter_position,
    request_page_table,
    lengths,
    migration_page_lists,
):
    rows, features = hidden.shape
    peers = lax.axis_size("replica")
    shards = lax.axis_size("tensor")
    heads = features // HEAD
    S = jax.ShapeDtypeStruct
    holder = adapter_holder.reshape(1, rows)
    position = adapter_position.reshape(1, rows)
    table = request_page_table.T
    length = lengths.reshape(1, rows)
    lists = migration_page_lists[0].T
    down = adapter_down_weight.reshape(-1, features)
    up = adapter_up_weight.reshape(-1, features)
    many = down.shape[0]

    ints = lambda n: pltpu.VMEM((n, rows), jnp.int32)
    sent = call(
        send_kernel,
        S((peers, 2, features + HEAD), BF16),
        10**8,
        "hhhhh",
        [pltpu.VMEM((rows, features), BF16), ints(1), ints(1), ints(table.shape[0]), ints(1), pltpu.SemaphoreType.DMA((5,))],
        limit=60,
    )(hidden, holder, position, table, length)
    got = exchange(sent)
    pages, route, start, down = call(
        prepare_kernel,
        (
            S((peers * lists.shape[0] * PAGE, 2 * HEAD), BF16),
            S((2 * peers, peers), BF16),
            S((peers, heads, HEAD), F32),
            S(down.shape, BF16),
        ),
        10**9,
        "svvvvv",
    )(lists, key_value_cache, holder, table, base_query, down)

    partial, pick, limit = call(
        down_kernel,
        (S((shards, RANK, 2 * peers), F32), S((many, 2 * peers), BF16), S((peers, heads, HEAD), F32)),
        10**8,
        "vv",
    )(got, down)
    partials = exchange(partial, "tensor")
    delta = call(up_kernel, S((peers, 2, features), BF16), 10**8, "vvv")(partials, pick, up)
    returned = exchange(delta)
    wide = pltpu.VMEM((rows, heads, HEAD), F32)
    asked = exchange(
        call(query_kernel, S((peers, heads, HEAD), BF16), 10**8, "vvv", (wide,))(returned, route, start)
    )
    local = call(local_kernel, S((rows, features), BF16), 10**9, "ssvvvvv", (wide, wide))(
        table, length, returned, base_query, holder, table, key_value_cache
    )
    answered = exchange(
        call(moved_kernel, S((peers, heads, HEAD), BF16), 10**8, "vvv")(asked, pages, limit)
    )
    return call(final_kernel, S((rows, features), BF16), 10**8, "vvv", (wide,))(answered, local, table)


def solution(mesh):
    in_specs = (
        P("replica", "tensor"),
        P("replica", "tensor"),
        P("replica", None, "tensor"),
        P("replica", None, "tensor"),
        P("replica", None, "tensor"),
        P("replica", None),
        P("replica"),
        P("replica", None),
        P("replica"),
        P("replica", None, None),
    )
    return jax.shard_map(body, mesh=mesh, in_specs=in_specs, out_specs=P("replica", "tensor"), check_vma=False)
```

time: 134 us -> 127 us (0.948)
  blocking collectives: 77.9 us -> 58.1 us
  starting transfers between devices: 13.1 us -> 25.3 us
    all_to_all x3, blocking collectives: 77.9 us -> 58.1 us  [exchange(): return lax.all_to_all(x, axis, split_axis=0, concat_axis=0, tiled=True)]
    all_to_all x2, starting transfers between devices: 13.1 us -> 25.3 us  [exchange(): return lax.all_to_all(x, axis, split_axis=0, concat_axis=0, tiled=True)]
    unnamed x30 -> x24, local copies, waits for them, and re-layouts: 6.22 us -> 7.15 us
  transfers between devices with their start and end apart: 2 -> 2, of which waited for: 2 -> 2; matrix products, arithmetic and copies ran while one was open for 0% -> 0% of each run, Pallas kernels for 6% -> 7%
where the time goes in v2:
time: 127 us
  blocking collectives  58.1 us (46%)
  starting transfers between devices  25.3 us (20%)
  waiting for transfers between devices  20.8 us (16%)
  Pallas kernels  15 us (12%)
  local copies, waits for them, and re-layouts  7.15 us (6%)
    all_to_all x3, blocking collectives, exchange(): return lax.all_to_all(x, axis, split_axis=0, concat_axis=0, tiled=True)  58.1 us
    all_to_all x2, starting transfers between devices, exchange(): return lax.all_to_all(x, axis, split_axis=0, concat_axis=0, tiled=True)  25.3 us
    all_to_all x2, waiting for transfers between devices, exchange(): return lax.all_to_all(x, axis, split_axis=0, concat_axis=0, tiled=True)  20.8 us
    pallas_call x1, Pallas kernels, body(): call(local_kernel, S((rows, features), BF16), 10 ** 9, 'ssvvvvv', (wide,...  7.23 us
    unnamed x24, local copies, waits for them, and re-layouts  7.15 us
  transfers between devices with their start and end apart: 2, of which 2 were waited for; matrix products, arithmetic and copies ran while one was open for 0% of the time, Pallas kernels for 7%

profile of v2, /device:TPU:6, one launch (start us, length us, event | category | flops | bytes accessed | tf_op | source)
XLA Modules:
  0.0 126.5 jit_solution(13058393936545429851)
XLA Ops:
  0.0 2.0 %shard_map.100 = bf16[64,2,1152]{2,1,0:T(2,128)(2,1)} custom-call(bf16[64,1024]{1,0:T(8,128)(2,1)} %hidden_hbm.1, s32[1,64]{1,0:T(1,128)} %bitcast.15, s32[1,64]{1,0:T(1,128)} %bitcast.22, s32[4,64]{1,0:T(4,128)} %bitcast.10, s32[1,64]{1,0:T(1,128)} %bitcast.18), custom_call_target="tpu_custom_call" | custom-call | flops 100000000 | bytes 1000000 | tf_op jit(solution)/shard_map/pallas_call | solution.py:276
  2.1 18.8 %all-to-all-start = ((bf16[64,2,1152]{2,1,0:T(2,128)(2,1)}), bf16[64,2,1152]{2,1,0:T(2,128)(2,1)S(1)}, u32[]{:S(2)}, u32[]{:S(2)}) async-start(bf16[64,2,1152]{2,1,0:T(2,128)(2,1)} %shard_map.100), calls=%async_computation | async-start | bytes 589824 | tf_op jit(solution)/shard_map/all_to_all | solution.py:246
  20.9 0.0 copy-start.1
  20.9 0.7 copy-done.1
  21.5 0.0 copy-start.3
  21.5 0.7 copy-done.3
  22.2 0.0 copy-start.6
  22.2 1.6 %copy-done.6 = bf16[256,16,256]{2,1,0:T(8,128)(2,1)S(1)} copy-done((bf16[256,16,256]{2,1,0:T(8,128)(2,1)S(1)}, bf16[256,16,256]{2,1,0:T(8,128)(2,1)}, u32[]{:S(2)}) %copy-start.6) | copy-done | bytes 2097176
  23.8 1.0 copy-done.8
  24.8 0.9 copy-done.9
  25.7 0.7 copy-done.11
  26.4 1.3 %shard_map.101 = (bf16[2048,256]{1,0:T(8,128)(2,1)S(1)}, bf16[128,64]{1,0:T(8,128)(2,1)S(1)}, f32[64,8,128]{2,1,0:T(8,128)S(1)}, bf16[256,1024]{1,0:T(8,128)(2,1)S(1)}) custom-call(s32[2,64]{1,0:T(2,128)S(1)} %bitcast.21, bf16[256,16,256]{2,1,0:T(8,128)(2,1)S(1)} %copy-done.6, s32[1,64]{1,0:T(1,128)S(1)} %bitcast.16, s32[4,64]{1,0:T(4,128)S(1)} %bitcast.11, ...), custom_call_target="tpu_custom_call" | custom-call | flops 1000000000 | bytes 10000000 | tf_op jit(solution)/shard_map/pallas_call | solution.py:285
  27.7 15.4 %all-to-all-done.got_ref = bf16[64,2,1152]{2,1,0:T(2,128)(2,1)S(1)} async-done(((bf16[64,2,1152]{2,1,0:T(2,128)(2,1)}), bf16[64,2,1152]{2,1,0:T(2,128)(2,1)S(1)}, u32[]{:S(2)}, u32[]{:S(2)}) %all-to-all-start) | async-done | bytes 294944 | tf_op jit(solution)/shard_map/all_to_all | solution.py:246
  43.1 0.9 shard_map.102
  44.0 9.9 %all_to_all.25.got_ref = f32[8,16,128]{2,1,0:T(8,128)S(1)} all-to-all(f32[8,16,128]{2,1,0:T(8,128)S(1)} %get-tuple-element.13), channel_id=1, replica_groups=mesh['replica'=64,'tensor'=8] {'tensor'}, dimensions={0} | all-to-all | bytes 131072 | tf_op jit(solution)/shard_map/all_to_all | solution.py:246
  53.9 0.0 copy-done
  54.0 0.0 copy-start.10
  54.0 0.3 shard_map.103
  54.3 27.1 %all_to_all.26.got_ref = bf16[64,2,1024]{2,1,0:T(2,128)(2,1)S(1)} all-to-all(bf16[64,2,1024]{2,1,0:T(2,128)(2,1)S(1)} %shard_map.103), channel_id=1, replica_groups=mesh['replica'=64,'tensor'=8] {'replica'}, dimensions={0} | all-to-all | bytes 524288 | tf_op jit(solution)/shard_map/all_to_all | solution.py:246
  81.4 0.8 shard_map.104
  82.2 21.1 %all_to_all.27.query_ref = bf16[64,8,128]{2,1,0:T(8,128)(2,1)S(1)} all-to-all(bf16[64,8,128]{2,1,0:T(8,128)(2,1)S(1)} %shard_map.104), channel_id=1, replica_groups=mesh['replica'=64,'tensor'=8] {'replica'}, dimensions={0} | all-to-all | bytes 262144 | tf_op jit(solution)/shard_map/all_to_all | solution.py:246
  103.3 1.3 %shard_map.105 = bf16[64,8,128]{2,1,0:T(8,128)(2,1)} custom-call(bf16[64,8,128]{2,1,0:T(8,128)(2,1)S(1)} %all_to_all.27.query_ref, bf16[2048,256]{1,0:T(8,128)(2,1)S(1)} %get-tuple-element.17.page_ref, f32[64,8,128]{2,1,0:T(8,128)S(1)} %get-tuple-element.18.limit_ref), custom_call_target="tpu_custom_call" | custom-call | flops 100000000 | bytes 1000000 | tf_op jit(solution)/shard_map/pallas_call | solution.py:314
  104.6 6.6 %all-to-all-start.4 = ((bf16[64,8,128]{2,1,0:T(8,128)(2,1)}), bf16[64,8,128]{2,1,0:T(8,128)(2,1)S(1)}, u32[]{:S(2)}, u32[]{:S(2)}) async-start(bf16[64,8,128]{2,1,0:T(8,128)(2,1)} %shard_map.105), calls=%async_computation.4 | async-start | bytes 262144 | tf_op jit(solution)/shard_map/all_to_all | solution.py:246
  111.2 0.0 copy-done.2
  111.2 0.0 copy-done.4
  111.2 0.0 copy-done.5
  111.2 0.0 copy-done.10
  111.2 0.0 copy-start.7
  111.2 1.6 %copy-done.7 = bf16[256,16,256]{2,1,0:T(8,128)(2,1)S(1)} copy-done((bf16[256,16,256]{2,1,0:T(8,128)(2,1)S(1)}, bf16[256,16,256]{2,1,0:T(8,128)(2,1)}, u32[]{:S(2)}) %copy-start.7) | copy-done | bytes 2097176
  112.8 7.2 %shard_map.106.local_ref = bf16[64,1024]{1,0:T(8,128)(2,1)S(1)} custom-call(s32[4,64]{1,0:T(4,128)S(1)} %bitcast.12, s32[1,64]{1,0:T(1,128)S(1)} %bitcast.19, bf16[64,2,1024]{2,1,0:T(2,128)(2,1)S(1)} %all_to_all.26.got_ref, bf16[64,1024]{1,0:T(8,128)(2,1)S(1)} %copy-done.10, s32[1,64]{1,0:T(1,128)S(1)} %bitcast.17, s32[4,64]{1,0:T(4,128)S(1)} %bitcast.13, ...), custom_call_target="tpu_custom_call" | custom-call | flops 1000000000 | bytes 10000000 | tf_op jit(solution)/shard_map/pallas_call | solution.py:310
  120.0 5.4 %all-to-all-done.4.got_ref = bf16[64,8,128]{2,1,0:T(8,128)(2,1)S(1)} async-done(((bf16[64,8,128]{2,1,0:T(8,128)(2,1)}), bf16[64,8,128]{2,1,0:T(8,128)(2,1)S(1)}, u32[]{:S(2)}, u32[]{:S(2)}) %all-to-all-start.4) | async-done | bytes 131104 | tf_op jit(solution)/shard_map/all_to_all | solution.py:246
  125.5 1.1 shard_map.107
  (7 shorter events, 0.0 us)
Async XLA Ops:
  2.1 41.0 %all-to-all-start = ((bf16[64,2,1152]{2,1,0:T(2,128)(2,1)}), bf16[64,2,1152]{2,1,0:T(2,128)(2,1)S(1)}, u32[]{:S(2)}, u32[]{:S(2)}) async-start(bf16[64,2,1152]{2,1,0:T(2,128)(2,1)} %shard_map.100), calls=%async_computation | async-start | bytes 589824 | tf_op jit(solution)/shard_map/all_to_all | solution.py:246
  20.9 0.7 copy-start.1
  21.5 0.7 copy-start.3
  22.2 1.6 %copy-start.6 = (bf16[256,16,256]{2,1,0:T(8,128)(2,1)S(1)}, bf16[256,16,256]{2,1,0:T(8,128)(2,1)}, u32[]{:S(2)}) copy-start(bf16[256,16,256]{2,1,0:T(8,128)(2,1)} %cache_ref.3) | copy-start | bytes 6291460
  23.8 1.0 copy-start.8
  24.8 0.9 copy-start.9
  25.7 0.7 copy-start.11
  26.4 27.5 %copy-start = (bf16[16,16,1024]{2,1,0:T(8,128)(2,1)S(1)}, bf16[16,16,1024]{2,1,0:T(8,128)(2,1)}, u32[]{:S(2)}) copy-start(bf16[16,16,1024]{2,1,0:T(8,128)(2,1)} %param.14) | copy-start | bytes 1572868
  53.9 57.2 %copy-start.2 = (s32[64,4]{0,1:T(4,128)S(1)}, s32[64,4]{0,1:T(4,128)}, u32[]{:S(2)}) copy-start(s32[64,4]{0,1:T(4,128)} %param.17) | copy-start | bytes 3076
  53.9 57.2 %copy-start.4 = (s32[64,1]{0,1:T(1,128)S(1)}, s32[64,1]{0,1:T(1,128)}, u32[]{:S(2)}) copy-start(s32[64,1]{0,1:T(1,128)} %param.15) | copy-start | bytes 772
  54.0 57.2 %copy-start.5 = (s32[64]{0:T(128)S(1)}, s32[64]{0:T(128)}, u32[]{:S(2)}) copy-start(s32[64]{0:T(128)} %param.18) | copy-start | bytes 772
  54.0 57.2 %copy-start.10 = (bf16[64,1024]{1,0:T(8,128)(2,1)S(1)}, bf16[64,1024]{1,0:T(8,128)(2,1)}, u32[]{:S(2)}) copy-start(bf16[64,1024]{1,0:T(8,128)(2,1)} %base_ref.3) | copy-start | bytes 393220
  104.6 20.9 %all-to-all-start.4 = ((bf16[64,8,128]{2,1,0:T(8,128)(2,1)}), bf16[64,8,128]{2,1,0:T(8,128)(2,1)S(1)}, u32[]{:S(2)}, u32[]{:S(2)}) async-start(bf16[64,8,128]{2,1,0:T(8,128)(2,1)} %shard_map.105), calls=%async_computation.4 | async-start | bytes 262144 | tf_op jit(solution)/shard_map/all_to_all | solution.py:246
  111.2 1.6 %copy-start.7 = (bf16[256,16,256]{2,1,0:T(8,128)(2,1)S(1)}, bf16[256,16,256]{2,1,0:T(8,128)(2,1)}, u32[]{:S(2)}) copy-start(bf16[256,16,256]{2,1,0:T(8,128)(2,1)} %cache_ref.3) | copy-start | bytes 6291460

commit v3 on v2

--- a/solution.py
+++ b/solution.py
@@ -13,6 +13,7 @@
 F32 = jnp.float32
 BF16 = jnp.bfloat16
 NEG = -1e30
+PLANES, DEPTH = 4, 16
 
 
 def dot(a, b, dims):
@@ -43,10 +44,22 @@
     return [(named & (rank == c)).astype(BF16) for c in range(2)]
 
 
+def my_plane():
+    return lax.div(lax.axis_index("replica"), DEPTH)
+
+
+def source_at(depth, step):
+    return ((my_plane() - step) & (PLANES - 1)) * DEPTH + depth
+
+
+def moved_from(table, source):
+    entry = table[0:1, :]
+    return (source == lax.shift_right_arithmetic(entry - POOL, 1)) & (entry >= POOL)
+
+
 def moved_map(table, peers):
-    entry = table[0:1, :]
-    source = lax.shift_right_arithmetic(entry - POOL, 1)
-    return (iota((peers, entry.shape[1]), 0) == source) & (entry >= POOL)
+    place = iota((peers, table.shape[1]), 0)
+    return moved_from(table, source_at(lax.shift_right_logical(place, 2), place & (PLANES - 1)))
 
 
 def fetch(pairs, sems):
@@ -77,9 +90,13 @@
     maps = slot_maps(holder_ref[...], peers)
     rows = hidden_ref.shape[0]
     place = (iota((HEAD, rows), 0) == position_ref[...]).astype(BF16)
-    moved = moved_map(table_ref[...], peers)
-    length = jnp.sum(jnp.where(moved, lengths_ref[...], 0).astype(F32), axis=1, keepdims=True)
     lane = iota((peers, HEAD), 1)
+    depth = iota((peers, rows), 0) & (DEPTH - 1)
+    length = jnp.zeros((peers, HEAD), F32)
+    for step in range(PLANES):
+        moved = moved_from(table_ref[...], source_at(depth, step))
+        total = jnp.sum(jnp.where(moved, lengths_ref[...], 0).astype(F32), axis=1, keepdims=True)
+        length = jnp.where(lane >= RANK * (step + 1), total, length)
     for c in range(2):
         out_ref[:, c, features:] = jnp.where(lane < RANK, nt(maps[c], place), length).astype(BF16)
     copies[4].wait()
@@ -98,8 +115,10 @@
     spread = (lax.shift_right_arithmetic(iota((many, HEAD), 0), 4) == iota((many, HEAD), 1)).astype(BF16)
     pick = nt(spread, place)
     pick_ref[...] = pick.astype(BF16)
-    tail = first[:, width - 1:].astype(F32)
-    limit_ref[...] = jnp.broadcast_to(tail[:, None, :], limit_ref.shape)
+    near = got_ref[pl.ds(my_plane() * DEPTH, DEPTH), 0, features:].astype(F32)
+    for step in range(PLANES):
+        lane = RANK * (step + 1)
+        limit_ref[:, step] = jnp.broadcast_to(near[:, lane:lane + 1][:, :, None], limit_ref.shape[:1] + limit_ref.shape[2:])
     projected = nt(down_ref[...], got) * pick
     partial = jnp.sum(projected.reshape(many // RANK, RANK, 2 * peers), axis=0)
     for t in range(partial_ref.shape[0]):
@@ -117,18 +136,21 @@
 
 
 def prepare_kernel(
-    list_ref, cache_ref, holder_ref, table_ref, base_ref, weight_ref, page_ref, route_ref, start_ref, down_ref
+    list_ref, cache_ref, holder_ref, table_ref, base_ref, weight_ref,
+    own_ref, one_ref, two_ref, three_ref, route_ref, start_ref, down_ref,
 ):
     down_ref[...] = weight_ref[...]
     count, owners = list_ref.shape
-
-    def step(o, carry):
-        for k in range(count):
-            at = pl.ds(pl.multiple_of((o * count + k) * PAGE, PAGE), PAGE)
-            page_ref[at, :] = cache_ref[list_ref[k, o]]
-        return carry
-
-    lax.fori_loop(0, owners, step, 0, unroll=8)
+    for step, page_ref in enumerate((own_ref, one_ref, two_ref, three_ref)):
+        first = ((my_plane() + step) & (PLANES - 1)) * DEPTH
+
+        def copy(z, carry, page_ref=page_ref, first=first):
+            for k in range(count):
+                at = pl.ds(pl.multiple_of((z * count + k) * PAGE, PAGE), PAGE)
+                page_ref[at, :] = cache_ref[list_ref[k, first + z]]
+            return carry
+
+        lax.fori_loop(0, DEPTH, copy, 0, unroll=8)
     maps = slot_maps(holder_ref[...], owners)
     moved = moved_map(table_ref[...], owners).astype(BF16)
     route_ref[...] = nt(jnp.concatenate(maps, axis=0), moved).astype(BF16)
@@ -137,12 +159,13 @@
         start_ref[:, h, :] = start[:, h * HEAD:(h + 1) * HEAD]
 
 
-def query_kernel(got_ref, route_ref, start_ref, out_ref, wide_ref):
+def query_kernel(got_ref, route_ref, start_ref, one_ref, two_ref, three_ref, out_ref, wide_ref):
+    del one_ref, two_ref, three_ref
     got = jnp.concatenate([got_ref[:, 0, :], got_ref[:, 1, :]], axis=0)
     chosen = tn(route_ref[...], got)
     for h in range(wide_ref.shape[1]):
         wide_ref[:, h, :] = chosen[:, h * HEAD:(h + 1) * HEAD]
-    out_ref[...] = (start_ref[...] + wide_ref[...]).astype(BF16)
+    out_ref[...] = (start_ref[...] + wide_ref[...]).reshape(out_ref.shape).astype(BF16)
 
 
 def weighted(scores, live, values):
@@ -194,34 +217,37 @@
         out_ref[:, h * HEAD:(h + 1) * HEAD] = (mixed_ref[:, h, :] * keep).astype(BF16)
 
 
-def moved_kernel(query_ref, page_ref, limit_ref, out_ref):
-    owners, heads, _ = query_ref.shape
-    span = page_ref.shape[0] // owners
+def moved_kernel(query_ref, own_ref, one_ref, two_ref, three_ref, limit_ref, out_ref, wide_ref):
+    depth, planes, heads, _ = limit_ref.shape
+    span = own_ref.shape[0] // depth
     batch = HEAD // span
-    groups = owners // batch
     wide = batch * heads
     shape = (wide, batch * span)
     own = lax.div(iota(shape, 0), heads) == lax.div(iota(shape, 1), span)
     place = jnp.where(own, lax.rem(iota(shape, 1), span), span).astype(F32)
-    query = query_ref[...].astype(F32).reshape(owners * heads, HEAD).astype(BF16)
-    pages = [page_ref[g * HEAD:(g + 1) * HEAD, :] for g in range(groups)]
-    scores = [nt(query[g * wide:(g + 1) * wide], pages[g][:, :HEAD]) for g in range(groups)]
-    live = [
-        place < limit_ref[g * batch:(g + 1) * batch].reshape(wide, HEAD) for g in range(groups)
+    query = query_ref[...].astype(F32)
+    parts = [(d, z) for d in range(planes) for z in range(0, depth, batch)]
+    handed = (own_ref, one_ref, two_ref, three_ref)
+    pages = [handed[d][z * span:(z + batch) * span, :] for d, z in parts]
+    queries = [
+        query[z:z + batch, d * heads:(d + 1) * heads].reshape(wide, HEAD).astype(BF16) for d, z in parts
     ]
+    scores = [nt(q, page[:, :HEAD]) for q, page in zip(queries, pages)]
+    live = [place < limit_ref[z:z + batch, d].reshape(wide, HEAD) for d, z in parts]
     scores = [jnp.where(m, x * (HEAD ** -0.5), NEG) for m, x in zip(live, scores)]
     tops = [jnp.max(x, axis=1, keepdims=True) for x in scores]
     weights = [jnp.exp(x - top) for x, top in zip(scores, tops)]
     totals = [jnp.sum(x, axis=1, keepdims=True) for x in weights]
     weights = [(x / total).astype(BF16) for x, total in zip(weights, totals)]
     mixed = [nn(x, page[:, HEAD:]) for x, page in zip(weights, pages)]
-    for g in range(groups):
-        out_ref[g * batch:(g + 1) * batch] = mixed[g].reshape(batch, heads, HEAD).astype(BF16)
+    for (d, z), x in zip(parts, mixed):
+        wide_ref[z:z + batch, d * heads:(d + 1) * heads] = x.reshape(batch, heads, HEAD)
+    out_ref[...] = wide_ref[...].astype(BF16)
 
 
 def final_kernel(got_ref, local_ref, table_ref, out_ref, wide_ref):
-    peers, heads, _ = got_ref.shape
-    wide_ref[...] = got_ref[...].astype(F32)
+    peers, heads, _ = wide_ref.shape
+    wide_ref[...] = got_ref[...].astype(F32).reshape(wide_ref.shape)
     moved = moved_map(table_ref[...], peers).astype(BF16)
     for h in range(heads):
         part = tn(moved, wide_ref[:, h, :].astype(BF16))
@@ -230,7 +256,7 @@
 
 
 def call(kernel, out_shape, cost, spaces, scratch=(), limit=24):
-    kinds = {"s": pltpu.SMEM, "v": pltpu.VMEM, "h": pltpu.HBM}
+    kinds = {"s": pltpu.SMEM, "v": pltpu.VMEM, "h": pltpu.HBM, "a": pl.ANY}
     return pl.pallas_call(
         kernel,
         out_shape=out_shape,
@@ -242,8 +268,19 @@
     )
 
 
-def exchange(x, axis="replica"):
-    return lax.all_to_all(x, axis, split_axis=0, concat_axis=0, tiled=True)
+def exchange(x, axis="replica", groups=None):
+    return lax.all_to_all(x, axis, split_axis=0, concat_axis=0, tiled=True, axis_index_groups=groups)
+
+
+def along_depth(x):
+    return exchange(x, groups=[[p * DEPTH + z for z in range(DEPTH)] for p in range(PLANES)])
+
+
+def hand_on(x, step):
+    pairs = [
+        (p * DEPTH + z, (p + step) % PLANES * DEPTH + z) for p in range(PLANES) for z in range(DEPTH)
+    ]
+    return lax.ppermute(x, "replica", pairs)
 
 
 def body(
@@ -282,10 +319,14 @@
         limit=60,
     )(hidden, holder, position, table, length)
     got = exchange(sent)
-    pages, route, start, down = call(
+    handed = S((DEPTH * lists.shape[0] * PAGE, 2 * HEAD), BF16)
+    *pages, route, start, down = call(
         prepare_kernel,
         (
-            S((peers * lists.shape[0] * PAGE, 2 * HEAD), BF16),
+            handed,
+            handed,
+            handed,
+            handed,
             S((2 * peers, peers), BF16),
             S((peers, heads, HEAD), F32),
             S(down.shape, BF16),
@@ -293,10 +334,11 @@
         10**9,
         "svvvvv",
     )(lists, key_value_cache, holder, table, base_query, down)
+    pages = [pages[0]] + [hand_on(pages[step], step) for step in range(1, PLANES)]
 
     partial, pick, limit = call(
         down_kernel,
-        (S((shards, RANK, 2 * peers), F32), S((many, 2 * peers), BF16), S((peers, heads, HEAD), F32)),
+        (S((shards, RANK, 2 * peers), F32), S((many, 2 * peers), BF16), S((DEPTH, PLANES, heads, HEAD), F32)),
         10**8,
         "vv",
     )(got, down)
@@ -304,14 +346,15 @@
     delta = call(up_kernel, S((peers, 2, features), BF16), 10**8, "vvv")(partials, pick, up)
     returned = exchange(delta)
     wide = pltpu.VMEM((rows, heads, HEAD), F32)
-    asked = exchange(
-        call(query_kernel, S((peers, heads, HEAD), BF16), 10**8, "vvv", (wide,))(returned, route, start)
+    flat = (DEPTH, PLANES * heads, HEAD)
+    asked = along_depth(
+        call(query_kernel, S(flat, BF16), 10**8, "vvvaaa", (wide,))(returned, route, start, *pages[1:])
     )
     local = call(local_kernel, S((rows, features), BF16), 10**9, "ssvvvvv", (wide, wide))(
         table, length, returned, base_query, holder, table, key_value_cache
     )
-    answered = exchange(
-        call(moved_kernel, S((peers, heads, HEAD), BF16), 10**8, "vvv")(asked, pages, limit)
+    answered = along_depth(
+        call(moved_kernel, S(flat, BF16), 10**8, "vvvvvv", (pltpu.VMEM(flat, F32),))(asked, *pages, limit)
     )
     return call(final_kernel, S((rows, features), BF16), 10**8, "vvv", (wide,))(answered, local, table)
 

time: 127 us -> 131 us (1.031)
  the two profiles are of different devices: /device:TPU:6 before, /device:TPU:2 now
where the time goes in v3:
time: 131 us; the launch traced here: 130 us
  starting transfers between devices  39.9 us (30%)
  blocking collectives  35.5 us (27%)
  waiting for transfers between devices  31.9 us (24%)
  Pallas kernels  15.7 us (12%)
  local copies, waits for them, and re-layouts  7.15 us (5%)
    all_to_all x2, blocking collectives, exchange(): lax.all_to_all(x, axis, split_axis=0, concat_axis=0, tiled=True, axis_ind...  35.5 us
    all_to_all x3, starting transfers between devices, exchange(): lax.all_to_all(x, axis, split_axis=0, concat_axis=0, tiled=True, axis_ind...  29.3 us
    all_to_all x3, waiting for transfers between devices, exchange(): lax.all_to_all(x, axis, split_axis=0, concat_axis=0, tiled=True, axis_ind...  21 us
    ppermute x3, waiting for transfers between devices, hand_on(): return lax.ppermute(x, 'replica', pairs)  10.8 us
    ppermute x3, starting transfers between devices, hand_on(): return lax.ppermute(x, 'replica', pairs)  10.6 us
    pallas_call x1, Pallas kernels, body(): call(local_kernel, S((rows, features), BF16), 10 ** 9, 'ssvvvvv', (wide,...  7.22 us
    unnamed x24, local copies, waits for them, and re-layouts  7.15 us
  transfers between devices with their start and end apart: 6, of which 5 were waited for; matrix products, arithmetic and copies ran while one was open for 0% of the time, Pallas kernels for 7%

profile of v3, /device:TPU:2, one launch (start us, length us, event | category | flops | bytes accessed | tf_op | source)
XLA Modules:
  0.0 130.3 jit_solution(8140803394565359808)
XLA Ops:
  0.0 2.0 %shard_map.100 = bf16[64,2,1152]{2,1,0:T(2,128)(2,1)} custom-call(bf16[64,1024]{1,0:T(8,128)(2,1)} %hidden_hbm.1, s32[1,64]{1,0:T(1,128)} %bitcast.15, s32[1,64]{1,0:T(1,128)} %bitcast.22, s32[4,64]{1,0:T(4,128)} %bitcast.10, s32[1,64]{1,0:T(1,128)} %bitcast.18), custom_call_target="tpu_custom_call" | custom-call | flops 100000000 | bytes 1000000 | tf_op jit(solution)/shard_map/pallas_call | solution.py:313
  2.1 18.7 %all-to-all-start = ((bf16[64,2,1152]{2,1,0:T(2,128)(2,1)}), bf16[64,2,1152]{2,1,0:T(2,128)(2,1)S(1)}, u32[]{:S(2)}, u32[]{:S(2)}) async-start(bf16[64,2,1152]{2,1,0:T(2,128)(2,1)} %shard_map.100), calls=%async_computation | async-start | bytes 589824 | tf_op jit(solution)/shard_map/all_to_all | solution.py:272
  20.7 0.0 copy-start.1
  20.7 0.7 copy-done.1
  21.4 0.7 copy-done.3
  22.1 1.6 %copy-done.6 = bf16[256,16,256]{2,1,0:T(8,128)(2,1)S(1)} copy-done((bf16[256,16,256]{2,1,0:T(8,128)(2,1)S(1)}, bf16[256,16,256]{2,1,0:T(8,128)(2,1)}, u32[]{:S(2)}) %copy-start.6) | copy-done | bytes 2097176
  23.7 1.0 copy-done.8
  24.7 0.9 copy-done.9
  25.6 0.7 copy-done.11
  26.3 1.3 %shard_map.101 = (bf16[512,256]{1,0:T(8,128)(2,1)S(1)}, bf16[512,256]{1,0:T(8,128)(2,1)S(1)}, bf16[512,256]{1,0:T(8,128)(2,1)S(1)}, bf16[512,256]{1,0:T(8,128)(2...) custom-call(s32[2,64]{1,0:T(2,128)S(1)} %bitcast.21, ...), custom_call_target="tpu_custom_call" | custom-call | flops 1000000000 | bytes 10000000 | tf_op jit(solution)/shard_map/pallas_call | solution.py:323
  27.6 15.4 %all-to-all-done.got_ref = bf16[64,2,1152]{2,1,0:T(2,128)(2,1)S(1)} async-done(((bf16[64,2,1152]{2,1,0:T(2,128)(2,1)}), bf16[64,2,1152]{2,1,0:T(2,128)(2,1)S(1)}, u32[]{:S(2)}, u32[]{:S(2)}) %all-to-all-start) | async-done | bytes 294944 | tf_op jit(solution)/shard_map/all_to_all | solution.py:272
  43.0 0.9 shard_map.102
  43.9 9.9 %all_to_all.25.got_ref = f32[8,16,128]{2,1,0:T(8,128)S(1)} all-to-all(f32[8,16,128]{2,1,0:T(8,128)S(1)} %get-tuple-element.16), channel_id=1, replica_groups=mesh['replica'=64,'tensor'=8] {'tensor'}, dimensions={0} | all-to-all | bytes 131072 | tf_op jit(solution)/shard_map/all_to_all | solution.py:272
  53.8 1.0 shard_map.103
  54.8 6.7 %all-to-all-start.2 = ((bf16[64,2,1024]{2,1,0:T(2,128)(2,1)}), bf16[64,2,1024]{2,1,0:T(2,128)(2,1)S(1)}, u32[]{:S(2)}, u32[]{:S(2)}) async-start(bf16[64,2,1024]{2,1,0:T(2,128)(2,1)} %shard_map.103), calls=%async_computation.2 | async-start | bytes 524288 | tf_op jit(solution)/shard_map/all_to_all | solution.py:272
  61.6 3.5 %collective-permute-start = (bf16[512,256]{1,0:T(8,128)(2,1)S(1)}, bf16[512,256]{1,0:T(8,128)(2,1)S(1)}, u32[]{:S(2)}, u32[]{:S(2)}) collective-permute-start(bf16[512,256]{1,0:T(8,128)(2,1)S(1)} %get-tuple-element.20), channel_id=1, source_target_pairs={{0,128},{8,136},{16,144},{24,152},{32,160},{40,168},{48,176},{56,1... | collective-permute-start | bytes 786440 | tf_op jit(solution)/shard_map/ppermute | solution.py:283
  65.0 2.9 %collective-permute-start.1 = (bf16[512,256]{1,0:T(8,128)(2,1)S(1)}, bf16[512,256]{1,0:T(8,128)(2,1)S(1)}, u32[]{:S(2)}, u32[]{:S(2)}) collective-permute-start(bf16[512,256]{1,0:T(8,128)(2,1)S(1)} %get-tuple-element.21), channel_id=1, source_target_pairs={{0,256},{8,264},{16,272},{24,280},{32,288},{40,296},{48,304},{56,3... | collective-permute-start | bytes 786440 | tf_op jit(solution)/shard_map/ppermute | solution.py:283
  67.9 4.3 %collective-permute-start.2 = (bf16[512,256]{1,0:T(8,128)(2,1)S(1)}, bf16[512,256]{1,0:T(8,128)(2,1)S(1)}, u32[]{:S(2)}, u32[]{:S(2)}) collective-permute-start(bf16[512,256]{1,0:T(8,128)(2,1)S(1)} %get-tuple-element.22), channel_id=1, source_target_pairs={{0,384},{8,392},{16,400},{24,408},{32,416},{40,424},{48,432},{56,4... | collective-permute-start | bytes 786440 | tf_op jit(solution)/shard_map/ppermute | solution.py:283
  72.2 2.4 %collective-permute-done.one_ref = bf16[512,256]{1,0:T(8,128)(2,1)S(1)} collective-permute-done((bf16[512,256]{1,0:T(8,128)(2,1)S(1)}, bf16[512,256]{1,0:T(8,128)(2,1)S(1)}, u32[]{:S(2)}, u32[]{:S(2)}) %collective-permute-start) | collective-permute-done | bytes 262176 | tf_op jit(solution)/shard_map/ppermute | solution.py:283
  74.6 4.3 %collective-permute-done.1.two_ref = bf16[512,256]{1,0:T(8,128)(2,1)S(1)} collective-permute-done((bf16[512,256]{1,0:T(8,128)(2,1)S(1)}, bf16[512,256]{1,0:T(8,128)(2,1)S(1)}, u32[]{:S(2)}, u32[]{:S(2)}) %collective-permute-start.1) | collective-permute-done | bytes 262176 | tf_op jit(solution)/shard_map/ppermute | solution.py:283
  78.9 4.1 %collective-permute-done.2.three_ref = bf16[512,256]{1,0:T(8,128)(2,1)S(1)} collective-permute-done((bf16[512,256]{1,0:T(8,128)(2,1)S(1)}, bf16[512,256]{1,0:T(8,128)(2,1)S(1)}, u32[]{:S(2)}, u32[]{:S(2)}) %collective-permute-start.2) | collective-permute-done | bytes 262176 | tf_op jit(solution)/shard_map/ppermute | solution.py:283
  83.0 0.0 all-to-all-done.2.got_ref
  83.0 0.8 shard_map.104
  83.8 25.6 %all_to_all.26.query_ref = bf16[16,32,128]{2,1,0:T(8,128)(2,1)S(1)} all-to-all(bf16[16,32,128]{2,1,0:T(8,128)(2,1)S(1)} %shard_map.104), channel_id=1, replica_groups={{0,8,16,24,32,40,48,56,64,72,80,88,96,104,112,120},{128,136,144,152,160..., dimensions={0} | all-to-all | bytes 262144 | tf_op jit(solution)/shard_map/all_to_all | solution.py:272
  109.4 1.3 %shard_map.105 = bf16[16,32,128]{2,1,0:T(8,128)(2,1)} custom-call(bf16[16,32,128]{2,1,0:T(8,128)(2,1)S(1)} %all_to_all.26.query_ref, bf16[512,256]{1,0:T(8,128)(2,1)S(1)} %get-tuple-element.23.own_ref, bf16[512,256]{1,0:T(8,128)(2,1)S(1)} %collective-permute-done.one_ref, bf16[512,256]{1,0:T(8,128)(2,1)S(1)} %collective-permute-done.1.two_ref, ...), custom_call_target="tpu_custom_call" | custom-call | flops 100000000 | bytes 1000000 | tf_op jit(solution)/shard_map/pallas_call | solution.py:357
  110.8 3.9 %all-to-all-start.4 = ((bf16[16,32,128]{2,1,0:T(8,128)(2,1)}), bf16[16,32,128]{2,1,0:T(8,128)(2,1)S(1)}, u32[]{:S(2)}, u32[]{:S(2)}) async-start(bf16[16,32,128]{2,1,0:T(8,128)(2,1)} %shard_map.105), calls=%async_computation.4 | async-start | bytes 262144 | tf_op jit(solution)/shard_map/all_to_all | solution.py:272
  114.7 0.0 copy-done.2
  114.7 0.0 copy-start.7
  114.7 1.6 %copy-done.7 = bf16[256,16,256]{2,1,0:T(8,128)(2,1)S(1)} copy-done((bf16[256,16,256]{2,1,0:T(8,128)(2,1)S(1)}, bf16[256,16,256]{2,1,0:T(8,128)(2,1)}, u32[]{:S(2)}) %copy-start.7) | copy-done | bytes 2097176
  116.3 7.2 %shard_map.106.local_ref = bf16[64,1024]{1,0:T(8,128)(2,1)S(1)} custom-call(s32[4,64]{1,0:T(4,128)S(1)} %bitcast.12, s32[1,64]{1,0:T(1,128)S(1)} %bitcast.19, bf16[64,2,1024]{2,1,0:T(2,128)(2,1)S(1)} %all-to-all-done.2.got_ref, bf16[64,1024]{1,0:T(8,128)(2,1)S(1)} %copy-done.10, s32[1,64]{1,0:T(1,128)S(1)} %bitcast.17, s32[4,64]{1,0:T(4,128)S(1)} %bitcast.13, ...), custom_call_target="tpu_custom_call" | custom-call | flops 1000000000 | bytes 10000000 | tf_op jit(solution)/shard_map/pallas_call | solution.py:353
  123.5 5.7 %all-to-all-done.4.got_ref = bf16[16,32,128]{2,1,0:T(8,128)(2,1)S(1)} async-done(((bf16[16,32,128]{2,1,0:T(8,128)(2,1)}), bf16[16,32,128]{2,1,0:T(8,128)(2,1)S(1)}, u32[]{:S(2)}, u32[]{:S(2)}) %all-to-all-start.4) | async-done | bytes 131104 | tf_op jit(solution)/shard_map/all_to_all | solution.py:272
  129.2 1.1 shard_map.107
  (14 shorter events, 0.0 us)
Async XLA Ops:
  2.1 40.9 %all-to-all-start = ((bf16[64,2,1152]{2,1,0:T(2,128)(2,1)}), bf16[64,2,1152]{2,1,0:T(2,128)(2,1)S(1)}, u32[]{:S(2)}, u32[]{:S(2)}) async-start(bf16[64,2,1152]{2,1,0:T(2,128)(2,1)} %shard_map.100), calls=%async_computation | async-start | bytes 589824 | tf_op jit(solution)/shard_map/all_to_all | solution.py:272
  20.7 0.7 copy-start.1
  21.4 0.7 copy-start.3
  22.1 1.6 %copy-start.6 = (bf16[256,16,256]{2,1,0:T(8,128)(2,1)S(1)}, bf16[256,16,256]{2,1,0:T(8,128)(2,1)}, u32[]{:S(2)}) copy-start(bf16[256,16,256]{2,1,0:T(8,128)(2,1)} %cache_ref.3) | copy-start | bytes 6291460
  23.7 1.0 copy-start.8
  24.7 0.9 copy-start.9
  25.6 0.7 copy-start.11
  26.3 27.5 %copy-start = (bf16[16,16,1024]{2,1,0:T(8,128)(2,1)S(1)}, bf16[16,16,1024]{2,1,0:T(8,128)(2,1)}, u32[]{:S(2)}) copy-start(bf16[16,16,1024]{2,1,0:T(8,128)(2,1)} %param.14) | copy-start | bytes 1572868
  54.8 59.8 %copy-start.2 = (s32[64,4]{0,1:T(4,128)S(1)}, s32[64,4]{0,1:T(4,128)}, u32[]{:S(2)}) copy-start(s32[64,4]{0,1:T(4,128)} %param.17) | copy-start | bytes 3076
  54.8 59.9 %copy-start.4 = (s32[64,1]{0,1:T(1,128)S(1)}, s32[64,1]{0,1:T(1,128)}, u32[]{:S(2)}) copy-start(s32[64,1]{0,1:T(1,128)} %param.15) | copy-start | bytes 772
  54.8 59.9 %copy-start.5 = (s32[64]{0:T(128)S(1)}, s32[64]{0:T(128)}, u32[]{:S(2)}) copy-start(s32[64]{0:T(128)} %param.18) | copy-start | bytes 772
  54.8 59.9 %copy-start.10 = (bf16[64,1024]{1,0:T(8,128)(2,1)S(1)}, bf16[64,1024]{1,0:T(8,128)(2,1)}, u32[]{:S(2)}) copy-start(bf16[64,1024]{1,0:T(8,128)(2,1)} %base_ref.3) | copy-start | bytes 393220
  54.8 28.2 %all-to-all-start.2 = ((bf16[64,2,1024]{2,1,0:T(2,128)(2,1)}), bf16[64,2,1024]{2,1,0:T(2,128)(2,1)S(1)}, u32[]{:S(2)}, u32[]{:S(2)}) async-start(bf16[64,2,1024]{2,1,0:T(2,128)(2,1)} %shard_map.103), calls=%async_computation.2 | async-start | bytes 524288 | tf_op jit(solution)/shard_map/all_to_all | solution.py:272
  61.6 13.0 %collective-permute-start = (bf16[512,256]{1,0:T(8,128)(2,1)S(1)}, bf16[512,256]{1,0:T(8,128)(2,1)S(1)}, u32[]{:S(2)}, u32[]{:S(2)}) collective-permute-start(bf16[512,256]{1,0:T(8,128)(2,1)S(1)} %get-tuple-element.20), channel_id=1, source_target_pairs={{0,128},{8,136},{16,144},{24,152},{32,160},{40,168},{48,176},{56,1... | collective-permute-start | bytes 786440 | tf_op jit(solution)/shard_map/ppermute | solution.py:283
  65.0 13.9 %collective-permute-start.1 = (bf16[512,256]{1,0:T(8,128)(2,1)S(1)}, bf16[512,256]{1,0:T(8,128)(2,1)S(1)}, u32[]{:S(2)}, u32[]{:S(2)}) collective-permute-start(bf16[512,256]{1,0:T(8,128)(2,1)S(1)} %get-tuple-element.21), channel_id=1, source_target_pairs={{0,256},{8,264},{16,272},{24,280},{32,288},{40,296},{48,304},{56,3... | collective-permute-start | bytes 786440 | tf_op jit(solution)/shard_map/ppermute | solution.py:283
  67.9 15.1 %collective-permute-start.2 = (bf16[512,256]{1,0:T(8,128)(2,1)S(1)}, bf16[512,256]{1,0:T(8,128)(2,1)S(1)}, u32[]{:S(2)}, u32[]{:S(2)}) collective-permute-start(bf16[512,256]{1,0:T(8,128)(2,1)S(1)} %get-tuple-element.22), channel_id=1, source_target_pairs={{0,384},{8,392},{16,400},{24,408},{32,416},{40,424},{48,432},{56,4... | collective-permute-start | bytes 786440 | tf_op jit(solution)/shard_map/ppermute | solution.py:283
  110.8 18.5 %all-to-all-start.4 = ((bf16[16,32,128]{2,1,0:T(8,128)(2,1)}), bf16[16,32,128]{2,1,0:T(8,128)(2,1)S(1)}, u32[]{:S(2)}, u32[]{:S(2)}) async-start(bf16[16,32,128]{2,1,0:T(8,128)(2,1)} %shard_map.105), calls=%async_computation.4 | async-start | bytes 262144 | tf_op jit(solution)/shard_map/all_to_all | solution.py:272
  114.7 1.6 %copy-start.7 = (bf16[256,16,256]{2,1,0:T(8,128)(2,1)S(1)}, bf16[256,16,256]{2,1,0:T(8,128)(2,1)}, u32[]{:S(2)}) copy-start(bf16[256,16,256]{2,1,0:T(8,128)(2,1)} %cache_ref.3) | copy-start | bytes 6291460

commit v4 on v3

--- a/solution.py
+++ b/solution.py
@@ -105,7 +105,8 @@
         out_ref[:, c, :features] = nn(maps[c], hidden).astype(BF16)
 
 
-def down_kernel(got_ref, down_ref, partial_ref, pick_ref, limit_ref):
+def down_kernel(got_ref, down_ref, two_ref, partial_ref, pick_ref, limit_ref):
+    del two_ref
     peers, _, width = got_ref.shape
     features = width - HEAD
     many = down_ref.shape[0]
@@ -159,8 +160,8 @@
         start_ref[:, h, :] = start[:, h * HEAD:(h + 1) * HEAD]
 
 
-def query_kernel(got_ref, route_ref, start_ref, one_ref, two_ref, three_ref, out_ref, wide_ref):
-    del one_ref, two_ref, three_ref
+def query_kernel(got_ref, route_ref, start_ref, one_ref, three_ref, out_ref, wide_ref):
+    del one_ref, three_ref
     got = jnp.concatenate([got_ref[:, 0, :], got_ref[:, 1, :]], axis=0)
     chosen = tn(route_ref[...], got)
     for h in range(wide_ref.shape[1]):
@@ -340,15 +341,15 @@
         down_kernel,
         (S((shards, RANK, 2 * peers), F32), S((many, 2 * peers), BF16), S((DEPTH, PLANES, heads, HEAD), F32)),
         10**8,
-        "vv",
-    )(got, down)
+        "vva",
+    )(got, down, pages[2])
     partials = exchange(partial, "tensor")
     delta = call(up_kernel, S((peers, 2, features), BF16), 10**8, "vvv")(partials, pick, up)
     returned = exchange(delta)
     wide = pltpu.VMEM((rows, heads, HEAD), F32)
     flat = (DEPTH, PLANES * heads, HEAD)
     asked = along_depth(
-        call(query_kernel, S(flat, BF16), 10**8, "vvvaaa", (wide,))(returned, route, start, *pages[1:])
+        call(query_kernel, S(flat, BF16), 10**8, "vvvaa", (wide,))(returned, route, start, pages[1], pages[3])
     )
     local = call(local_kernel, S((rows, features), BF16), 10**9, "ssvvvvv", (wide, wide))(
         table, length, returned, base_query, holder, table, key_value_cache

time: 131 us -> 126 us (0.962)
  the two profiles are of different devices: /device:TPU:2 before, /device:TPU:6 now
where the time goes in v4:
time: 126 us; the launch traced here: 125 us
  starting transfers between devices  42.3 us (34%)
  waiting for transfers between devices  31.7 us (25%)
  blocking collectives  28.4 us (23%)
  Pallas kernels  15.8 us (13%)
  local copies, waits for them, and re-layouts  7.15 us (6%)
    all_to_all x3, starting transfers between devices, exchange(): lax.all_to_all(x, axis, split_axis=0, concat_axis=0, tiled=True, axis_ind...  33.3 us
    all_to_all x2, blocking collectives, exchange(): lax.all_to_all(x, axis, split_axis=0, concat_axis=0, tiled=True, axis_ind...  28.4 us
    ppermute x3, waiting for transfers between devices, hand_on(): return lax.ppermute(x, 'replica', pairs)  17.1 us
    all_to_all x3, waiting for transfers between devices, exchange(): lax.all_to_all(x, axis, split_axis=0, concat_axis=0, tiled=True, axis_ind...  14.6 us
    ppermute x3, starting transfers between devices, hand_on(): return lax.ppermute(x, 'replica', pairs)  9.01 us
    pallas_call x1, Pallas kernels, body(): call(local_kernel, S((rows, features), BF16), 10 ** 9, 'ssvvvvv', (wide,...  7.23 us
    unnamed x24, local copies, waits for them, and re-layouts  7.15 us
  transfers between devices with their start and end apart: 6, of which 6 were waited for; matrix products, arithmetic and copies ran while one was open for 0% of the time, Pallas kernels for 7%

profile of v4, /device:TPU:6, one launch (start us, length us, event | category | flops | bytes accessed | tf_op | source)
XLA Modules:
  0.0 125.5 jit_solution(16113276191267056417)
XLA Ops:
  0.0 2.1 %shard_map.100 = bf16[64,2,1152]{2,1,0:T(2,128)(2,1)} custom-call(bf16[64,1024]{1,0:T(8,128)(2,1)} %hidden_hbm.1, s32[1,64]{1,0:T(1,128)} %bitcast.15, s32[1,64]{1,0:T(1,128)} %bitcast.22, s32[4,64]{1,0:T(4,128)} %bitcast.10, s32[1,64]{1,0:T(1,128)} %bitcast.18), custom_call_target="tpu_custom_call" | custom-call | flops 100000000 | bytes 1000000 | tf_op jit(solution)/shard_map/pallas_call | solution.py:314
  2.1 18.8 %all-to-all-start = ((bf16[64,2,1152]{2,1,0:T(2,128)(2,1)}), bf16[64,2,1152]{2,1,0:T(2,128)(2,1)S(1)}, u32[]{:S(2)}, u32[]{:S(2)}) async-start(bf16[64,2,1152]{2,1,0:T(2,128)(2,1)} %shard_map.100), calls=%async_computation | async-start | bytes 589824 | tf_op jit(solution)/shard_map/all_to_all | solution.py:273
  20.9 0.0 copy-start.1
  20.9 0.7 copy-done.1
  21.6 0.7 copy-done.3
  22.2 1.6 %copy-done.6 = bf16[256,16,256]{2,1,0:T(8,128)(2,1)S(1)} copy-done((bf16[256,16,256]{2,1,0:T(8,128)(2,1)S(1)}, bf16[256,16,256]{2,1,0:T(8,128)(2,1)}, u32[]{:S(2)}) %copy-start.6) | copy-done | bytes 2097176
  23.8 1.0 copy-done.8
  24.8 0.9 copy-done.9
  25.7 0.7 copy-done.11
  26.4 1.3 %shard_map.101 = (bf16[512,256]{1,0:T(8,128)(2,1)S(1)}, bf16[512,256]{1,0:T(8,128)(2,1)S(1)}, bf16[512,256]{1,0:T(8,128)(2,1)S(1)}, bf16[512,256]{1,0:T(8,128)(2...) custom-call(s32[2,64]{1,0:T(2,128)S(1)} %bitcast.21, ...), custom_call_target="tpu_custom_call" | custom-call | flops 1000000000 | bytes 10000000 | tf_op jit(solution)/shard_map/pallas_call | solution.py:324
  27.8 3.2 %collective-permute-start = (bf16[512,256]{1,0:T(8,128)(2,1)S(1)}, bf16[512,256]{1,0:T(8,128)(2,1)S(1)}, u32[]{:S(2)}, u32[]{:S(2)}) collective-permute-start(bf16[512,256]{1,0:T(8,128)(2,1)S(1)} %get-tuple-element.16), channel_id=1, source_target_pairs={{0,256},{8,264},{16,272},{24,280},{32,288},{40,296},{48,304},{56,3... | collective-permute-start | bytes 786440 | tf_op jit(solution)/shard_map/ppermute | solution.py:284
  30.9 8.7 %collective-permute-done.two_ref = bf16[512,256]{1,0:T(8,128)(2,1)S(1)} collective-permute-done((bf16[512,256]{1,0:T(8,128)(2,1)S(1)}, bf16[512,256]{1,0:T(8,128)(2,1)S(1)}, u32[]{:S(2)}, u32[]{:S(2)}) %collective-permute-start) | collective-permute-done | bytes 262176 | tf_op jit(solution)/shard_map/ppermute | solution.py:284
  39.7 3.5 %all-to-all-done.got_ref = bf16[64,2,1152]{2,1,0:T(2,128)(2,1)S(1)} async-done(((bf16[64,2,1152]{2,1,0:T(2,128)(2,1)}), bf16[64,2,1152]{2,1,0:T(2,128)(2,1)S(1)}, u32[]{:S(2)}, u32[]{:S(2)}) %all-to-all-start) | async-done | bytes 294944 | tf_op jit(solution)/shard_map/all_to_all | solution.py:273
  43.1 0.9 shard_map.102
  44.1 9.9 %all_to_all.25.got_ref = f32[8,16,128]{2,1,0:T(8,128)S(1)} all-to-all(f32[8,16,128]{2,1,0:T(8,128)S(1)} %get-tuple-element.17), channel_id=1, replica_groups=mesh['replica'=64,'tensor'=8] {'tensor'}, dimensions={0} | all-to-all | bytes 131072 | tf_op jit(solution)/shard_map/all_to_all | solution.py:273
  54.0 0.0 copy-done
  54.0 1.0 shard_map.103
  55.0 11.0 %all-to-all-start.2 = ((bf16[64,2,1024]{2,1,0:T(2,128)(2,1)}), bf16[64,2,1024]{2,1,0:T(2,128)(2,1)S(1)}, u32[]{:S(2)}, u32[]{:S(2)}) async-start(bf16[64,2,1024]{2,1,0:T(2,128)(2,1)} %shard_map.103), calls=%async_computation.2 | async-start | bytes 524288 | tf_op jit(solution)/shard_map/all_to_all | solution.py:273
  66.0 2.2 %collective-permute-start.1 = (bf16[512,256]{1,0:T(8,128)(2,1)S(1)}, bf16[512,256]{1,0:T(8,128)(2,1)S(1)}, u32[]{:S(2)}, u32[]{:S(2)}) collective-permute-start(bf16[512,256]{1,0:T(8,128)(2,1)S(1)} %get-tuple-element.21), channel_id=1, source_target_pairs={{0,128},{8,136},{16,144},{24,152},{32,160},{40,168},{48,176},{56,1... | collective-permute-start | bytes 786440 | tf_op jit(solution)/shard_map/ppermute | solution.py:284
  68.1 3.7 %collective-permute-start.2 = (bf16[512,256]{1,0:T(8,128)(2,1)S(1)}, bf16[512,256]{1,0:T(8,128)(2,1)S(1)}, u32[]{:S(2)}, u32[]{:S(2)}) collective-permute-start(bf16[512,256]{1,0:T(8,128)(2,1)S(1)} %get-tuple-element.22), channel_id=1, source_target_pairs={{0,384},{8,392},{16,400},{24,408},{32,416},{40,424},{48,432},{56,4... | collective-permute-start | bytes 786440 | tf_op jit(solution)/shard_map/ppermute | solution.py:284
  71.8 5.0 %collective-permute-done.1.one_ref = bf16[512,256]{1,0:T(8,128)(2,1)S(1)} collective-permute-done((bf16[512,256]{1,0:T(8,128)(2,1)S(1)}, bf16[512,256]{1,0:T(8,128)(2,1)S(1)}, u32[]{:S(2)}, u32[]{:S(2)}) %collective-permute-start.1) | collective-permute-done | bytes 262176 | tf_op jit(solution)/shard_map/ppermute | solution.py:284
  76.8 3.3 %collective-permute-done.2.three_ref = bf16[512,256]{1,0:T(8,128)(2,1)S(1)} collective-permute-done((bf16[512,256]{1,0:T(8,128)(2,1)S(1)}, bf16[512,256]{1,0:T(8,128)(2,1)S(1)}, u32[]{:S(2)}, u32[]{:S(2)}) %collective-permute-start.2) | collective-permute-done | bytes 262176 | tf_op jit(solution)/shard_map/ppermute | solution.py:284
  80.2 6.6 %all-to-all-done.2.got_ref = bf16[64,2,1024]{2,1,0:T(2,128)(2,1)S(1)} async-done(((bf16[64,2,1024]{2,1,0:T(2,128)(2,1)}), bf16[64,2,1024]{2,1,0:T(2,128)(2,1)S(1)}, u32[]{:S(2)}, u32[]{:S(2)}) %all-to-all-start.2) | async-done | bytes 262176 | tf_op jit(solution)/shard_map/all_to_all | solution.py:273
  86.7 0.8 shard_map.104
  87.5 18.5 %all_to_all.26.query_ref = bf16[16,32,128]{2,1,0:T(8,128)(2,1)S(1)} all-to-all(bf16[16,32,128]{2,1,0:T(8,128)(2,1)S(1)} %shard_map.104), channel_id=1, replica_groups={{0,8,16,24,32,40,48,56,64,72,80,88,96,104,112,120},{128,136,144,152,160..., dimensions={0} | all-to-all | bytes 262144 | tf_op jit(solution)/shard_map/all_to_all | solution.py:273
  106.1 1.3 %shard_map.105 = bf16[16,32,128]{2,1,0:T(8,128)(2,1)} custom-call(bf16[16,32,128]{2,1,0:T(8,128)(2,1)S(1)} %all_to_all.26.query_ref, bf16[512,256]{1,0:T(8,128)(2,1)S(1)} %get-tuple-element.23.own_ref, bf16[512,256]{1,0:T(8,128)(2,1)S(1)} %collective-permute-done.1.one_ref, bf16[512,256]{1,0:T(8,128)(2,1)S(1)} %collective-permute-done.two_ref, ...), custom_call_target="tpu_custom_call" | custom-call | flops 100000000 | bytes 1000000 | tf_op jit(solution)/shard_map/pallas_call | solution.py:358
  107.4 3.5 %all-to-all-start.4 = ((bf16[16,32,128]{2,1,0:T(8,128)(2,1)}), bf16[16,32,128]{2,1,0:T(8,128)(2,1)S(1)}, u32[]{:S(2)}, u32[]{:S(2)}) async-start(bf16[16,32,128]{2,1,0:T(8,128)(2,1)} %shard_map.105), calls=%async_computation.4 | async-start | bytes 262144 | tf_op jit(solution)/shard_map/all_to_all | solution.py:273
  111.0 0.0 copy-start.7
  111.0 1.6 %copy-done.7 = bf16[256,16,256]{2,1,0:T(8,128)(2,1)S(1)} copy-done((bf16[256,16,256]{2,1,0:T(8,128)(2,1)S(1)}, bf16[256,16,256]{2,1,0:T(8,128)(2,1)}, u32[]{:S(2)}) %copy-start.7) | copy-done | bytes 2097176
  112.6 7.2 %shard_map.106.local_ref = bf16[64,1024]{1,0:T(8,128)(2,1)S(1)} custom-call(s32[4,64]{1,0:T(4,128)S(1)} %bitcast.12, s32[1,64]{1,0:T(1,128)S(1)} %bitcast.19, bf16[64,2,1024]{2,1,0:T(2,128)(2,1)S(1)} %all-to-all-done.2.got_ref, bf16[64,1024]{1,0:T(8,128)(2,1)S(1)} %copy-done.10, s32[1,64]{1,0:T(1,128)S(1)} %bitcast.17, s32[4,64]{1,0:T(4,128)S(1)} %bitcast.13, ...), custom_call_target="tpu_custom_call" | custom-call | flops 1000000000 | bytes 10000000 | tf_op jit(solution)/shard_map/pallas_call | solution.py:354
  119.8 4.6 %all-to-all-done.4.got_ref = bf16[16,32,128]{2,1,0:T(8,128)(2,1)S(1)} async-done(((bf16[16,32,128]{2,1,0:T(8,128)(2,1)}), bf16[16,32,128]{2,1,0:T(8,128)(2,1)S(1)}, u32[]{:S(2)}, u32[]{:S(2)}) %all-to-all-start.4) | async-done | bytes 131104 | tf_op jit(solution)/shard_map/all_to_all | solution.py:273
  124.4 1.1 shard_map.107
  (14 shorter events, 0.0 us)
Async XLA Ops:
  2.1 41.0 %all-to-all-start = ((bf16[64,2,1152]{2,1,0:T(2,128)(2,1)}), bf16[64,2,1152]{2,1,0:T(2,128)(2,1)S(1)}, u32[]{:S(2)}, u32[]{:S(2)}) async-start(bf16[64,2,1152]{2,1,0:T(2,128)(2,1)} %shard_map.100), calls=%async_computation | async-start | bytes 589824 | tf_op jit(solution)/shard_map/all_to_all | solution.py:273
  20.9 0.7 copy-start.1
  21.5 0.7 copy-start.3
  22.2 1.6 %copy-start.6 = (bf16[256,16,256]{2,1,0:T(8,128)(2,1)S(1)}, bf16[256,16,256]{2,1,0:T(8,128)(2,1)}, u32[]{:S(2)}) copy-start(bf16[256,16,256]{2,1,0:T(8,128)(2,1)} %cache_ref.3) | copy-start | bytes 6291460
  23.8 1.0 copy-start.8
  24.8 0.9 copy-start.9
  25.7 0.7 copy-start.11
  26.4 27.5 %copy-start = (bf16[16,16,1024]{2,1,0:T(8,128)(2,1)S(1)}, bf16[16,16,1024]{2,1,0:T(8,128)(2,1)}, u32[]{:S(2)}) copy-start(bf16[16,16,1024]{2,1,0:T(8,128)(2,1)} %param.14) | copy-start | bytes 1572868
  27.8 11.9 %collective-permute-start = (bf16[512,256]{1,0:T(8,128)(2,1)S(1)}, bf16[512,256]{1,0:T(8,128)(2,1)S(1)}, u32[]{:S(2)}, u32[]{:S(2)}) collective-permute-start(bf16[512,256]{1,0:T(8,128)(2,1)S(1)} %get-tuple-element.16), channel_id=1, source_target_pairs={{0,256},{8,264},{16,272},{24,280},{32,288},{40,296},{48,304},{56,3... | collective-permute-start | bytes 786440 | tf_op jit(solution)/shard_map/ppermute | solution.py:284
  55.0 56.0 %copy-start.2 = (s32[64,4]{0,1:T(4,128)S(1)}, s32[64,4]{0,1:T(4,128)}, u32[]{:S(2)}) copy-start(s32[64,4]{0,1:T(4,128)} %param.17) | copy-start | bytes 3076
  55.0 56.0 %copy-start.4 = (s32[64,1]{0,1:T(1,128)S(1)}, s32[64,1]{0,1:T(1,128)}, u32[]{:S(2)}) copy-start(s32[64,1]{0,1:T(1,128)} %param.15) | copy-start | bytes 772
  55.0 56.0 %copy-start.5 = (s32[64]{0:T(128)S(1)}, s32[64]{0:T(128)}, u32[]{:S(2)}) copy-start(s32[64]{0:T(128)} %param.18) | copy-start | bytes 772
  55.0 56.0 %copy-start.10 = (bf16[64,1024]{1,0:T(8,128)(2,1)S(1)}, bf16[64,1024]{1,0:T(8,128)(2,1)}, u32[]{:S(2)}) copy-start(bf16[64,1024]{1,0:T(8,128)(2,1)} %base_ref.3) | copy-start | bytes 393220
  55.0 31.8 %all-to-all-start.2 = ((bf16[64,2,1024]{2,1,0:T(2,128)(2,1)}), bf16[64,2,1024]{2,1,0:T(2,128)(2,1)S(1)}, u32[]{:S(2)}, u32[]{:S(2)}) async-start(bf16[64,2,1024]{2,1,0:T(2,128)(2,1)} %shard_map.103), calls=%async_computation.2 | async-start | bytes 524288 | tf_op jit(solution)/shard_map/all_to_all | solution.py:273
  66.0 10.9 %collective-permute-start.1 = (bf16[512,256]{1,0:T(8,128)(2,1)S(1)}, bf16[512,256]{1,0:T(8,128)(2,1)S(1)}, u32[]{:S(2)}, u32[]{:S(2)}) collective-permute-start(bf16[512,256]{1,0:T(8,128)(2,1)S(1)} %get-tuple-element.21), channel_id=1, source_target_pairs={{0,128},{8,136},{16,144},{24,152},{32,160},{40,168},{48,176},{56,1... | collective-permute-start | bytes 786440 | tf_op jit(solution)/shard_map/ppermute | solution.py:284
  68.1 12.0 %collective-permute-start.2 = (bf16[512,256]{1,0:T(8,128)(2,1)S(1)}, bf16[512,256]{1,0:T(8,128)(2,1)S(1)}, u32[]{:S(2)}, u32[]{:S(2)}) collective-permute-start(bf16[512,256]{1,0:T(8,128)(2,1)S(1)} %get-tuple-element.22), channel_id=1, source_target_pairs={{0,384},{8,392},{16,400},{24,408},{32,416},{40,424},{48,432},{56,4... | collective-permute-start | bytes 786440 | tf_op jit(solution)/shard_map/ppermute | solution.py:284
  107.4 17.0 %all-to-all-start.4 = ((bf16[16,32,128]{2,1,0:T(8,128)(2,1)}), bf16[16,32,128]{2,1,0:T(8,128)(2,1)S(1)}, u32[]{:S(2)}, u32[]{:S(2)}) async-start(bf16[16,32,128]{2,1,0:T(8,128)(2,1)} %shard_map.105), calls=%async_computation.4 | async-start | bytes 262144 | tf_op jit(solution)/shard_map/all_to_all | solution.py:273
  111.0 1.6 %copy-start.7 = (bf16[256,16,256]{2,1,0:T(8,128)(2,1)S(1)}, bf16[256,16,256]{2,1,0:T(8,128)(2,1)}, u32[]{:S(2)}) copy-start(bf16[256,16,256]{2,1,0:T(8,128)(2,1)} %cache_ref.3) | copy-start | bytes 6291460

commit v5 on v4

--- a/solution.py
+++ b/solution.py
@@ -105,8 +105,8 @@
         out_ref[:, c, :features] = nn(maps[c], hidden).astype(BF16)
 
 
-def down_kernel(got_ref, down_ref, two_ref, partial_ref, pick_ref, limit_ref):
-    del two_ref
+def down_kernel(got_ref, down_ref, one_ref, partial_ref, pick_ref, limit_ref):
+    del one_ref
     peers, _, width = got_ref.shape
     features = width - HEAD
     many = down_ref.shape[0]
@@ -136,12 +136,8 @@
         out_ref[:, c, :] = delta[c * peers:(c + 1) * peers, :]
 
 
-def prepare_kernel(
-    list_ref, cache_ref, holder_ref, table_ref, base_ref, weight_ref,
-    own_ref, one_ref, two_ref, three_ref, route_ref, start_ref, down_ref,
-):
-    down_ref[...] = weight_ref[...]
-    count, owners = list_ref.shape
+def gather_kernel(list_ref, cache_ref, own_ref, one_ref, two_ref, three_ref):
+    count = list_ref.shape[0]
     for step, page_ref in enumerate((own_ref, one_ref, two_ref, three_ref)):
         first = ((my_plane() + step) & (PLANES - 1)) * DEPTH
 
@@ -152,6 +148,11 @@
             return carry
 
         lax.fori_loop(0, DEPTH, copy, 0, unroll=8)
+
+
+def prepare_kernel(holder_ref, table_ref, base_ref, weight_ref, route_ref, start_ref, down_ref):
+    down_ref[...] = weight_ref[...]
+    owners = route_ref.shape[1]
     maps = slot_maps(holder_ref[...], owners)
     moved = moved_map(table_ref[...], owners).astype(BF16)
     route_ref[...] = nt(jnp.concatenate(maps, axis=0), moved).astype(BF16)
@@ -160,8 +161,8 @@
         start_ref[:, h, :] = start[:, h * HEAD:(h + 1) * HEAD]
 
 
-def query_kernel(got_ref, route_ref, start_ref, one_ref, three_ref, out_ref, wide_ref):
-    del one_ref, three_ref
+def query_kernel(got_ref, route_ref, start_ref, two_ref, three_ref, out_ref, wide_ref):
+    del two_ref, three_ref
     got = jnp.concatenate([got_ref[:, 0, :], got_ref[:, 1, :]], axis=0)
     chosen = tn(route_ref[...], got)
     for h in range(wide_ref.shape[1]):
@@ -321,20 +322,13 @@
     )(hidden, holder, position, table, length)
     got = exchange(sent)
     handed = S((DEPTH * lists.shape[0] * PAGE, 2 * HEAD), BF16)
-    *pages, route, start, down = call(
+    pages = call(gather_kernel, (handed,) * PLANES, 10**9, "sv")(lists, key_value_cache)
+    route, start, down = call(
         prepare_kernel,
-        (
-            handed,
-            handed,
-            handed,
-            handed,
-            S((2 * peers, peers), BF16),
-            S((peers, heads, HEAD), F32),
-            S(down.shape, BF16),
-        ),
-        10**9,
-        "svvvvv",
-    )(lists, key_value_cache, holder, table, base_query, down)
+        (S((2 * peers, peers), BF16), S((peers, heads, HEAD), F32), S(down.shape, BF16)),
+        10**8,
+        "vvvv",
+    )(holder, table, base_query, down)
     pages = [pages[0]] + [hand_on(pages[step], step) for step in range(1, PLANES)]
 
     partial, pick, limit = call(
@@ -342,14 +336,14 @@
         (S((shards, RANK, 2 * peers), F32), S((many, 2 * peers), BF16), S((DEPTH, PLANES, heads, HEAD), F32)),
         10**8,
         "vva",
-    )(got, down, pages[2])
+    )(got, down, pages[1])
     partials = exchange(partial, "tensor")
     delta = call(up_kernel, S((peers, 2, features), BF16), 10**8, "vvv")(partials, pick, up)
     returned = exchange(delta)
     wide = pltpu.VMEM((rows, heads, HEAD), F32)
     flat = (DEPTH, PLANES * heads, HEAD)
     asked = along_depth(
-        call(query_kernel, S(flat, BF16), 10**8, "vvvaa", (wide,))(returned, route, start, pages[1], pages[3])
+        call(query_kernel, S(flat, BF16), 10**8, "vvvaa", (wide,))(returned, route, start, pages[2], pages[3])
     )
     local = call(local_kernel, S((rows, features), BF16), 10**9, "ssvvvvv", (wide, wide))(
         table, length, returned, base_query, holder, table, key_value_cache

time: 126 us -> 129 us (1.024)
  waiting for transfers between devices: 31.7 us -> 37.2 us
  blocking collectives: 28.4 us -> 33.4 us
  starting transfers between devices: 42.3 us -> 37.7 us
  local copies, waits for them, and re-layouts: 7.15 us -> 4.59 us
    ppermute x3, waiting for transfers between devices: 17.1 us -> 22.3 us  [hand_on(): return lax.ppermute(x, 'replica', pairs)]
    all_to_all x2, blocking collectives: 28.4 us -> 33.4 us  [exchange(): lax.all_to_all(x, axis, split_axis=0, concat_axis=0, tiled=True, axis_ind...]
    all_to_all x3, starting transfers between devices: 33.3 us -> 30.4 us  [exchange(): lax.all_to_all(x, axis, split_axis=0, concat_axis=0, tiled=True, axis_ind...]
    unnamed x24 -> x22, local copies, waits for them, and re-layouts: 7.15 us -> 4.59 us
    ppermute x3, starting transfers between devices: 9.01 us -> 7.23 us  [hand_on(): return lax.ppermute(x, 'replica', pairs)]
where the time goes in v5:
time: 129 us
  starting transfers between devices  37.7 us (29%)
  waiting for transfers between devices  37.2 us (29%)
  blocking collectives  33.4 us (26%)
  Pallas kernels  15.8 us (12%)
  local copies, waits for them, and re-layouts  4.59 us (4%)
    all_to_all x2, blocking collectives, exchange(): lax.all_to_all(x, axis, split_axis=0, concat_axis=0, tiled=True, axis_ind...  33.4 us
    all_to_all x3, starting transfers between devices, exchange(): lax.all_to_all(x, axis, split_axis=0, concat_axis=0, tiled=True, axis_ind...  30.4 us
    ppermute x3, waiting for transfers between devices, hand_on(): return lax.ppermute(x, 'replica', pairs)  22.3 us
    all_to_all x3, waiting for transfers between devices, exchange(): lax.all_to_all(x, axis, split_axis=0, concat_axis=0, tiled=True, axis_ind...  14.9 us
    ppermute x3, starting transfers between devices, hand_on(): return lax.ppermute(x, 'replica', pairs)  7.23 us
    pallas_call x1, Pallas kernels, body(): call(local_kernel, S((rows, features), BF16), 10 ** 9, 'ssvvvvv', (wide,...  7.23 us
    unnamed x22, local copies, waits for them, and re-layouts  4.59 us
  transfers between devices with their start and end apart: 6, of which 6 were waited for; matrix products, arithmetic and copies ran while one was open for 0% of the time, Pallas kernels for 7%

profile of v5, /device:TPU:6, one launch (start us, length us, event | category | flops | bytes accessed | tf_op | source)
XLA Modules:
  0.0 128.9 jit_solution(6547935392273232118)
XLA Ops:
  0.0 2.1 %shard_map.100 = bf16[64,2,1152]{2,1,0:T(2,128)(2,1)} custom-call(bf16[64,1024]{1,0:T(8,128)(2,1)} %hidden_hbm.1, s32[1,64]{1,0:T(1,128)} %bitcast.16, s32[1,64]{1,0:T(1,128)} %bitcast.22, s32[4,64]{1,0:T(4,128)} %bitcast.11, s32[1,64]{1,0:T(1,128)} %bitcast.19), custom_call_target="tpu_custom_call" | custom-call | flops 100000000 | bytes 1000000 | tf_op jit(solution)/shard_map/pallas_call | solution.py:315
  2.1 0.0 copy-start.1
  2.1 0.0 copy-start.2
  2.1 0.0 copy-start.3
  2.1 0.0 copy-start.4
  2.1 18.9 %all-to-all-start = ((bf16[64,2,1152]{2,1,0:T(2,128)(2,1)}), bf16[64,2,1152]{2,1,0:T(2,128)(2,1)S(1)}, u32[]{:S(2)}, u32[]{:S(2)}) async-start(bf16[64,2,1152]{2,1,0:T(2,128)(2,1)} %shard_map.100), calls=%async_computation | async-start | bytes 589824 | tf_op jit(solution)/shard_map/all_to_all | solution.py:274
  21.0 0.0 copy-start.6
  21.1 1.6 %copy-done.6 = bf16[256,16,256]{2,1,0:T(8,128)(2,1)S(1)} copy-done((bf16[256,16,256]{2,1,0:T(8,128)(2,1)S(1)}, bf16[256,16,256]{2,1,0:T(8,128)(2,1)}, u32[]{:S(2)}) %copy-start.6) | copy-done | bytes 2097176
  22.6 0.7 copy-done.10
  23.3 1.0 shard_map.102
  24.4 0.7 copy-done.8
  25.1 2.1 %collective-permute-start = (bf16[512,256]{1,0:T(8,128)(2,1)S(1)}, bf16[512,256]{1,0:T(8,128)(2,1)S(1)}, u32[]{:S(2)}, u32[]{:S(2)}) collective-permute-start(bf16[512,256]{1,0:T(8,128)(2,1)S(1)} %get-tuple-element.16), channel_id=1, source_target_pairs={{0,128},{8,136},{16,144},{24,152},{32,160},{40,168},{48,176},{56,1... | collective-permute-start | bytes 786440 | tf_op jit(solution)/shard_map/ppermute | solution.py:285
  27.2 0.3 shard_map.101
  27.6 8.8 %collective-permute-done.one_ref = bf16[512,256]{1,0:T(8,128)(2,1)S(1)} collective-permute-done((bf16[512,256]{1,0:T(8,128)(2,1)S(1)}, bf16[512,256]{1,0:T(8,128)(2,1)S(1)}, u32[]{:S(2)}, u32[]{:S(2)}) %collective-permute-start) | collective-permute-done | bytes 262176 | tf_op jit(solution)/shard_map/ppermute | solution.py:285
  36.4 6.9 %all-to-all-done.got_ref = bf16[64,2,1152]{2,1,0:T(2,128)(2,1)S(1)} async-done(((bf16[64,2,1152]{2,1,0:T(2,128)(2,1)}), bf16[64,2,1152]{2,1,0:T(2,128)(2,1)S(1)}, u32[]{:S(2)}, u32[]{:S(2)}) %all-to-all-start) | async-done | bytes 294944 | tf_op jit(solution)/shard_map/all_to_all | solution.py:274
  43.3 0.9 shard_map.103
  44.2 9.9 %all_to_all.25.got_ref = f32[8,16,128]{2,1,0:T(8,128)S(1)} all-to-all(f32[8,16,128]{2,1,0:T(8,128)S(1)} %get-tuple-element.17), channel_id=1, replica_groups=mesh['replica'=64,'tensor'=8] {'tensor'}, dimensions={0} | all-to-all | bytes 131072 | tf_op jit(solution)/shard_map/all_to_all | solution.py:274
  54.1 1.0 shard_map.104
  55.1 7.4 %all-to-all-start.2 = ((bf16[64,2,1024]{2,1,0:T(2,128)(2,1)}), bf16[64,2,1024]{2,1,0:T(2,128)(2,1)S(1)}, u32[]{:S(2)}, u32[]{:S(2)}) async-start(bf16[64,2,1024]{2,1,0:T(2,128)(2,1)} %shard_map.104), calls=%async_computation.2 | async-start | bytes 524288 | tf_op jit(solution)/shard_map/all_to_all | solution.py:274
  62.6 3.2 %collective-permute-start.1 = (bf16[512,256]{1,0:T(8,128)(2,1)S(1)}, bf16[512,256]{1,0:T(8,128)(2,1)S(1)}, u32[]{:S(2)}, u32[]{:S(2)}) collective-permute-start(bf16[512,256]{1,0:T(8,128)(2,1)S(1)} %copy-done.9), channel_id=1, source_target_pairs={{0,256},{8,264},{16,272},{24,280},{32,288},{40,296},{48,304},{56,3... | collective-permute-start | bytes 786440 | tf_op jit(solution)/shard_map/ppermute | solution.py:285
  65.8 1.9 %collective-permute-start.2 = (bf16[512,256]{1,0:T(8,128)(2,1)S(1)}, bf16[512,256]{1,0:T(8,128)(2,1)S(1)}, u32[]{:S(2)}, u32[]{:S(2)}) collective-permute-start(bf16[512,256]{1,0:T(8,128)(2,1)S(1)} %get-tuple-element.22), channel_id=1, source_target_pairs={{0,384},{8,392},{16,400},{24,408},{32,416},{40,424},{48,432},{56,4... | collective-permute-start | bytes 786440 | tf_op jit(solution)/shard_map/ppermute | solution.py:285
  67.7 9.1 %collective-permute-done.1.two_ref = bf16[512,256]{1,0:T(8,128)(2,1)S(1)} collective-permute-done((bf16[512,256]{1,0:T(8,128)(2,1)S(1)}, bf16[512,256]{1,0:T(8,128)(2,1)S(1)}, u32[]{:S(2)}, u32[]{:S(2)}) %collective-permute-start.1) | collective-permute-done | bytes 262176 | tf_op jit(solution)/shard_map/ppermute | solution.py:285
  76.8 4.4 %collective-permute-done.2.three_ref = bf16[512,256]{1,0:T(8,128)(2,1)S(1)} collective-permute-done((bf16[512,256]{1,0:T(8,128)(2,1)S(1)}, bf16[512,256]{1,0:T(8,128)(2,1)S(1)}, u32[]{:S(2)}, u32[]{:S(2)}) %collective-permute-start.2) | collective-permute-done | bytes 262176 | tf_op jit(solution)/shard_map/ppermute | solution.py:285
  81.2 2.1 %all-to-all-done.2.got_ref = bf16[64,2,1024]{2,1,0:T(2,128)(2,1)S(1)} async-done(((bf16[64,2,1024]{2,1,0:T(2,128)(2,1)}), bf16[64,2,1024]{2,1,0:T(2,128)(2,1)S(1)}, u32[]{:S(2)}, u32[]{:S(2)}) %all-to-all-start.2) | async-done | bytes 262176 | tf_op jit(solution)/shard_map/all_to_all | solution.py:274
  83.4 0.8 shard_map.105
  84.2 23.5 %all_to_all.26.query_ref = bf16[16,32,128]{2,1,0:T(8,128)(2,1)S(1)} all-to-all(bf16[16,32,128]{2,1,0:T(8,128)(2,1)S(1)} %shard_map.105), channel_id=1, replica_groups={{0,8,16,24,32,40,48,56,64,72,80,88,96,104,112,120},{128,136,144,152,160..., dimensions={0} | all-to-all | bytes 262144 | tf_op jit(solution)/shard_map/all_to_all | solution.py:274
  107.7 1.3 %shard_map.106 = bf16[16,32,128]{2,1,0:T(8,128)(2,1)} custom-call(bf16[16,32,128]{2,1,0:T(8,128)(2,1)S(1)} %all_to_all.26.query_ref, bf16[512,256]{1,0:T(8,128)(2,1)S(1)} %get-tuple-element.23.own_ref, bf16[512,256]{1,0:T(8,128)(2,1)S(1)} %collective-permute-done.one_ref, bf16[512,256]{1,0:T(8,128)(2,1)S(1)} %collective-permute-done.1.two_ref, ...), custom_call_target="tpu_custom_call" | custom-call | flops 100000000 | bytes 1000000 | tf_op jit(solution)/shard_map/pallas_call | solution.py:352
  109.0 4.1 %all-to-all-start.4 = ((bf16[16,32,128]{2,1,0:T(8,128)(2,1)}), bf16[16,32,128]{2,1,0:T(8,128)(2,1)S(1)}, u32[]{:S(2)}, u32[]{:S(2)}) async-start(bf16[16,32,128]{2,1,0:T(8,128)(2,1)} %shard_map.106), calls=%async_computation.4 | async-start | bytes 262144 | tf_op jit(solution)/shard_map/all_to_all | solution.py:274
  113.1 1.6 %copy-done.7 = bf16[256,16,256]{2,1,0:T(8,128)(2,1)S(1)} copy-done((bf16[256,16,256]{2,1,0:T(8,128)(2,1)S(1)}, bf16[256,16,256]{2,1,0:T(8,128)(2,1)}, u32[]{:S(2)}) %copy-start.7) | copy-done | bytes 2097176
  114.7 7.2 %shard_map.107.local_ref = bf16[64,1024]{1,0:T(8,128)(2,1)S(1)} custom-call(s32[4,64]{1,0:T(4,128)S(1)} %bitcast.13, s32[1,64]{1,0:T(1,128)S(1)} %bitcast.20, bf16[64,2,1024]{2,1,0:T(2,128)(2,1)S(1)} %all-to-all-done.2.got_ref, bf16[64,1024]{1,0:T(8,128)(2,1)S(1)} %copy-done.2, s32[1,64]{1,0:T(1,128)S(1)} %bitcast.18, s32[4,64]{1,0:T(4,128)S(1)} %bitcast.14, ...), custom_call_target="tpu_custom_call" | custom-call | flops 1000000000 | bytes 10000000 | tf_op jit(solution)/shard_map/pallas_call | solution.py:348
  121.9 5.9 %all-to-all-done.4.got_ref = bf16[16,32,128]{2,1,0:T(8,128)(2,1)S(1)} async-done(((bf16[16,32,128]{2,1,0:T(8,128)(2,1)}), bf16[16,32,128]{2,1,0:T(8,128)(2,1)S(1)}, u32[]{:S(2)}, u32[]{:S(2)}) %all-to-all-start.4) | async-done | bytes 131104 | tf_op jit(solution)/shard_map/all_to_all | solution.py:274
  127.8 1.1 shard_map.108
  (13 shorter events, 0.0 us)
Async XLA Ops:
  2.1 25.1 %copy-start.1 = (bf16[16,16,1024]{2,1,0:T(8,128)(2,1)S(1)}, bf16[16,16,1024]{2,1,0:T(8,128)(2,1)}, u32[]{:S(2)}) copy-start(bf16[16,16,1024]{2,1,0:T(8,128)(2,1)} %param.13) | copy-start | bytes 1572868
  2.1 25.1 %copy-start.2 = (bf16[64,1024]{1,0:T(8,128)(2,1)S(1)}, bf16[64,1024]{1,0:T(8,128)(2,1)}, u32[]{:S(2)}) copy-start(bf16[64,1024]{1,0:T(8,128)(2,1)} %base_ref.3) | copy-start | bytes 393220
  2.1 25.1 %copy-start.3 = (s32[64,4]{0,1:T(4,128)S(1)}, s32[64,4]{0,1:T(4,128)}, u32[]{:S(2)}) copy-start(s32[64,4]{0,1:T(4,128)} %param.17) | copy-start | bytes 3076
  2.1 25.1 %copy-start.4 = (s32[64,1]{0,1:T(1,128)S(1)}, s32[64,1]{0,1:T(1,128)}, u32[]{:S(2)}) copy-start(s32[64,1]{0,1:T(1,128)} %param.15) | copy-start | bytes 772
  2.1 41.2 %all-to-all-start = ((bf16[64,2,1152]{2,1,0:T(2,128)(2,1)}), bf16[64,2,1152]{2,1,0:T(2,128)(2,1)S(1)}, u32[]{:S(2)}, u32[]{:S(2)}) async-start(bf16[64,2,1152]{2,1,0:T(2,128)(2,1)} %shard_map.100), calls=%async_computation | async-start | bytes 589824 | tf_op jit(solution)/shard_map/all_to_all | solution.py:274
  21.0 1.6 %copy-start.6 = (bf16[256,16,256]{2,1,0:T(8,128)(2,1)S(1)}, bf16[256,16,256]{2,1,0:T(8,128)(2,1)}, u32[]{:S(2)}) copy-start(bf16[256,16,256]{2,1,0:T(8,128)(2,1)} %cache_ref.3) | copy-start | bytes 6291460
  22.6 0.7 copy-start.10
  23.3 30.8 %copy-start = (bf16[16,16,1024]{2,1,0:T(8,128)(2,1)S(1)}, bf16[16,16,1024]{2,1,0:T(8,128)(2,1)}, u32[]{:S(2)}) copy-start(bf16[16,16,1024]{2,1,0:T(8,128)(2,1)} %param.14) | copy-start | bytes 1572868
  24.3 0.7 copy-start.8
  25.1 11.3 %collective-permute-start = (bf16[512,256]{1,0:T(8,128)(2,1)S(1)}, bf16[512,256]{1,0:T(8,128)(2,1)S(1)}, u32[]{:S(2)}, u32[]{:S(2)}) collective-permute-start(bf16[512,256]{1,0:T(8,128)(2,1)S(1)} %get-tuple-element.16), channel_id=1, source_target_pairs={{0,128},{8,136},{16,144},{24,152},{32,160},{40,168},{48,176},{56,1... | collective-permute-start | bytes 786440 | tf_op jit(solution)/shard_map/ppermute | solution.py:285
  27.6 35.0 %copy-start.9 = (bf16[512,256]{1,0:T(8,128)(2,1)S(1)}, bf16[512,256]{1,0:T(8,128)(2,1)}, u32[]{:S(2)}) copy-start(bf16[512,256]{1,0:T(8,128)(2,1)} %copy-done.8) | copy-start | bytes 786436
  55.1 58.0 %copy-start.5 = (s32[64]{0:T(128)S(1)}, s32[64]{0:T(128)}, u32[]{:S(2)}) copy-start(s32[64]{0:T(128)} %param.18) | copy-start | bytes 772
  55.1 28.2 %all-to-all-start.2 = ((bf16[64,2,1024]{2,1,0:T(2,128)(2,1)}), bf16[64,2,1024]{2,1,0:T(2,128)(2,1)S(1)}, u32[]{:S(2)}, u32[]{:S(2)}) async-start(bf16[64,2,1024]{2,1,0:T(2,128)(2,1)} %shard_map.104), calls=%async_computation.2 | async-start | bytes 524288 | tf_op jit(solution)/shard_map/all_to_all | solution.py:274
  62.6 14.2 %collective-permute-start.1 = (bf16[512,256]{1,0:T(8,128)(2,1)S(1)}, bf16[512,256]{1,0:T(8,128)(2,1)S(1)}, u32[]{:S(2)}, u32[]{:S(2)}) collective-permute-start(bf16[512,256]{1,0:T(8,128)(2,1)S(1)} %copy-done.9), channel_id=1, source_target_pairs={{0,256},{8,264},{16,272},{24,280},{32,288},{40,296},{48,304},{56,3... | collective-permute-start | bytes 786440 | tf_op jit(solution)/shard_map/ppermute | solution.py:285
  65.8 15.4 %collective-permute-start.2 = (bf16[512,256]{1,0:T(8,128)(2,1)S(1)}, bf16[512,256]{1,0:T(8,128)(2,1)S(1)}, u32[]{:S(2)}, u32[]{:S(2)}) collective-permute-start(bf16[512,256]{1,0:T(8,128)(2,1)S(1)} %get-tuple-element.22), channel_id=1, source_target_pairs={{0,384},{8,392},{16,400},{24,408},{32,416},{40,424},{48,432},{56,4... | collective-permute-start | bytes 786440 | tf_op jit(solution)/shard_map/ppermute | solution.py:285
  109.0 18.8 %all-to-all-start.4 = ((bf16[16,32,128]{2,1,0:T(8,128)(2,1)}), bf16[16,32,128]{2,1,0:T(8,128)(2,1)S(1)}, u32[]{:S(2)}, u32[]{:S(2)}) async-start(bf16[16,32,128]{2,1,0:T(8,128)(2,1)} %shard_map.106), calls=%async_computation.4 | async-start | bytes 262144 | tf_op jit(solution)/shard_map/all_to_all | solution.py:274
  113.1 1.6 %copy-start.7 = (bf16[256,16,256]{2,1,0:T(8,128)(2,1)S(1)}, bf16[256,16,256]{2,1,0:T(8,128)(2,1)}, u32[]{:S(2)}) copy-start(bf16[256,16,256]{2,1,0:T(8,128)(2,1)} %cache_ref.3) | copy-start | bytes 6291460

commit v6 on v5

--- a/solution.py
+++ b/solution.py
@@ -136,10 +136,11 @@
         out_ref[:, c, :] = delta[c * peers:(c + 1) * peers, :]
 
 
-def gather_kernel(list_ref, cache_ref, own_ref, one_ref, two_ref, three_ref):
+def gather_kernel(list_ref, cache_ref, own_ref, one_ref, fore_ref, back_ref, three_ref):
     count = list_ref.shape[0]
-    for step, page_ref in enumerate((own_ref, one_ref, two_ref, three_ref)):
-        first = ((my_plane() + step) & (PLANES - 1)) * DEPTH
+    half = DEPTH // 2
+    for step, low, page_ref in ((0, 0, own_ref), (1, 0, one_ref), (2, 0, fore_ref), (2, half, back_ref), (3, 0, three_ref)):
+        first = ((my_plane() + step) & (PLANES - 1)) * DEPTH + low
 
         def copy(z, carry, page_ref=page_ref, first=first):
             for k in range(count):
@@ -147,7 +148,7 @@
                 page_ref[at, :] = cache_ref[list_ref[k, first + z]]
             return carry
 
-        lax.fori_loop(0, DEPTH, copy, 0, unroll=8)
+        lax.fori_loop(0, page_ref.shape[0] // (count * PAGE), copy, 0, unroll=8)
 
 
 def prepare_kernel(holder_ref, table_ref, base_ref, weight_ref, route_ref, start_ref, down_ref):
@@ -161,8 +162,8 @@
         start_ref[:, h, :] = start[:, h * HEAD:(h + 1) * HEAD]
 
 
-def query_kernel(got_ref, route_ref, start_ref, two_ref, three_ref, out_ref, wide_ref):
-    del two_ref, three_ref
+def query_kernel(got_ref, route_ref, start_ref, fore_ref, back_ref, three_ref, out_ref, wide_ref):
+    del fore_ref, back_ref, three_ref
     got = jnp.concatenate([got_ref[:, 0, :], got_ref[:, 1, :]], axis=0)
     chosen = tn(route_ref[...], got)
     for h in range(wide_ref.shape[1]):
@@ -219,7 +220,7 @@
         out_ref[:, h * HEAD:(h + 1) * HEAD] = (mixed_ref[:, h, :] * keep).astype(BF16)
 
 
-def moved_kernel(query_ref, own_ref, one_ref, two_ref, three_ref, limit_ref, out_ref, wide_ref):
+def moved_kernel(query_ref, own_ref, one_ref, fore_ref, back_ref, three_ref, limit_ref, out_ref, wide_ref):
     depth, planes, heads, _ = limit_ref.shape
     span = own_ref.shape[0] // depth
     batch = HEAD // span
@@ -229,8 +230,12 @@
     place = jnp.where(own, lax.rem(iota(shape, 1), span), span).astype(F32)
     query = query_ref[...].astype(F32)
     parts = [(d, z) for d in range(planes) for z in range(0, depth, batch)]
-    handed = (own_ref, one_ref, two_ref, three_ref)
-    pages = [handed[d][z * span:(z + batch) * span, :] for d, z in parts]
+    handed = ((own_ref,), (one_ref,), (fore_ref, back_ref), (three_ref,))
+    pages = []
+    for d, z in parts:
+        each = depth // len(handed[d])
+        first = z % each * span
+        pages.append(handed[d][z // each][first:first + batch * span, :])
     queries = [
         query[z:z + batch, d * heads:(d + 1) * heads].reshape(wide, HEAD).astype(BF16) for d, z in parts
     ]
@@ -322,34 +327,40 @@
     )(hidden, holder, position, table, length)
     got = exchange(sent)
     handed = S((DEPTH * lists.shape[0] * PAGE, 2 * HEAD), BF16)
-    pages = call(gather_kernel, (handed,) * PLANES, 10**9, "sv")(lists, key_value_cache)
+    part = S((handed.shape[0] // 2, 2 * HEAD), BF16)
+    own, one, fore, back, three = call(gather_kernel, (handed, handed, part, part, handed), 10**9, "sv")(
+        lists, key_value_cache
+    )
+    one, three = hand_on(one, 1), hand_on(three, -1)
+    fore, back = hand_on(fore, 1), hand_on(back, -1)
     route, start, down = call(
         prepare_kernel,
         (S((2 * peers, peers), BF16), S((peers, heads, HEAD), F32), S(down.shape, BF16)),
         10**8,
         "vvvv",
     )(holder, table, base_query, down)
-    pages = [pages[0]] + [hand_on(pages[step], step) for step in range(1, PLANES)]
 
     partial, pick, limit = call(
         down_kernel,
         (S((shards, RANK, 2 * peers), F32), S((many, 2 * peers), BF16), S((DEPTH, PLANES, heads, HEAD), F32)),
         10**8,
         "vva",
-    )(got, down, pages[1])
+    )(got, down, one)
     partials = exchange(partial, "tensor")
     delta = call(up_kernel, S((peers, 2, features), BF16), 10**8, "vvv")(partials, pick, up)
     returned = exchange(delta)
     wide = pltpu.VMEM((rows, heads, HEAD), F32)
     flat = (DEPTH, PLANES * heads, HEAD)
     asked = along_depth(
-        call(query_kernel, S(flat, BF16), 10**8, "vvvaa", (wide,))(returned, route, start, pages[2], pages[3])
+        call(query_kernel, S(flat, BF16), 10**8, "vvvaaa", (wide,))(returned, route, start, fore, back, three)
     )
     local = call(local_kernel, S((rows, features), BF16), 10**9, "ssvvvvv", (wide, wide))(
         table, length, returned, base_query, holder, table, key_value_cache
     )
     answered = along_depth(
-        call(moved_kernel, S(flat, BF16), 10**8, "vvvvvv", (pltpu.VMEM(flat, F32),))(asked, *pages, limit)
+        call(moved_kernel, S(flat, BF16), 10**8, "vvvvvvv", (pltpu.VMEM(flat, F32),))(
+            asked, own, one, hand_on(fore, 1), hand_on(back, -1), three, limit
+        )
     )
     return call(final_kernel, S((rows, features), BF16), 10**8, "vvv", (wide,))(answered, local, table)
 

time: 129 us -> 129 us (level)
  blocking collectives: 33.4 us -> 9.9 us
  starting transfers between devices: 37.7 us -> 57.4 us
  waiting for transfers between devices: 37.2 us -> 40 us
    all_to_all x2 -> x1, blocking collectives: 33.4 us -> 9.9 us  [exchange(): lax.all_to_all(x, axis, split_axis=0, concat_axis=0, tiled=True, axis_ind...]
    all_to_all x3 -> x4, starting transfers between devices: 30.4 us -> 40.5 us  [exchange(): lax.all_to_all(x, axis, split_axis=0, concat_axis=0, tiled=True, axis_ind...]
    ppermute x3 -> x6, starting transfers between devices: 7.23 us -> 17 us  [hand_on(): return lax.ppermute(x, 'replica', pairs)]
    all_to_all x3 -> x4, waiting for transfers between devices: 14.9 us -> 20.5 us  [exchange(): lax.all_to_all(x, axis, split_axis=0, concat_axis=0, tiled=True, axis_ind...]
    ppermute x3 -> x6, waiting for transfers between devices: 22.3 us -> 19.5 us  [hand_on(): return lax.ppermute(x, 'replica', pairs)]
  transfers between devices with their start and end apart: 6 -> 10, of which waited for: 6 -> 9; matrix products, arithmetic and copies ran while one was open for 0% -> 0% of each run, Pallas kernels for 7% -> 7%
where the time goes in v6:
time: 129 us; the launch traced here: 128 us
  starting transfers between devices  57.4 us (44%)
  waiting for transfers between devices  40 us (31%)
  Pallas kernels  16.4 us (13%)
  blocking collectives  9.9 us (8%)
  local copies, waits for them, and re-layouts  3.89 us (3%)
    all_to_all x4, starting transfers between devices, exchange(): lax.all_to_all(x, axis, split_axis=0, concat_axis=0, tiled=True, axis_ind...  40.5 us
    all_to_all x4, waiting for transfers between devices, exchange(): lax.all_to_all(x, axis, split_axis=0, concat_axis=0, tiled=True, axis_ind...  20.5 us
    ppermute x6, waiting for transfers between devices, hand_on(): return lax.ppermute(x, 'replica', pairs)  19.5 us
    ppermute x6, starting transfers between devices, hand_on(): return lax.ppermute(x, 'replica', pairs)  17 us
    all_to_all x1, blocking collectives, exchange(): lax.all_to_all(x, axis, split_axis=0, concat_axis=0, tiled=True, axis_ind...  9.9 us
    pallas_call x1, Pallas kernels, body(): call(local_kernel, S((rows, features), BF16), 10 ** 9, 'ssvvvvv', (wide,...  7.23 us
    unnamed x22, local copies, waits for them, and re-layouts  3.89 us
  transfers between devices with their start and end apart: 10, of which 9 were waited for; matrix products, arithmetic and copies ran while one was open for 0% of the time, Pallas kernels for 7%

profile of v6, /device:TPU:6, one launch (start us, length us, event | category | flops | bytes accessed | tf_op | source)
XLA Modules:
  0.0 127.8 jit_solution(10738392690852937502)
XLA Ops:
  0.0 2.0 %shard_map.100 = bf16[64,2,1152]{2,1,0:T(2,128)(2,1)} custom-call(bf16[64,1024]{1,0:T(8,128)(2,1)} %hidden_hbm.1, s32[1,64]{1,0:T(1,128)} %bitcast.16, s32[1,64]{1,0:T(1,128)} %bitcast.22, s32[4,64]{1,0:T(4,128)} %bitcast.11, s32[1,64]{1,0:T(1,128)} %bitcast.19), custom_call_target="tpu_custom_call" | custom-call | flops 100000000 | bytes 1000000 | tf_op jit(solution)/shard_map/pallas_call | solution.py:320
  2.1 18.9 %all-to-all-start = ((bf16[64,2,1152]{2,1,0:T(2,128)(2,1)}), bf16[64,2,1152]{2,1,0:T(2,128)(2,1)S(1)}, u32[]{:S(2)}, u32[]{:S(2)}) async-start(bf16[64,2,1152]{2,1,0:T(2,128)(2,1)} %shard_map.100), calls=%async_computation | async-start | bytes 589824 | tf_op jit(solution)/shard_map/all_to_all | solution.py:279
  21.0 1.6 %copy-done.6 = bf16[256,16,256]{2,1,0:T(8,128)(2,1)S(1)} copy-done((bf16[256,16,256]{2,1,0:T(8,128)(2,1)S(1)}, bf16[256,16,256]{2,1,0:T(8,128)(2,1)}, u32[]{:S(2)}) %copy-start.6) | copy-done | bytes 2097176
  22.6 0.7 copy-done.10
  23.3 1.0 shard_map.102
  24.3 2.2 %collective-permute-start = (bf16[512,256]{1,0:T(8,128)(2,1)S(1)}, bf16[512,256]{1,0:T(8,128)(2,1)S(1)}, u32[]{:S(2)}, u32[]{:S(2)}) collective-permute-start(bf16[512,256]{1,0:T(8,128)(2,1)S(1)} %get-tuple-element.17), channel_id=1, source_target_pairs={{0,128},{8,136},{16,144},{24,152},{32,160},{40,168},{48,176},{56,1... | collective-permute-start | bytes 786440 | tf_op jit(solution)/shard_map/ppermute | solution.py:290
  26.5 0.3 shard_map.101
  26.8 8.9 %collective-permute-done.one_ref = bf16[512,256]{1,0:T(8,128)(2,1)S(1)} collective-permute-done((bf16[512,256]{1,0:T(8,128)(2,1)S(1)}, bf16[512,256]{1,0:T(8,128)(2,1)S(1)}, u32[]{:S(2)}, u32[]{:S(2)}) %collective-permute-start) | collective-permute-done | bytes 262176 | tf_op jit(solution)/shard_map/ppermute | solution.py:290
  35.7 7.6 %all-to-all-done.got_ref = bf16[64,2,1152]{2,1,0:T(2,128)(2,1)S(1)} async-done(((bf16[64,2,1152]{2,1,0:T(2,128)(2,1)}), bf16[64,2,1152]{2,1,0:T(2,128)(2,1)S(1)}, u32[]{:S(2)}, u32[]{:S(2)}) %all-to-all-start) | async-done | bytes 294944 | tf_op jit(solution)/shard_map/all_to_all | solution.py:279
  43.3 0.9 shard_map.103
  44.2 9.9 %all_to_all.25.got_ref = f32[8,16,128]{2,1,0:T(8,128)S(1)} all-to-all(f32[8,16,128]{2,1,0:T(8,128)S(1)} %get-tuple-element.18), channel_id=1, replica_groups=mesh['replica'=64,'tensor'=8] {'tensor'}, dimensions={0} | all-to-all | bytes 131072 | tf_op jit(solution)/shard_map/all_to_all | solution.py:279
  54.1 1.0 shard_map.104
  55.1 6.9 %all-to-all-start.2 = ((bf16[64,2,1024]{2,1,0:T(2,128)(2,1)}), bf16[64,2,1024]{2,1,0:T(2,128)(2,1)S(1)}, u32[]{:S(2)}, u32[]{:S(2)}) async-start(bf16[64,2,1024]{2,1,0:T(2,128)(2,1)} %shard_map.104), calls=%async_computation.2 | async-start | bytes 524288 | tf_op jit(solution)/shard_map/all_to_all | solution.py:279
  62.1 2.7 %collective-permute-start.3 = (bf16[512,256]{1,0:T(8,128)(2,1)S(1)}, bf16[512,256]{1,0:T(8,128)(2,1)S(1)}, u32[]{:S(2)}, u32[]{:S(2)}) collective-permute-start(bf16[512,256]{1,0:T(8,128)(2,1)S(1)} %get-tuple-element.24), channel_id=1, source_target_pairs={{0,384},{8,392},{16,400},{24,408},{32,416},{40,424},{48,432},{56,4... | collective-permute-start | bytes 786440 | tf_op jit(solution)/shard_map/ppermute | solution.py:290
  64.7 4.4 %collective-permute-start.1 = (bf16[256,256]{1,0:T(8,128)(2,1)S(1)}, bf16[256,256]{1,0:T(8,128)(2,1)S(1)}, u32[]{:S(2)}, u32[]{:S(2)}) collective-permute-start(bf16[256,256]{1,0:T(8,128)(2,1)S(1)} %copy-done.9), channel_id=1, source_target_pairs={{0,128},{8,136},{16,144},{24,152},{32,160},{40,168},{48,176},{56,1... | collective-permute-start | bytes 393224 | tf_op jit(solution)/shard_map/ppermute | solution.py:290
  69.1 1.9 %collective-permute-start.2 = (bf16[256,256]{1,0:T(8,128)(2,1)S(1)}, bf16[256,256]{1,0:T(8,128)(2,1)S(1)}, u32[]{:S(2)}, u32[]{:S(2)}) collective-permute-start(bf16[256,256]{1,0:T(8,128)(2,1)S(1)} %get-tuple-element.23), channel_id=1, source_target_pairs={{0,384},{8,392},{16,400},{24,408},{32,416},{40,424},{48,432},{56,4... | collective-permute-start | bytes 393224 | tf_op jit(solution)/shard_map/ppermute | solution.py:290
  71.1 1.0 collective-permute-done.1.fore_ref
  72.1 5.5 %collective-permute-done.2.back_ref = bf16[256,256]{1,0:T(8,128)(2,1)S(1)} collective-permute-done((bf16[256,256]{1,0:T(8,128)(2,1)S(1)}, bf16[256,256]{1,0:T(8,128)(2,1)S(1)}, u32[]{:S(2)}, u32[]{:S(2)}) %collective-permute-start.2) | collective-permute-done | bytes 131104 | tf_op jit(solution)/shard_map/ppermute | solution.py:290
  77.6 5.3 %all-to-all-done.2.got_ref = bf16[64,2,1024]{2,1,0:T(2,128)(2,1)S(1)} async-done(((bf16[64,2,1024]{2,1,0:T(2,128)(2,1)}), bf16[64,2,1024]{2,1,0:T(2,128)(2,1)S(1)}, u32[]{:S(2)}, u32[]{:S(2)}) %all-to-all-start.2) | async-done | bytes 262176 | tf_op jit(solution)/shard_map/all_to_all | solution.py:279
  82.8 1.4 %shard_map.105 = bf16[16,32,128]{2,1,0:T(8,128)(2,1)} custom-call(bf16[64,2,1024]{2,1,0:T(2,128)(2,1)S(1)} %all-to-all-done.2.got_ref, bf16[128,64]{1,0:T(8,128)(2,1)S(1)} %get-tuple-element.20.route_ref, f32[64,8,128]{2,1,0:T(8,128)S(1)} %get-tuple-element.21.start_ref, bf16[256,256]{1,0:T(8,128)(2,1)S(1)} %collective-permute-done.1.fore_ref, ...), custom_call_target="tpu_custom_call" | custom-call | flops 100000000 | bytes 1000000 | tf_op jit(solution)/shard_map/pallas_call | solution.py:355
  84.3 6.0 %all-to-all-start.3 = ((bf16[16,32,128]{2,1,0:T(8,128)(2,1)}), bf16[16,32,128]{2,1,0:T(8,128)(2,1)S(1)}, u32[]{:S(2)}, u32[]{:S(2)}) async-start(bf16[16,32,128]{2,1,0:T(8,128)(2,1)} %shard_map.105), calls=%async_computation.3 | async-start | bytes 262144 | tf_op jit(solution)/shard_map/all_to_all | solution.py:279
  90.3 1.9 %collective-permute-start.4 = (bf16[256,256]{1,0:T(8,128)(2,1)S(1)}, bf16[256,256]{1,0:T(8,128)(2,1)S(1)}, u32[]{:S(2)}, u32[]{:S(2)}) collective-permute-start(bf16[256,256]{1,0:T(8,128)(2,1)S(1)} %collective-permute-done.1.fore_ref), channel_id=1, source_target_pairs={{0,128},{8,136},{16,144},{24,152},{32,160},{40,168},{48,176},{56,1... | collective-permute-start | bytes 393224 | tf_op jit(solution)/shard_map/ppermute | solution.py:290
  92.2 3.9 %collective-permute-start.5 = (bf16[256,256]{1,0:T(8,128)(2,1)S(1)}, bf16[256,256]{1,0:T(8,128)(2,1)S(1)}, u32[]{:S(2)}, u32[]{:S(2)}) collective-permute-start(bf16[256,256]{1,0:T(8,128)(2,1)S(1)} %collective-permute-done.2.back_ref), channel_id=1, source_target_pairs={{0,384},{8,392},{16,400},{24,408},{32,416},{40,424},{48,432},{56,4... | collective-permute-start | bytes 393224 | tf_op jit(solution)/shard_map/ppermute | solution.py:290
  96.1 1.0 collective-permute-done.4.fore_ref
  97.1 3.1 %collective-permute-done.5.back_ref = bf16[256,256]{1,0:T(8,128)(2,1)S(1)} collective-permute-done((bf16[256,256]{1,0:T(8,128)(2,1)S(1)}, bf16[256,256]{1,0:T(8,128)(2,1)S(1)}, u32[]{:S(2)}, u32[]{:S(2)}) %collective-permute-start.5) | collective-permute-done | bytes 131104 | tf_op jit(solution)/shard_map/ppermute | solution.py:290
  100.3 3.4 %all-to-all-done.3.query_ref = bf16[16,32,128]{2,1,0:T(8,128)(2,1)S(1)} async-done(((bf16[16,32,128]{2,1,0:T(8,128)(2,1)}), bf16[16,32,128]{2,1,0:T(8,128)(2,1)S(1)}, u32[]{:S(2)}, u32[]{:S(2)}) %all-to-all-start.3) | async-done | bytes 131104 | tf_op jit(solution)/shard_map/all_to_all | solution.py:279
  103.7 1.3 %shard_map.106 = bf16[16,32,128]{2,1,0:T(8,128)(2,1)} custom-call(bf16[16,32,128]{2,1,0:T(8,128)(2,1)S(1)} %all-to-all-done.3.query_ref, bf16[512,256]{1,0:T(8,128)(2,1)S(1)} %get-tuple-element.25.own_ref, bf16[512,256]{1,0:T(8,128)(2,1)S(1)} %collective-permute-done.one_ref, bf16[256,256]{1,0:T(8,128)(2,1)S(1)} %collective-permute-done.4.fore_ref, ...), custom_call_target="tpu_custom_call" | custom-call | flops 100000000 | bytes 1000000 | tf_op jit(solution)/shard_map/pallas_call | solution.py:361
  105.0 8.6 %all-to-all-start.4 = ((bf16[16,32,128]{2,1,0:T(8,128)(2,1)}), bf16[16,32,128]{2,1,0:T(8,128)(2,1)S(1)}, u32[]{:S(2)}, u32[]{:S(2)}) async-start(bf16[16,32,128]{2,1,0:T(8,128)(2,1)} %shard_map.106), calls=%async_computation.4 | async-start | bytes 262144 | tf_op jit(solution)/shard_map/all_to_all | solution.py:279
  113.7 1.6 %copy-done.7 = bf16[256,16,256]{2,1,0:T(8,128)(2,1)S(1)} copy-done((bf16[256,16,256]{2,1,0:T(8,128)(2,1)S(1)}, bf16[256,16,256]{2,1,0:T(8,128)(2,1)}, u32[]{:S(2)}) %copy-start.7) | copy-done | bytes 2097176
  115.2 7.2 %shard_map.107.local_ref = bf16[64,1024]{1,0:T(8,128)(2,1)S(1)} custom-call(s32[4,64]{1,0:T(4,128)S(1)} %bitcast.13, s32[1,64]{1,0:T(1,128)S(1)} %bitcast.20, bf16[64,2,1024]{2,1,0:T(2,128)(2,1)S(1)} %all-to-all-done.2.got_ref, bf16[64,1024]{1,0:T(8,128)(2,1)S(1)} %copy-done.2, s32[1,64]{1,0:T(1,128)S(1)} %bitcast.18, s32[4,64]{1,0:T(4,128)S(1)} %bitcast.14, ...), custom_call_target="tpu_custom_call" | custom-call | flops 1000000000 | bytes 10000000 | tf_op jit(solution)/shard_map/pallas_call | solution.py:357
  122.5 4.3 %all-to-all-done.4.got_ref = bf16[16,32,128]{2,1,0:T(8,128)(2,1)S(1)} async-done(((bf16[16,32,128]{2,1,0:T(8,128)(2,1)}), bf16[16,32,128]{2,1,0:T(8,128)(2,1)S(1)}, u32[]{:S(2)}, u32[]{:S(2)}) %all-to-all-start.4) | async-done | bytes 131104 | tf_op jit(solution)/shard_map/all_to_all | solution.py:279
  126.8 1.1 shard_map.108
  (20 shorter events, 0.1 us)
Async XLA Ops:
  2.1 24.4 %copy-start.1 = (bf16[16,16,1024]{2,1,0:T(8,128)(2,1)S(1)}, bf16[16,16,1024]{2,1,0:T(8,128)(2,1)}, u32[]{:S(2)}) copy-start(bf16[16,16,1024]{2,1,0:T(8,128)(2,1)} %param.13) | copy-start | bytes 1572868
  2.1 24.4 %copy-start.2 = (bf16[64,1024]{1,0:T(8,128)(2,1)S(1)}, bf16[64,1024]{1,0:T(8,128)(2,1)}, u32[]{:S(2)}) copy-start(bf16[64,1024]{1,0:T(8,128)(2,1)} %base_ref.3) | copy-start | bytes 393220
  2.1 24.4 %copy-start.3 = (s32[64,4]{0,1:T(4,128)S(1)}, s32[64,4]{0,1:T(4,128)}, u32[]{:S(2)}) copy-start(s32[64,4]{0,1:T(4,128)} %param.17) | copy-start | bytes 3076
  2.1 24.4 %copy-start.4 = (s32[64,1]{0,1:T(1,128)S(1)}, s32[64,1]{0,1:T(1,128)}, u32[]{:S(2)}) copy-start(s32[64,1]{0,1:T(1,128)} %param.15) | copy-start | bytes 772
  2.1 41.2 %all-to-all-start = ((bf16[64,2,1152]{2,1,0:T(2,128)(2,1)}), bf16[64,2,1152]{2,1,0:T(2,128)(2,1)S(1)}, u32[]{:S(2)}, u32[]{:S(2)}) async-start(bf16[64,2,1152]{2,1,0:T(2,128)(2,1)} %shard_map.100), calls=%async_computation | async-start | bytes 589824 | tf_op jit(solution)/shard_map/all_to_all | solution.py:279
  21.0 1.6 %copy-start.6 = (bf16[256,16,256]{2,1,0:T(8,128)(2,1)S(1)}, bf16[256,16,256]{2,1,0:T(8,128)(2,1)}, u32[]{:S(2)}) copy-start(bf16[256,16,256]{2,1,0:T(8,128)(2,1)} %cache_ref.3) | copy-start | bytes 6291460
  22.6 0.7 copy-start.10
  23.3 30.8 %copy-start = (bf16[16,16,1024]{2,1,0:T(8,128)(2,1)S(1)}, bf16[16,16,1024]{2,1,0:T(8,128)(2,1)}, u32[]{:S(2)}) copy-start(bf16[16,16,1024]{2,1,0:T(8,128)(2,1)} %param.14) | copy-start | bytes 1572868
  24.3 19.0 %copy-start.8 = (bf16[256,256]{1,0:T(8,128)(2,1)}, bf16[256,256]{1,0:T(8,128)(2,1)S(1)}, u32[]{:S(2)}) copy-start(bf16[256,256]{1,0:T(8,128)(2,1)S(1)} %get-tuple-element.22) | copy-start | bytes 393220
  24.3 11.4 %collective-permute-start = (bf16[512,256]{1,0:T(8,128)(2,1)S(1)}, bf16[512,256]{1,0:T(8,128)(2,1)S(1)}, u32[]{:S(2)}, u32[]{:S(2)}) collective-permute-start(bf16[512,256]{1,0:T(8,128)(2,1)S(1)} %get-tuple-element.17), channel_id=1, source_target_pairs={{0,128},{8,136},{16,144},{24,152},{32,160},{40,168},{48,176},{56,1... | collective-permute-start | bytes 786440 | tf_op jit(solution)/shard_map/ppermute | solution.py:290
  43.3 21.4 %copy-start.9 = (bf16[256,256]{1,0:T(8,128)(2,1)S(1)}, bf16[256,256]{1,0:T(8,128)(2,1)}, u32[]{:S(2)}) copy-start(bf16[256,256]{1,0:T(8,128)(2,1)} %copy-done.8) | copy-start | bytes 393220
  55.1 58.5 %copy-start.5 = (s32[64]{0:T(128)S(1)}, s32[64]{0:T(128)}, u32[]{:S(2)}) copy-start(s32[64]{0:T(128)} %param.18) | copy-start | bytes 772
  55.1 27.7 %all-to-all-start.2 = ((bf16[64,2,1024]{2,1,0:T(2,128)(2,1)}), bf16[64,2,1024]{2,1,0:T(2,128)(2,1)S(1)}, u32[]{:S(2)}, u32[]{:S(2)}) async-start(bf16[64,2,1024]{2,1,0:T(2,128)(2,1)} %shard_map.104), calls=%async_computation.2 | async-start | bytes 524288 | tf_op jit(solution)/shard_map/all_to_all | solution.py:279
  62.1 15.5 %collective-permute-start.3 = (bf16[512,256]{1,0:T(8,128)(2,1)S(1)}, bf16[512,256]{1,0:T(8,128)(2,1)S(1)}, u32[]{:S(2)}, u32[]{:S(2)}) collective-permute-start(bf16[512,256]{1,0:T(8,128)(2,1)S(1)} %get-tuple-element.24), channel_id=1, source_target_pairs={{0,384},{8,392},{16,400},{24,408},{32,416},{40,424},{48,432},{56,4... | collective-permute-start | bytes 786440 | tf_op jit(solution)/shard_map/ppermute | solution.py:290
  64.7 7.4 %collective-permute-start.1 = (bf16[256,256]{1,0:T(8,128)(2,1)S(1)}, bf16[256,256]{1,0:T(8,128)(2,1)S(1)}, u32[]{:S(2)}, u32[]{:S(2)}) collective-permute-start(bf16[256,256]{1,0:T(8,128)(2,1)S(1)} %copy-done.9), channel_id=1, source_target_pairs={{0,128},{8,136},{16,144},{24,152},{32,160},{40,168},{48,176},{56,1... | collective-permute-start | bytes 393224 | tf_op jit(solution)/shard_map/ppermute | solution.py:290
  69.1 8.4 %collective-permute-start.2 = (bf16[256,256]{1,0:T(8,128)(2,1)S(1)}, bf16[256,256]{1,0:T(8,128)(2,1)S(1)}, u32[]{:S(2)}, u32[]{:S(2)}) collective-permute-start(bf16[256,256]{1,0:T(8,128)(2,1)S(1)} %get-tuple-element.23), channel_id=1, source_target_pairs={{0,384},{8,392},{16,400},{24,408},{32,416},{40,424},{48,432},{56,4... | collective-permute-start | bytes 393224 | tf_op jit(solution)/shard_map/ppermute | solution.py:290
  84.3 19.4 %all-to-all-start.3 = ((bf16[16,32,128]{2,1,0:T(8,128)(2,1)}), bf16[16,32,128]{2,1,0:T(8,128)(2,1)S(1)}, u32[]{:S(2)}, u32[]{:S(2)}) async-start(bf16[16,32,128]{2,1,0:T(8,128)(2,1)} %shard_map.105), calls=%async_computation.3 | async-start | bytes 262144 | tf_op jit(solution)/shard_map/all_to_all | solution.py:279
  90.3 6.9 %collective-permute-start.4 = (bf16[256,256]{1,0:T(8,128)(2,1)S(1)}, bf16[256,256]{1,0:T(8,128)(2,1)S(1)}, u32[]{:S(2)}, u32[]{:S(2)}) collective-permute-start(bf16[256,256]{1,0:T(8,128)(2,1)S(1)} %collective-permute-done.1.fore_ref), channel_id=1, source_target_pairs={{0,128},{8,136},{16,144},{24,152},{32,160},{40,168},{48,176},{56,1... | collective-permute-start | bytes 393224 | tf_op jit(solution)/shard_map/ppermute | solution.py:290
  92.2 8.1 %collective-permute-start.5 = (bf16[256,256]{1,0:T(8,128)(2,1)S(1)}, bf16[256,256]{1,0:T(8,128)(2,1)S(1)}, u32[]{:S(2)}, u32[]{:S(2)}) collective-permute-start(bf16[256,256]{1,0:T(8,128)(2,1)S(1)} %collective-permute-done.2.back_ref), channel_id=1, source_target_pairs={{0,384},{8,392},{16,400},{24,408},{32,416},{40,424},{48,432},{56,4... | collective-permute-start | bytes 393224 | tf_op jit(solution)/shard_map/ppermute | solution.py:290
  105.0 21.8 %all-to-all-start.4 = ((bf16[16,32,128]{2,1,0:T(8,128)(2,1)}), bf16[16,32,128]{2,1,0:T(8,128)(2,1)S(1)}, u32[]{:S(2)}, u32[]{:S(2)}) async-start(bf16[16,32,128]{2,1,0:T(8,128)(2,1)} %shard_map.106), calls=%async_computation.4 | async-start | bytes 262144 | tf_op jit(solution)/shard_map/all_to_all | solution.py:279
  113.6 1.6 %copy-start.7 = (bf16[256,16,256]{2,1,0:T(8,128)(2,1)S(1)}, bf16[256,16,256]{2,1,0:T(8,128)(2,1)}, u32[]{:S(2)}) copy-start(bf16[256,16,256]{2,1,0:T(8,128)(2,1)} %cache_ref.3) | copy-start | bytes 6291460

commit v7 on v5

--- a/solution.py
+++ b/solution.py
@@ -105,8 +105,8 @@
         out_ref[:, c, :features] = nn(maps[c], hidden).astype(BF16)
 
 
-def down_kernel(got_ref, down_ref, one_ref, partial_ref, pick_ref, limit_ref):
-    del one_ref
+def down_kernel(got_ref, down_ref, two_ref, partial_ref, pick_ref, limit_ref):
+    del two_ref
     peers, _, width = got_ref.shape
     features = width - HEAD
     many = down_ref.shape[0]
@@ -161,8 +161,8 @@
         start_ref[:, h, :] = start[:, h * HEAD:(h + 1) * HEAD]
 
 
-def query_kernel(got_ref, route_ref, start_ref, two_ref, three_ref, out_ref, wide_ref):
-    del two_ref, three_ref
+def query_kernel(got_ref, route_ref, start_ref, one_ref, three_ref, out_ref, wide_ref):
+    del one_ref, three_ref
     got = jnp.concatenate([got_ref[:, 0, :], got_ref[:, 1, :]], axis=0)
     chosen = tn(route_ref[...], got)
     for h in range(wide_ref.shape[1]):
@@ -336,14 +336,14 @@
         (S((shards, RANK, 2 * peers), F32), S((many, 2 * peers), BF16), S((DEPTH, PLANES, heads, HEAD), F32)),
         10**8,
         "vva",
-    )(got, down, pages[1])
+    )(got, down, pages[2])
     partials = exchange(partial, "tensor")
     delta = call(up_kernel, S((peers, 2, features), BF16), 10**8, "vvv")(partials, pick, up)
     returned = exchange(delta)
     wide = pltpu.VMEM((rows, heads, HEAD), F32)
     flat = (DEPTH, PLANES * heads, HEAD)
     asked = along_depth(
-        call(query_kernel, S(flat, BF16), 10**8, "vvvaa", (wide,))(returned, route, start, pages[2], pages[3])
+        call(query_kernel, S(flat, BF16), 10**8, "vvvaa", (wide,))(returned, route, start, pages[1], pages[3])
     )
     local = call(local_kernel, S((rows, features), BF16), 10**9, "ssvvvvv", (wide, wide))(
         table, length, returned, base_query, holder, table, key_value_cache

time: 129 us -> 124 us (0.961)
  blocking collectives: 33.4 us -> 28.4 us
  waiting for transfers between devices: 37.2 us -> 34.2 us
  starting transfers between devices: 37.7 us -> 40.4 us
    all_to_all x2, blocking collectives: 33.4 us -> 28.4 us  [exchange(): lax.all_to_all(x, axis, split_axis=0, concat_axis=0, tiled=True, axis_ind...]
    ppermute x3, waiting for transfers between devices: 22.3 us -> 17.4 us  [hand_on(): return lax.ppermute(x, 'replica', pairs)]
    all_to_all x3, waiting for transfers between devices: 14.9 us -> 16.8 us  [exchange(): lax.all_to_all(x, axis, split_axis=0, concat_axis=0, tiled=True, axis_ind...]
    ppermute x3, starting transfers between devices: 7.23 us -> 9 us  [hand_on(): return lax.ppermute(x, 'replica', pairs)]
where the time goes in v7:
time: 124 us
  starting transfers between devices  40.4 us (33%)
  waiting for transfers between devices  34.2 us (28%)
  blocking collectives  28.4 us (23%)
  Pallas kernels  15.8 us (13%)
  local copies, waits for them, and re-layouts  4.59 us (4%)
    all_to_all x3, starting transfers between devices, exchange(): lax.all_to_all(x, axis, split_axis=0, concat_axis=0, tiled=True, axis_ind...  31.4 us
    all_to_all x2, blocking collectives, exchange(): lax.all_to_all(x, axis, split_axis=0, concat_axis=0, tiled=True, axis_ind...  28.4 us
    ppermute x3, waiting for transfers between devices, hand_on(): return lax.ppermute(x, 'replica', pairs)  17.4 us
    all_to_all x3, waiting for transfers between devices, exchange(): lax.all_to_all(x, axis, split_axis=0, concat_axis=0, tiled=True, axis_ind...  16.8 us
    ppermute x3, starting transfers between devices, hand_on(): return lax.ppermute(x, 'replica', pairs)  9 us
    pallas_call x1, Pallas kernels, body(): call(local_kernel, S((rows, features), BF16), 10 ** 9, 'ssvvvvv', (wide,...  7.23 us
    unnamed x22, local copies, waits for them, and re-layouts  4.59 us
  transfers between devices with their start and end apart: 6, of which 6 were waited for; matrix products, arithmetic and copies ran while one was open for 0% of the time, Pallas kernels for 7%

profile of v7, /device:TPU:6, one launch (start us, length us, event | category | flops | bytes accessed | tf_op | source)
XLA Modules:
  0.0 123.6 jit_solution(3198623399703349186)
XLA Ops:
  0.0 2.1 %shard_map.100 = bf16[64,2,1152]{2,1,0:T(2,128)(2,1)} custom-call(bf16[64,1024]{1,0:T(8,128)(2,1)} %hidden_hbm.1, s32[1,64]{1,0:T(1,128)} %bitcast.16, s32[1,64]{1,0:T(1,128)} %bitcast.22, s32[4,64]{1,0:T(4,128)} %bitcast.11, s32[1,64]{1,0:T(1,128)} %bitcast.19), custom_call_target="tpu_custom_call" | custom-call | flops 100000000 | bytes 1000000 | tf_op jit(solution)/shard_map/pallas_call | solution.py:315
  2.1 0.0 copy-start.1
  2.1 0.0 copy-start.3
  2.1 0.0 copy-start.4
  2.1 18.9 %all-to-all-start = ((bf16[64,2,1152]{2,1,0:T(2,128)(2,1)}), bf16[64,2,1152]{2,1,0:T(2,128)(2,1)S(1)}, u32[]{:S(2)}, u32[]{:S(2)}) async-start(bf16[64,2,1152]{2,1,0:T(2,128)(2,1)} %shard_map.100), calls=%async_computation | async-start | bytes 589824 | tf_op jit(solution)/shard_map/all_to_all | solution.py:274
  21.0 0.0 copy-start.6
  21.1 1.6 %copy-done.6 = bf16[256,16,256]{2,1,0:T(8,128)(2,1)S(1)} copy-done((bf16[256,16,256]{2,1,0:T(8,128)(2,1)S(1)}, bf16[256,16,256]{2,1,0:T(8,128)(2,1)}, u32[]{:S(2)}) %copy-start.6) | copy-done | bytes 2097176
  22.6 0.7 copy-done.10
  23.3 1.0 shard_map.102
  24.4 0.7 copy-done.8
  25.1 3.2 %collective-permute-start = (bf16[512,256]{1,0:T(8,128)(2,1)S(1)}, bf16[512,256]{1,0:T(8,128)(2,1)S(1)}, u32[]{:S(2)}, u32[]{:S(2)}) collective-permute-start(bf16[512,256]{1,0:T(8,128)(2,1)S(1)} %get-tuple-element.16), channel_id=1, source_target_pairs={{0,256},{8,264},{16,272},{24,280},{32,288},{40,296},{48,304},{56,3... | collective-permute-start | bytes 786440 | tf_op jit(solution)/shard_map/ppermute | solution.py:285
  28.3 0.3 shard_map.101
  28.6 9.0 %collective-permute-done.two_ref = bf16[512,256]{1,0:T(8,128)(2,1)S(1)} collective-permute-done((bf16[512,256]{1,0:T(8,128)(2,1)S(1)}, bf16[512,256]{1,0:T(8,128)(2,1)S(1)}, u32[]{:S(2)}, u32[]{:S(2)}) %collective-permute-start) | collective-permute-done | bytes 262176 | tf_op jit(solution)/shard_map/ppermute | solution.py:285
  37.6 5.7 %all-to-all-done.got_ref = bf16[64,2,1152]{2,1,0:T(2,128)(2,1)S(1)} async-done(((bf16[64,2,1152]{2,1,0:T(2,128)(2,1)}), bf16[64,2,1152]{2,1,0:T(2,128)(2,1)S(1)}, u32[]{:S(2)}, u32[]{:S(2)}) %all-to-all-start) | async-done | bytes 294944 | tf_op jit(solution)/shard_map/all_to_all | solution.py:274
  43.3 0.9 shard_map.103
  44.2 9.9 %all_to_all.25.got_ref = f32[8,16,128]{2,1,0:T(8,128)S(1)} all-to-all(f32[8,16,128]{2,1,0:T(8,128)S(1)} %get-tuple-element.17), channel_id=1, replica_groups=mesh['replica'=64,'tensor'=8] {'tensor'}, dimensions={0} | all-to-all | bytes 131072 | tf_op jit(solution)/shard_map/all_to_all | solution.py:274
  54.1 1.0 shard_map.104
  55.1 8.9 %all-to-all-start.2 = ((bf16[64,2,1024]{2,1,0:T(2,128)(2,1)}), bf16[64,2,1024]{2,1,0:T(2,128)(2,1)S(1)}, u32[]{:S(2)}, u32[]{:S(2)}) async-start(bf16[64,2,1024]{2,1,0:T(2,128)(2,1)} %shard_map.104), calls=%async_computation.2 | async-start | bytes 524288 | tf_op jit(solution)/shard_map/all_to_all | solution.py:274
  64.1 2.2 %collective-permute-start.1 = (bf16[512,256]{1,0:T(8,128)(2,1)S(1)}, bf16[512,256]{1,0:T(8,128)(2,1)S(1)}, u32[]{:S(2)}, u32[]{:S(2)}) collective-permute-start(bf16[512,256]{1,0:T(8,128)(2,1)S(1)} %copy-done.9), channel_id=1, source_target_pairs={{0,128},{8,136},{16,144},{24,152},{32,160},{40,168},{48,176},{56,1... | collective-permute-start | bytes 786440 | tf_op jit(solution)/shard_map/ppermute | solution.py:285
  66.3 3.7 %collective-permute-start.2 = (bf16[512,256]{1,0:T(8,128)(2,1)S(1)}, bf16[512,256]{1,0:T(8,128)(2,1)S(1)}, u32[]{:S(2)}, u32[]{:S(2)}) collective-permute-start(bf16[512,256]{1,0:T(8,128)(2,1)S(1)} %get-tuple-element.22), channel_id=1, source_target_pairs={{0,384},{8,392},{16,400},{24,408},{32,416},{40,424},{48,432},{56,4... | collective-permute-start | bytes 786440 | tf_op jit(solution)/shard_map/ppermute | solution.py:285
  70.0 5.0 %collective-permute-done.1.one_ref = bf16[512,256]{1,0:T(8,128)(2,1)S(1)} collective-permute-done((bf16[512,256]{1,0:T(8,128)(2,1)S(1)}, bf16[512,256]{1,0:T(8,128)(2,1)S(1)}, u32[]{:S(2)}, u32[]{:S(2)}) %collective-permute-start.1) | collective-permute-done | bytes 262176 | tf_op jit(solution)/shard_map/ppermute | solution.py:285
  75.0 3.4 %collective-permute-done.2.three_ref = bf16[512,256]{1,0:T(8,128)(2,1)S(1)} collective-permute-done((bf16[512,256]{1,0:T(8,128)(2,1)S(1)}, bf16[512,256]{1,0:T(8,128)(2,1)S(1)}, u32[]{:S(2)}, u32[]{:S(2)}) %collective-permute-start.2) | collective-permute-done | bytes 262176 | tf_op jit(solution)/shard_map/ppermute | solution.py:285
  78.3 6.5 %all-to-all-done.2.got_ref = bf16[64,2,1024]{2,1,0:T(2,128)(2,1)S(1)} async-done(((bf16[64,2,1024]{2,1,0:T(2,128)(2,1)}), bf16[64,2,1024]{2,1,0:T(2,128)(2,1)S(1)}, u32[]{:S(2)}, u32[]{:S(2)}) %all-to-all-start.2) | async-done | bytes 262176 | tf_op jit(solution)/shard_map/all_to_all | solution.py:274
  84.9 0.8 shard_map.105
  85.6 18.5 %all_to_all.26.query_ref = bf16[16,32,128]{2,1,0:T(8,128)(2,1)S(1)} all-to-all(bf16[16,32,128]{2,1,0:T(8,128)(2,1)S(1)} %shard_map.105), channel_id=1, replica_groups={{0,8,16,24,32,40,48,56,64,72,80,88,96,104,112,120},{128,136,144,152,160..., dimensions={0} | all-to-all | bytes 262144 | tf_op jit(solution)/shard_map/all_to_all | solution.py:274
  104.2 1.3 %shard_map.106 = bf16[16,32,128]{2,1,0:T(8,128)(2,1)} custom-call(bf16[16,32,128]{2,1,0:T(8,128)(2,1)S(1)} %all_to_all.26.query_ref, bf16[512,256]{1,0:T(8,128)(2,1)S(1)} %get-tuple-element.23.own_ref, bf16[512,256]{1,0:T(8,128)(2,1)S(1)} %collective-permute-done.1.one_ref, bf16[512,256]{1,0:T(8,128)(2,1)S(1)} %collective-permute-done.two_ref, ...), custom_call_target="tpu_custom_call" | custom-call | flops 100000000 | bytes 1000000 | tf_op jit(solution)/shard_map/pallas_call | solution.py:352
  105.5 3.5 %all-to-all-start.4 = ((bf16[16,32,128]{2,1,0:T(8,128)(2,1)}), bf16[16,32,128]{2,1,0:T(8,128)(2,1)S(1)}, u32[]{:S(2)}, u32[]{:S(2)}) async-start(bf16[16,32,128]{2,1,0:T(8,128)(2,1)} %shard_map.106), calls=%async_computation.4 | async-start | bytes 262144 | tf_op jit(solution)/shard_map/all_to_all | solution.py:274
  109.0 0.0 copy-start.7
  109.1 1.6 %copy-done.7 = bf16[256,16,256]{2,1,0:T(8,128)(2,1)S(1)} copy-done((bf16[256,16,256]{2,1,0:T(8,128)(2,1)S(1)}, bf16[256,16,256]{2,1,0:T(8,128)(2,1)}, u32[]{:S(2)}) %copy-start.7) | copy-done | bytes 2097176
  110.6 7.2 %shard_map.107.local_ref = bf16[64,1024]{1,0:T(8,128)(2,1)S(1)} custom-call(s32[4,64]{1,0:T(4,128)S(1)} %bitcast.13, s32[1,64]{1,0:T(1,128)S(1)} %bitcast.20, bf16[64,2,1024]{2,1,0:T(2,128)(2,1)S(1)} %all-to-all-done.2.got_ref, bf16[64,1024]{1,0:T(8,128)(2,1)S(1)} %copy-done.2, s32[1,64]{1,0:T(1,128)S(1)} %bitcast.18, s32[4,64]{1,0:T(4,128)S(1)} %bitcast.14, ...), custom_call_target="tpu_custom_call" | custom-call | flops 1000000000 | bytes 10000000 | tf_op jit(solution)/shard_map/pallas_call | solution.py:348
  117.9 4.6 %all-to-all-done.4.got_ref = bf16[16,32,128]{2,1,0:T(8,128)(2,1)S(1)} async-done(((bf16[16,32,128]{2,1,0:T(8,128)(2,1)}), bf16[16,32,128]{2,1,0:T(8,128)(2,1)S(1)}, u32[]{:S(2)}, u32[]{:S(2)}) %all-to-all-start.4) | async-done | bytes 131104 | tf_op jit(solution)/shard_map/all_to_all | solution.py:274
  122.5 1.1 shard_map.108
  (13 shorter events, 0.0 us)
Async XLA Ops:
  2.1 26.2 %copy-start.1 = (bf16[16,16,1024]{2,1,0:T(8,128)(2,1)S(1)}, bf16[16,16,1024]{2,1,0:T(8,128)(2,1)}, u32[]{:S(2)}) copy-start(bf16[16,16,1024]{2,1,0:T(8,128)(2,1)} %param.13) | copy-start | bytes 1572868
  2.1 26.2 %copy-start.2 = (bf16[64,1024]{1,0:T(8,128)(2,1)S(1)}, bf16[64,1024]{1,0:T(8,128)(2,1)}, u32[]{:S(2)}) copy-start(bf16[64,1024]{1,0:T(8,128)(2,1)} %base_ref.3) | copy-start | bytes 393220
  2.1 26.1 %copy-start.3 = (s32[64,4]{0,1:T(4,128)S(1)}, s32[64,4]{0,1:T(4,128)}, u32[]{:S(2)}) copy-start(s32[64,4]{0,1:T(4,128)} %param.17) | copy-start | bytes 3076
  2.1 26.1 %copy-start.4 = (s32[64,1]{0,1:T(1,128)S(1)}, s32[64,1]{0,1:T(1,128)}, u32[]{:S(2)}) copy-start(s32[64,1]{0,1:T(1,128)} %param.15) | copy-start | bytes 772
  2.1 41.2 %all-to-all-start = ((bf16[64,2,1152]{2,1,0:T(2,128)(2,1)}), bf16[64,2,1152]{2,1,0:T(2,128)(2,1)S(1)}, u32[]{:S(2)}, u32[]{:S(2)}) async-start(bf16[64,2,1152]{2,1,0:T(2,128)(2,1)} %shard_map.100), calls=%async_computation | async-start | bytes 589824 | tf_op jit(solution)/shard_map/all_to_all | solution.py:274
  21.0 1.6 %copy-start.6 = (bf16[256,16,256]{2,1,0:T(8,128)(2,1)S(1)}, bf16[256,16,256]{2,1,0:T(8,128)(2,1)}, u32[]{:S(2)}) copy-start(bf16[256,16,256]{2,1,0:T(8,128)(2,1)} %cache_ref.3) | copy-start | bytes 6291460
  22.6 0.7 copy-start.10
  23.3 30.8 %copy-start = (bf16[16,16,1024]{2,1,0:T(8,128)(2,1)S(1)}, bf16[16,16,1024]{2,1,0:T(8,128)(2,1)}, u32[]{:S(2)}) copy-start(bf16[16,16,1024]{2,1,0:T(8,128)(2,1)} %param.14) | copy-start | bytes 1572868
  24.3 0.7 copy-start.8
  25.1 12.6 %collective-permute-start = (bf16[512,256]{1,0:T(8,128)(2,1)S(1)}, bf16[512,256]{1,0:T(8,128)(2,1)S(1)}, u32[]{:S(2)}, u32[]{:S(2)}) collective-permute-start(bf16[512,256]{1,0:T(8,128)(2,1)S(1)} %get-tuple-element.16), channel_id=1, source_target_pairs={{0,256},{8,264},{16,272},{24,280},{32,288},{40,296},{48,304},{56,3... | collective-permute-start | bytes 786440 | tf_op jit(solution)/shard_map/ppermute | solution.py:285
  28.6 35.5 %copy-start.9 = (bf16[512,256]{1,0:T(8,128)(2,1)S(1)}, bf16[512,256]{1,0:T(8,128)(2,1)}, u32[]{:S(2)}) copy-start(bf16[512,256]{1,0:T(8,128)(2,1)} %copy-done.8) | copy-start | bytes 786436
  55.1 53.9 %copy-start.5 = (s32[64]{0:T(128)S(1)}, s32[64]{0:T(128)}, u32[]{:S(2)}) copy-start(s32[64]{0:T(128)} %param.18) | copy-start | bytes 772
  55.1 29.7 %all-to-all-start.2 = ((bf16[64,2,1024]{2,1,0:T(2,128)(2,1)}), bf16[64,2,1024]{2,1,0:T(2,128)(2,1)S(1)}, u32[]{:S(2)}, u32[]{:S(2)}) async-start(bf16[64,2,1024]{2,1,0:T(2,128)(2,1)} %shard_map.104), calls=%async_computation.2 | async-start | bytes 524288 | tf_op jit(solution)/shard_map/all_to_all | solution.py:274
  64.1 10.9 %collective-permute-start.1 = (bf16[512,256]{1,0:T(8,128)(2,1)S(1)}, bf16[512,256]{1,0:T(8,128)(2,1)S(1)}, u32[]{:S(2)}, u32[]{:S(2)}) collective-permute-start(bf16[512,256]{1,0:T(8,128)(2,1)S(1)} %copy-done.9), channel_id=1, source_target_pairs={{0,128},{8,136},{16,144},{24,152},{32,160},{40,168},{48,176},{56,1... | collective-permute-start | bytes 786440 | tf_op jit(solution)/shard_map/ppermute | solution.py:285
  66.3 12.0 %collective-permute-start.2 = (bf16[512,256]{1,0:T(8,128)(2,1)S(1)}, bf16[512,256]{1,0:T(8,128)(2,1)S(1)}, u32[]{:S(2)}, u32[]{:S(2)}) collective-permute-start(bf16[512,256]{1,0:T(8,128)(2,1)S(1)} %get-tuple-element.22), channel_id=1, source_target_pairs={{0,384},{8,392},{16,400},{24,408},{32,416},{40,424},{48,432},{56,4... | collective-permute-start | bytes 786440 | tf_op jit(solution)/shard_map/ppermute | solution.py:285
  105.5 17.0 %all-to-all-start.4 = ((bf16[16,32,128]{2,1,0:T(8,128)(2,1)}), bf16[16,32,128]{2,1,0:T(8,128)(2,1)S(1)}, u32[]{:S(2)}, u32[]{:S(2)}) async-start(bf16[16,32,128]{2,1,0:T(8,128)(2,1)} %shard_map.106), calls=%async_computation.4 | async-start | bytes 262144 | tf_op jit(solution)/shard_map/all_to_all | solution.py:274
  109.0 1.6 %copy-start.7 = (bf16[256,16,256]{2,1,0:T(8,128)(2,1)S(1)}, bf16[256,16,256]{2,1,0:T(8,128)(2,1)}, u32[]{:S(2)}) copy-start(bf16[256,16,256]{2,1,0:T(8,128)(2,1)} %cache_ref.3) | copy-start | bytes 6291460
